TPU v7x, 32 devices: a whole 2x2x4 slice. The times are simulated.
32 devices in a mesh: seq: 8 (over z, x), batch: 4 (over y, core).
Axes of the slice: x: 2, y: 2, z: 4, core: 2. Of those that a mesh axis runs over, the one named last changes fastest.
Arguments:
- tokens: float32 [4, 1024, 2048], P('batch', 'seq'), may hold values from -6 to 6
- language: int32 [4], P('batch'), may hold values from 0 to 6
- language_weight: float32 [7], replicated, may hold values from 0.5 to 2
- output_grad: float32 [4, 1024, 2048], P('batch', 'seq'), may hold values from -6 to 6
- attention_gain: bfloat16 [2048], P(('seq', 'batch')), may hold values from 0.5 to 1.5
- attention_shift: bfloat16 [2048], P(('seq', 'batch')), may hold values from -4 to 4
- joint_weight: bfloat16 [2048, 6144], P(('seq', 'batch')), may hold values from -0.1875 to 0.1875
- joint_bias: bfloat16 [6144], P(('seq', 'batch')), may hold values from -4 to 4
- output_weight: bfloat16 [2048, 2048], P(('seq', 'batch')), may hold values from -0.75 to 0.75
- feedfwd_gain: bfloat16 [2048], P(('seq', 'batch')), may hold values from 0.5 to 1.5
- feedfwd_shift: bfloat16 [2048], P(('seq', 'batch')), may hold values from -4 to 4
- gate_weight: bfloat16 [2048, 5632], P(('seq', 'batch')), may hold values from -0.125 to 0.125
- up_weight: bfloat16 [2048, 5632], P(('seq', 'batch')), may hold values from -0.125 to 0.125
- down_weight: bfloat16 [2048, 5632], P(('seq', 'batch')), may hold values from -0.15625 to 0.15625
Outputs:
- result: float32 [4, 1024, 2048], P('batch', 'seq')
- grad_tokens: float32 [4, 1024, 2048], P('batch', 'seq')
- grad_attgain: float32 [2048], P(('seq', 'batch'))
- grad_attshift: float32 [2048], P(('seq', 'batch'))
- grad_joint: float32 [2048, 6144], P(('seq', 'batch'))
- grad_jointbias: float32 [6144], P(('seq', 'batch'))
- grad_output: float32 [2048, 2048], P(('seq', 'batch'))
- grad_ffgain: float32 [2048], P(('seq', 'batch'))
- grad_ffshift: float32 [2048], P(('seq', 'batch'))
- grad_gate: float32 [2048, 5632], P(('seq', 'batch'))
- grad_up: float32 [2048, 5632], P(('seq', 'batch'))
- grad_down: float32 [2048, 5632], P(('seq', 'batch'))
All inputs are finite; a program needn't handle non-finite values.
Results may differ from a plain program's by a relative error of at most 0.025.
Values may be sent and summed in bfloat16 or wider, within the bound.
No kernel may reach another device: no remote copies, remote signals or barrier semaphores. Data moves between devices by JAX's collectives and lax.ppermute only.
A program may use at most 448 MiB of HBM per device.

v0:
```python
import math

import jax
import jax.numpy as jnp
from jax import lax
from jax.sharding import PartitionSpec as P

HEADS = 32
HEAD_DIM = 64
ROT_DIMS = 16
LANGS = 7


EPSILON = 1e-05
THETA_BASE = 10000.0
NEGATIVE = -1e30


def normalize(values, gain_values, shift_values):
    center = values - jnp.mean(values, axis=-1, keepdims=True)
    inverse_std = lax.rsqrt(jnp.mean(center * center, axis=-1, keepdims=True) + EPSILON)
    unit_rows = center * inverse_std
    return (unit_rows * gain_values + shift_values, unit_rows, inverse_std)


def norm_back(incoming, unit_rows, inverse_std, gain_values):
    inner = incoming * gain_values
    return inverse_std * (
        inner
        - jnp.mean(inner, axis=-1, keepdims=True)
        - unit_rows * jnp.mean(inner * unit_rows, axis=-1, keepdims=True)
    )


def rotary_tables(positions):
    half_rot = ROT_DIMS // 2
    frequency = THETA_BASE ** (-jnp.arange(half_rot, dtype=jnp.float32) / half_rot)
    angles = positions.astype(jnp.float32)[:, None] * frequency[None, :]
    return (jnp.cos(angles)[:, None, :], jnp.sin(angles)[:, None, :])


def rotate(values, cosine_table, sine_table):
    half_rot = ROT_DIMS // 2
    first_half = values[..., :half_rot]
    second_half = values[..., half_rot:ROT_DIMS]
    remainder = values[..., ROT_DIMS:]
    return jnp.concatenate(
        [
            first_half * cosine_table - second_half * sine_table,
            second_half * cosine_table + first_half * sine_table,
            remainder,
        ],
        axis=-1,
    )


def unrotate(values, cosine_table, sine_table):
    half_rot = ROT_DIMS // 2
    first_half = values[..., :half_rot]
    second_half = values[..., half_rot:ROT_DIMS]
    remainder = values[..., ROT_DIMS:]
    return jnp.concatenate(
        [
            first_half * cosine_table + second_half * sine_table,
            second_half * cosine_table - first_half * sine_table,
            remainder,
        ],
        axis=-1,
    )


def over_blocks(step, carried, arrays):
    total_rows = arrays[0].shape[1]
    block_rows = math.gcd(total_rows, 512)
    number = total_rows // block_rows
    reshaped = tuple(
        (
            jnp.moveaxis(item.reshape((item.shape[0], number, block_rows) + item.shape[2:]), 1, 0)
            for item in arrays
        )
    )
    offsets = block_rows * jnp.arange(number, dtype=jnp.int32)

    def inner(state, element):
        return (step(state, element[0], element[1]), None)

    carried, _ = lax.scan(inner, carried, (reshaped, offsets))
    return carried


def body(
    tokens,
    language,
    language_weight,
    output_grad,
    attention_gain,
    attention_shift,
    joint_weight,
    joint_bias,
    output_weight,
    feedfwd_gain,
    feedfwd_shift,
    gate_weight,
    up_weight,
    down_weight,
):
    seq_count = tokens.shape[0]
    local_rows = tokens.shape[1]
    model_width = tokens.shape[2]
    flat_rows = seq_count * local_rows
    values = tokens.reshape(flat_rows, model_width)
    score_scale = 1.0 / math.sqrt(HEAD_DIM)
    first_pos = lax.axis_index("seq") * local_rows
    positions = first_pos + jnp.arange(local_rows, dtype=jnp.int32)
    cosine_table, sine_table = rotary_tables(positions)
    joint_all, output_all, bias_all, gain_one, shift_one = (
        lax.all_gather(joint_weight, ("seq", "batch"), axis=0, tiled=True),
        lax.all_gather(output_weight, ("seq", "batch"), axis=0, tiled=True),
        lax.all_gather(joint_bias, ("seq", "batch"), axis=0, tiled=True),
        lax.all_gather(attention_gain, ("seq", "batch"), axis=0, tiled=True),
        lax.all_gather(attention_shift, ("seq", "batch"), axis=0, tiled=True),
    )
    normed_one, unit_one, inverse_one = normalize(
        values, gain_one.astype(jnp.float32), shift_one.astype(jnp.float32)
    )
    first_input = normed_one.astype(jnp.bfloat16)
    joint_value = (
        jnp.dot(first_input, joint_all, preferred_element_type=jnp.float32)
        + bias_all.astype(jnp.float32)
    ).reshape(seq_count, local_rows, 3 * model_width)
    queries = rotate(
        joint_value[..., :model_width].reshape(seq_count, local_rows, HEADS, HEAD_DIM),
        cosine_table,
        sine_table,
    ).astype(jnp.bfloat16)
    key_rows = rotate(
        joint_value[..., model_width : 2 * model_width].reshape(
            seq_count, local_rows, HEADS, HEAD_DIM
        ),
        cosine_table,
        sine_table,
    ).astype(jnp.bfloat16)
    value_flat = joint_value[..., 2 * model_width :].astype(jnp.bfloat16)
    value_rows = value_flat.reshape(seq_count, local_rows, HEADS, HEAD_DIM)
    key_flat = key_rows.reshape(seq_count, local_rows, model_width)

    def forward_step(carried, blocks, offset):
        running_max, denominator, weighted = carried
        block_rows = blocks[0].shape[1]
        key_block = blocks[0].reshape(seq_count, block_rows, HEADS, HEAD_DIM)
        value_block = blocks[1].reshape(seq_count, block_rows, HEADS, HEAD_DIM)
        scores = (
            jnp.einsum("sqhe,skhe->shqk", queries, key_block, preferred_element_type=jnp.float32)
            * score_scale
        )
        allowed = (
            (offset + jnp.arange(block_rows, dtype=jnp.int32))[None, :] <= positions[:, None]
        )[None, None]
        scores = jnp.where(allowed, scores, NEGATIVE)
        new_max = jnp.maximum(running_max, jnp.max(scores, axis=-1))
        factor = jnp.exp(running_max - new_max)
        exponent = jnp.where(allowed, jnp.exp(scores - new_max[..., None]), 0.0)
        denominator = denominator * factor + jnp.sum(exponent, axis=-1)
        weighted = weighted * factor[..., None] + jnp.einsum(
            "shqk,skhe->shqe",
            exponent.astype(jnp.bfloat16),
            value_block,
            preferred_element_type=jnp.float32,
        )
        return (new_max, denominator, weighted)

    start_state = (
        jnp.full((seq_count, HEADS, local_rows), NEGATIVE, jnp.float32),
        jnp.zeros((seq_count, HEADS, local_rows), jnp.float32),
        jnp.zeros((seq_count, HEADS, local_rows, HEAD_DIM), jnp.float32),
    )
    running_max, denominator, weighted = over_blocks(
        forward_step,
        start_state,
        (
            lax.all_gather(key_flat, "seq", axis=1, tiled=True),
            lax.all_gather(value_flat, "seq", axis=1, tiled=True),
        ),
    )
    context = jnp.transpose(weighted / denominator[..., None], (0, 2, 1, 3))
    logsum_hq = running_max + jnp.log(denominator)
    mixed = context.reshape(flat_rows, model_width).astype(jnp.bfloat16)
    middle = values + jnp.dot(mixed, output_all, preferred_element_type=jnp.float32)
    gate_all, up_all, down_all, gain_two, shift_two = (
        lax.all_gather(gate_weight, ("seq", "batch"), axis=0, tiled=True),
        lax.all_gather(up_weight, ("seq", "batch"), axis=0, tiled=True),
        lax.all_gather(down_weight, ("seq", "batch"), axis=0, tiled=True),
        lax.all_gather(feedfwd_gain, ("seq", "batch"), axis=0, tiled=True),
        lax.all_gather(feedfwd_shift, ("seq", "batch"), axis=0, tiled=True),
    )
    normed_two, unit_two, inverse_two = normalize(
        middle, gain_two.astype(jnp.float32), shift_two.astype(jnp.float32)
    )
    second_input = normed_two.astype(jnp.bfloat16)
    gate_value = jnp.dot(second_input, gate_all, preferred_element_type=jnp.float32)
    up_value = jnp.dot(second_input, up_all, preferred_element_type=jnp.float32)
    gate_sigmoid = jax.nn.sigmoid(gate_value)
    activated = gate_value * gate_sigmoid
    hidden = (activated * up_value).astype(jnp.bfloat16)
    result = middle + jnp.einsum("qf,df->qd", hidden, down_all, preferred_element_type=jnp.float32)
    chosen = language[:, None] == jnp.arange(LANGS, dtype=jnp.int32)[None, :]
    row_scale = jnp.sum(jnp.where(chosen, language_weight[None, :], 0.0), axis=1)
    cotangent = (output_grad * row_scale[:, None, None]).reshape(flat_rows, model_width)
    down_grad = cotangent.astype(jnp.bfloat16)
    gate_all, up_all, down_all, gain_two, shift_two = (
        lax.all_gather(gate_weight, ("seq", "batch"), axis=0, tiled=True),
        lax.all_gather(up_weight, ("seq", "batch"), axis=0, tiled=True),
        lax.all_gather(down_weight, ("seq", "batch"), axis=0, tiled=True),
        lax.all_gather(feedfwd_gain, ("seq", "batch"), axis=0, tiled=True),
        lax.all_gather(feedfwd_shift, ("seq", "batch"), axis=0, tiled=True),
    )
    hidden_grad = jnp.dot(down_grad, down_all, preferred_element_type=jnp.float32)
    gate_slope = gate_sigmoid * (1.0 + gate_value * (1.0 - gate_sigmoid))
    gate_grad = (hidden_grad * up_value * gate_slope).astype(jnp.bfloat16)
    up_grad = (hidden_grad * activated).astype(jnp.bfloat16)
    second_grad = jnp.einsum(
        "qf,df->qd", gate_grad, gate_all, preferred_element_type=jnp.float32
    ) + jnp.einsum("qf,df->qd", up_grad, up_all, preferred_element_type=jnp.float32)
    middle_grad = cotangent + norm_back(
        second_grad, unit_two, inverse_two, gain_two.astype(jnp.float32)
    )
    attn_grad = middle_grad.astype(jnp.bfloat16)
    contract = (((0,), (0,)), ((), ()))
    joint_all, output_all, bias_all, gain_one, shift_one = (
        lax.all_gather(joint_weight, ("seq", "batch"), axis=0, tiled=True),
        lax.all_gather(output_weight, ("seq", "batch"), axis=0, tiled=True),
        lax.all_gather(joint_bias, ("seq", "batch"), axis=0, tiled=True),
        lax.all_gather(attention_gain, ("seq", "batch"), axis=0, tiled=True),
        lax.all_gather(attention_shift, ("seq", "batch"), axis=0, tiled=True),
    )
    context_flat = jnp.einsum(
        "qo,io->qi", attn_grad, output_all, preferred_element_type=jnp.float32
    ).astype(jnp.bfloat16)
    context_grad = context_flat.reshape(seq_count, local_rows, HEADS, HEAD_DIM)
    balance = jnp.sum(context_grad.astype(jnp.float32) * context, axis=-1)
    balance_hq = jnp.transpose(balance, (0, 2, 1))
    logsum = jnp.transpose(logsum_hq, (0, 2, 1))

    def query_step(carried, blocks, offset):
        block_rows = blocks[0].shape[1]
        key_block = blocks[0].reshape(seq_count, block_rows, HEADS, HEAD_DIM)
        value_block = blocks[1].reshape(seq_count, block_rows, HEADS, HEAD_DIM)
        scores = (
            jnp.einsum("sqhe,skhe->shqk", queries, key_block, preferred_element_type=jnp.float32)
            * score_scale
        )
        allowed = (
            (offset + jnp.arange(block_rows, dtype=jnp.int32))[None, :] <= positions[:, None]
        )[None, None]
        scores = jnp.where(allowed, scores, NEGATIVE)
        probabilities = jnp.where(allowed, jnp.exp(scores - logsum_hq[..., None]), 0.0)
        value_dots = jnp.einsum(
            "sqhe,skhe->shqk", context_grad, value_block, preferred_element_type=jnp.float32
        )
        score_grad = (probabilities * (value_dots - balance_hq[..., None])).astype(jnp.bfloat16)
        return carried + jnp.einsum(
            "shqk,skhe->sqhe", score_grad, key_block, preferred_element_type=jnp.float32
        )

    zero_rows = jnp.zeros((seq_count, local_rows, HEADS, HEAD_DIM), jnp.float32)
    query_grad = (
        over_blocks(
            query_step,
            zero_rows,
            (
                lax.all_gather(key_flat, "seq", axis=1, tiled=True),
                lax.all_gather(value_flat, "seq", axis=1, tiled=True),
            ),
        )
        * score_scale
    )

    def key_step(carried, blocks, offset):
        key_acc, value_acc = carried
        block_rows = blocks[0].shape[1]
        query_block = blocks[0].astype(jnp.bfloat16).reshape(seq_count, block_rows, HEADS, HEAD_DIM)
        grad_block = blocks[1].astype(jnp.bfloat16).reshape(seq_count, block_rows, HEADS, HEAD_DIM)
        logsum_block = jnp.transpose(blocks[2], (0, 2, 1))
        balance_block = jnp.transpose(blocks[3], (0, 2, 1))
        scores = (
            jnp.einsum("sqhe,skhe->shqk", query_block, key_rows, preferred_element_type=jnp.float32)
            * score_scale
        )
        allowed = (
            positions[None, :] <= (offset + jnp.arange(block_rows, dtype=jnp.int32))[:, None]
        )[None, None]
        scores = jnp.where(allowed, scores, NEGATIVE)
        probabilities = jnp.where(allowed, jnp.exp(scores - logsum_block[..., None]), 0.0)
        value_acc = value_acc + jnp.einsum(
            "shqk,sqhe->skhe",
            probabilities.astype(jnp.bfloat16),
            grad_block,
            preferred_element_type=jnp.float32,
        )
        value_dots = jnp.einsum(
            "sqhe,skhe->shqk", grad_block, value_rows, preferred_element_type=jnp.float32
        )
        score_grad = (probabilities * (value_dots - balance_block[..., None])).astype(jnp.bfloat16)
        key_acc = key_acc + jnp.einsum(
            "shqk,sqhe->skhe", score_grad, query_block, preferred_element_type=jnp.float32
        )
        return (key_acc, value_acc)

    query_send = queries.reshape(seq_count, local_rows, model_width).astype(jnp.float32)
    context_send = context_flat.reshape(seq_count, local_rows, model_width).astype(jnp.float32)
    key_grad, value_grad = over_blocks(
        key_step,
        (zero_rows, zero_rows),
        (
            lax.all_gather(query_send, "seq", axis=1, tiled=True),
            lax.all_gather(context_send, "seq", axis=1, tiled=True),
            lax.all_gather(logsum, "seq", axis=1, tiled=True),
            lax.all_gather(balance, "seq", axis=1, tiled=True),
        ),
    )
    key_grad = key_grad * score_scale
    joint_grad = jnp.concatenate(
        [
            unrotate(query_grad, cosine_table, sine_table).reshape(flat_rows, model_width),
            unrotate(key_grad, cosine_table, sine_table).reshape(flat_rows, model_width),
            value_grad.reshape(flat_rows, model_width),
        ],
        axis=1,
    ).astype(jnp.bfloat16)
    first_grad = jnp.einsum("qj,dj->qd", joint_grad, joint_all, preferred_element_type=jnp.float32)
    token_grad = middle_grad + norm_back(
        first_grad, unit_one, inverse_one, gain_one.astype(jnp.float32)
    )
    vector_sums = (
        lax.psum_scatter(
            jnp.sum(first_grad * unit_one, axis=0),
            ("seq", "batch"),
            scatter_dimension=0,
            tiled=True,
        ),
        lax.psum_scatter(
            jnp.sum(first_grad, axis=0), ("seq", "batch"), scatter_dimension=0, tiled=True
        ),
        lax.psum_scatter(
            jnp.sum(joint_grad.astype(jnp.float32), axis=0),
            ("seq", "batch"),
            scatter_dimension=0,
            tiled=True,
        ),
        lax.psum_scatter(
            jnp.sum(second_grad * unit_two, axis=0),
            ("seq", "batch"),
            scatter_dimension=0,
            tiled=True,
        ),
        lax.psum_scatter(
            jnp.sum(second_grad, axis=0), ("seq", "batch"), scatter_dimension=0, tiled=True
        ),
    )
    weight_sums = lax.psum_scatter(
        jnp.concatenate(
            [
                jnp.concatenate(
                    [
                        lax.dot_general(
                            first_input, joint_grad, contract, preferred_element_type=jnp.float32
                        ),
                        lax.dot_general(
                            mixed, attn_grad, contract, preferred_element_type=jnp.float32
                        ),
                    ],
                    axis=1,
                ),
                jnp.concatenate(
                    [
                        lax.dot_general(
                            second_input, gate_grad, contract, preferred_element_type=jnp.float32
                        ),
                        lax.dot_general(
                            second_input, up_grad, contract, preferred_element_type=jnp.float32
                        ),
                        lax.dot_general(
                            down_grad, hidden, contract, preferred_element_type=jnp.float32
                        ),
                    ],
                    axis=1,
                ),
            ],
            axis=1,
        ),
        ("seq", "batch"),
        scatter_dimension=0,
        tiled=True,
    )
    ff_width = gate_value.shape[1]
    grad_joint = weight_sums[:, : 3 * model_width]
    grad_output = weight_sums[:, 3 * model_width : 4 * model_width]
    grad_gate = weight_sums[:, 4 * model_width : 4 * model_width + ff_width]
    grad_up = weight_sums[:, 4 * model_width + ff_width : 4 * model_width + 2 * ff_width]
    grad_down = weight_sums[:, 4 * model_width + 2 * ff_width :]
    result_out = result.reshape(seq_count, local_rows, model_width)
    token_out = token_grad.reshape(seq_count, local_rows, model_width)
    return (
        result_out,
        token_out,
        vector_sums[0],
        vector_sums[1],
        grad_joint,
        vector_sums[2],
        grad_output,
        vector_sums[3],
        vector_sums[4],
        grad_gate,
        grad_up,
        grad_down,
    )


def solution(mesh):
    return jax.shard_map(
        body,
        mesh=mesh,
        in_specs=(
            P("batch", "seq", None),
            P("batch"),
            P(),
            P("batch", "seq", None),
            P(("seq", "batch")),
            P(("seq", "batch")),
            P(("seq", "batch"), None),
            P(("seq", "batch")),
            P(("seq", "batch"), None),
            P(("seq", "batch")),
            P(("seq", "batch")),
            P(("seq", "batch"), None),
            P(("seq", "batch"), None),
            P(("seq", "batch"), None),
        ),
        out_specs=(
            P("batch", "seq", None),
            P("batch", "seq", None),
            P(("seq", "batch")),
            P(("seq", "batch")),
            P(("seq", "batch"), None),
            P(("seq", "batch")),
            P(("seq", "batch"), None),
            P(("seq", "batch")),
            P(("seq", "batch")),
            P(("seq", "batch"), None),
            P(("seq", "batch"), None),
            P(("seq", "batch"), None),
        ),
        check_vma=False,
    )
```

profile of v0, /device:TPU:8, one launch (start us, length us, event | category | flops | bytes accessed | tf_op | source)
XLA Modules:
  0.0 3324.9 jit_solution(9967611302763725659)
XLA Ops:
  12.2 42.0 %all-reduce.11 = (bf16[6144]{0:T(1024)(128)(2,1)S(1)}, bf16[2048]{0:T(1024)(128)(2,1)S(1)}, bf16[2048]{0:T(1024)(128)(2,1)S(1)}, bf16[2048]{0:T(1024)(128)(2,1)S(1)}, bf16[2048]{0:T(1024)(128)(2,1)S(1)}) all-reduce(bf16[6144]{0:T(1024)(128)(2,1)S(1)} %dynamic-update-slice.2, ...), channel_id=1, replica_groups=mesh['seq'=8,'batch'=4] {'seq','batch'}, use_global_device_ids=true, to_apply=%add.2 | all-reduce | flops 14336 | bytes 57344
  57.2 109.2 %all-gather.12.cloned.1.call-done = bf16[2048,6144]{1,0:T(8,128)(2,1)} async-done(((bf16[64,6144]{1,0:T(8,128)(2,1)}), bf16[2048,6144]{1,0:T(8,128)(2,1)}) %all-gather.12.cloned.1.call-update) | async-done | bytes 25165840 | tf_op jit(solution)/shard_map/all_gather | solution.py:117
  166.4 10.4 fusion.72
  188.8 61.8 %all-gather.16.cloned.1.call-done = bf16[1,1024,2048]{2,1,0:T(8,128)(2,1)} async-done(((bf16[1,128,2048]{2,1,0:T(8,128)(2,1)}), bf16[1,1024,2048]{2,1,0:T(8,128)(2,1)}) %all-gather.16.cloned.1.call-update) | async-done | bytes 4194320 | tf_op jit(solution)/shard_map/all_gather | solution.py:182
  256.9 68.2 %all-gather.14.cloned.1.call-done = bf16[1,1024,2048]{2,1,0:T(8,128)(2,1)} async-done(((bf16[1,128,2048]{2,1,0:T(8,128)(2,1)}), bf16[1,1024,2048]{2,1,0:T(8,128)(2,1)}) %all-gather.14.cloned.1.call-update) | async-done | bytes 4194320 | tf_op jit(solution)/shard_map/all_gather | solution.py:181
  331.3 22.2 while.39
  354.9 49.4 %all-gather.18.cloned.1.call-done = bf16[2048,2048]{1,0:T(8,128)(2,1)} async-done(((bf16[64,2048]{1,0:T(8,128)(2,1)}), bf16[2048,2048]{1,0:T(8,128)(2,1)}) %all-gather.18.cloned.1.call-update) | async-done | bytes 8388624 | tf_op jit(solution)/shard_map/all_gather | solution.py:118
  409.6 138.9 %all-gather.22.cloned.1.call-done = bf16[2048,5632]{1,0:T(8,128)(2,1)} async-done(((bf16[64,5632]{1,0:T(8,128)(2,1)}), bf16[2048,5632]{1,0:T(8,128)(2,1)}) %all-gather.22.cloned.1.call-update) | async-done | bytes 23068688 | tf_op jit(solution)/shard_map/all_gather | solution.py:191
  548.5 12.4 fusion.86
  560.8 133.2 %all-gather.20.cloned.1.call-done = bf16[2048,5632]{1,0:T(8,128)(2,1)} async-done(((bf16[64,5632]{1,0:T(8,128)(2,1)}), bf16[2048,5632]{1,0:T(8,128)(2,1)}) %all-gather.20.cloned.1.call-update) | async-done | bytes 23068688 | tf_op jit(solution)/shard_map/all_gather | solution.py:190
  694.0 12.3 fusion.85
  706.4 133.4 %all-gather.24.cloned.1.call-done = bf16[2048,5632]{1,0:T(8,128)(2,1)} async-done(((bf16[64,5632]{1,0:T(8,128)(2,1)}), bf16[2048,5632]{1,0:T(8,128)(2,1)}) %all-gather.24.cloned.1.call-update) | async-done | bytes 23068688 | tf_op jit(solution)/shard_map/all_gather | solution.py:192
  839.7 15.6 multiply_convert_fusion.6
  855.3 22.6 fusion.87
  878.0 14.5 multiply_reduce_fusion
  905.6 30.0 all_gather.70
  936.0 31.2 all-gather.1
  967.3 37.7 %while.40 = (s32[]{:T(128)}, f32[1,128,32,64]{1,3,2,0:T(8,128)}, bf16[2,1,512,2048]{2,3,1,0:T(8,128)(2,1)}, s32[2]{0:T(128)S(1)}, bf16[1,128,32,64]{1,3,2,0:T(8,...) while((s32[]{:T(128)}, f32[1,128,32,64]{1,3,2,0:T(8,128)}, ...), condition=%wide.region_13.14_spmd.clone, body=%wide.region_12.13_spmd.clone.sunk | while | flops 820576896 | bytes 34772124 | solution.py:87
  977.1 9.0 fusion.158
  995.9 9.1 fusion.158
  1014.0 67.7 %while.41 = (s32[]{:T(128)}, f32[1,128,32,64]{1,3,2,0:T(8,128)}, f32[1,128,32,64]{1,3,2,0:T(8,128)}, bf16[2,1,512,2048]{3,2,0,1:T(8,128)(2,1)}, s32[2]{0:T(128)S...) while((s32[]{:T(128)}, f32[1,128,32,64]{1,3,2,0:T(8,128)}, ...), condition=%wide.region_15.16_spmd.clone, body=%wide.region_14.15_spmd.clone.sunk | while | flops 1100022400 | bytes 56497320 | solution.py:87
  1032.1 9.5 fusion.167
  1065.6 9.6 fusion.167
  1086.3 21.2 convolution_dynamic-update-slice_fusion.3
  1107.5 8.2 convolution_dynamic-update-slice_fusion.4
  1115.7 18.0 convolution_dynamic-update-slice_fusion.2
  1133.7 18.1 convolution_dynamic-update-slice_fusion.1
  1151.7 18.6 convolution_dynamic-update-slice_fusion
  1171.5 14.0 fusion.74
  1186.1 14.1 multiply_reduce_fusion.1
  1200.2 54.9 %all-reduce.10 = (f32[2048]{0:T(1024)S(1)}, f32[2048]{0:T(1024)S(1)}, f32[6144]{0:T(1024)S(1)}, f32[2048]{0:T(1024)S(1)}, f32[2048]{0:T(1024)S(1)}) all-reduce(f32[2048]{0:T(1024)S(1)} %get-tuple-element.377, f32[2048]{0:T(1024)S(1)} %get-tuple-element.382, ...), channel_id=4, replica_groups=mesh['seq'=8,'batch'=4] {'seq','batch'}, use_global_device_ids=true, to_apply=%region_19.20.clone | all-reduce | flops 14336 | bytes 114688
  1259.5 2049.4 %reduce-scatter.2.cloned.1.call-done = f32[64,25088]{1,0:T(8,128)} async-done(((f32[2048,25088]{1,0:T(8,128)}), f32[64,25088]{1,0:T(8,128)}) %reduce-scatter.2.cloned.1.call-update) | async-done | bytes 6422544 | tf_op jit(solution)/shard_map/reduce_scatter | solution.py:360
  (252 shorter events, 169.6 us)
Async XLA Ops:
  7.2 159.2 %all-gather.12.cloned.1.call-start = ((), (), s32[]{:S(2)}) async-start(), calls=%async_computation.1 | async-start | bytes 25952256 | tf_op jit(solution)/shard_map/all_gather | solution.py:117
  7.9 242.7 %all-gather.16.cloned.1.call-start = ((), (), s32[]{:S(2)}) async-start(), calls=%async_computation.3 | async-start | bytes 4718592 | tf_op jit(solution)/shard_map/all_gather | solution.py:182
  54.3 122.5 %copy-start.30 = (f32[2048]{0:T(1024)}, f32[2048]{0:T(1024)S(1)}, u32[]{:S(2)}) copy-start(f32[2048]{0:T(1024)S(1)} %convert_element_type.169) | copy-start | bytes 24580
  54.3 122.5 %copy-start.32 = (f32[2048]{0:T(1024)}, f32[2048]{0:T(1024)S(1)}, u32[]{:S(2)}) copy-start(f32[2048]{0:T(1024)S(1)} %convert_element_type.170) | copy-start | bytes 24580
  55.7 121.1 %copy-start.38 = (f32[128]{0:T(128)}, f32[128]{0:T(128)S(1)}, u32[]{:S(2)}) copy-start(f32[128]{0:T(128)S(1)} %broadcast_multiply_fusion.7) | copy-start | bytes 1540
  57.2 119.6 %copy-start.42 = (f32[128]{0:T(128)}, f32[128]{0:T(128)S(1)}, u32[]{:S(2)}) copy-start(f32[128]{0:T(128)S(1)} %add_rsqrt_fusion.1) | copy-start | bytes 1540
  177.7 147.3 %all-gather.14.cloned.1.call-start = ((), (), s32[]{:S(2)}) async-start(), calls=%async_computation.2 | async-start | bytes 4718592 | tf_op jit(solution)/shard_map/all_gather | solution.py:181
  182.7 74.1 %copy-start.5 = (bf16[1,128,32,64]{1,3,2,0:T(8,128)(2,1)}, bf16[1,128,32,64]{1,3,2,0:T(8,128)(2,1)S(1)}, u32[]{:S(2)}) copy-start(bf16[1,128,32,64]{1,3,2,0:T(8,128)(2,1)S(1)} %maximum_convert_fusion) | copy-start | bytes 1572868
  183.8 220.5 %all-gather.18.cloned.1.call-start = ((), (), s32[]{:S(2)}) async-start(), calls=%async_computation.4 | async-start | bytes 8650752 | tf_op jit(solution)/shard_map/all_gather | solution.py:118
  184.3 364.1 %all-gather.22.cloned.1.call-start = ((), (), s32[]{:S(2)}) async-start(), calls=%async_computation.6 | async-start | bytes 23789568 | tf_op jit(solution)/shard_map/all_gather | solution.py:191
  184.9 509.1 %all-gather.20.cloned.1.call-start = ((), (), s32[]{:S(2)}) async-start(), calls=%async_computation.5 | async-start | bytes 23789568 | tf_op jit(solution)/shard_map/all_gather | solution.py:190
  185.5 654.2 %all-gather.24.cloned.1.call-start = ((), (), s32[]{:S(2)}) async-start(), calls=%async_computation.7 | async-start | bytes 23789568 | tf_op jit(solution)/shard_map/all_gather | solution.py:192
  186.3 821.1 %all-gather.26.cloned.1.call-start = ((), (), s32[]{:S(2)}) async-start(), calls=%async_computation.8 | async-start | bytes 4718592 | tf_op jit(solution)/shard_map/all_gather | solution.py:315
  188.6 825.4 %all-gather.28.cloned.1.call-start = ((), (), s32[]{:S(2)}) async-start(), calls=%async_computation.10 | async-start | bytes 4718592 | tf_op jit(solution)/shard_map/all_gather | solution.py:316
  331.3 73.0 %copy-start.1 = (f32[1,128,2048]{2,1,0:T(8,128)S(1)}, f32[1,128,2048]{2,1,0:T(8,128)}, u32[]{:S(2)}) copy-start(f32[1,128,2048]{2,1,0:T(8,128)} %param.20) | copy-start | bytes 3145732
  354.9 54.1 %copy-start.16 = (bf16[1,128,32,64]{1,3,2,0:T(8,128)(2,1)}, bf16[1,128,32,64]{1,3,2,0:T(8,128)(2,1)S(1)}, u32[]{:S(2)}) copy-start(bf16[1,128,32,64]{1,3,2,0:T(8,128)(2,1)S(1)} %bitcast_convert_fusion.1) | copy-start | bytes 1572868
  409.0 483.5 %copy-start.3 = (f32[128,2048]{1,0:T(8,128)}, f32[128,2048]{1,0:T(8,128)S(1)}, u32[]{:S(2)}) copy-start(f32[128,2048]{1,0:T(8,128)S(1)} %get-tuple-element.488) | copy-start | bytes 3145732
  409.6 284.4 %copy-start.9 = (bf16[128,2048]{1,0:T(8,128)(2,1)}, bf16[128,2048]{1,0:T(8,128)(2,1)S(1)}, u32[]{:S(2)}) copy-start(bf16[128,2048]{1,0:T(8,128)(2,1)S(1)} %add_convert_fusion) | copy-start | bytes 1572868
  855.3 22.6 copy-start.13
  855.3 22.6 copy-start.11
  877.9 14.5 copy-start.18
  895.9 39.8 %copy-start.27 = (f32[1,32,128,64]{2,3,1,0:T(8,128)S(1)}, f32[1,32,128,64]{2,3,1,0:T(8,128)}, u32[]{:S(2)}) copy-start(f32[1,32,128,64]{2,3,1,0:T(8,128)} %get-tuple-element.171) | copy-start | bytes 3145732
  903.1 2405.8 %reduce-scatter.2.cloned.1.call-start = ((), (), s32[]{:S(2)}) async-start(), calls=%async_computation.9 | async-start | bytes 211943424 | tf_op jit(solution)/shard_map/reduce_scatter | solution.py:360
  1013.9 69.2 %copy-start.35 = (f32[128,8]{0,1:T(8,128)S(1)}, f32[128,8]{0,1:T(8,128)}, u32[]{:S(2)}) copy-start(f32[128,8]{0,1:T(8,128)} %copy-done.34) | copy-start | bytes 12292
  1013.9 69.2 %copy-start.37 = (f32[128,8]{0,1:T(8,128)S(1)}, f32[128,8]{0,1:T(8,128)}, u32[]{:S(2)}) copy-start(f32[128,8]{0,1:T(8,128)} %copy-done.36) | copy-start | bytes 12292
  1086.3 21.2 copy-start.8
  1086.3 21.2 copy-start.17
  1115.7 18.0 copy-start.12
  1133.7 18.1 copy-start.15
  1133.7 18.1 copy-start.19
  1186.1 14.1 copy-start.40
  1186.1 14.1 copy-start.41
  (25 other events, 133.3 us)
Sparse Core Ops, SparseCore 0:
  10.9 155.4 all-gather.11
  177.8 72.7 all-gather.15
  253.3 71.6 all-gather.13
  327.7 76.5 all-gather.17
  407.0 141.4 all-gather.21
  551.2 142.7 all-gather.19
  696.9 142.7 all-gather.23
  841.8 73.2 all-gather.25
  917.8 74.4 all-gather.27
  1170.5 2138.4 reduce-scatter.1
where the time goes:
time: 3330 us; the launch traced here: 3320 us
  waiting for transfers between devices  2750 us (83%)
  matrix products  290 us (9%)
  blocking collectives  158 us (5%)
  local copies, waits for them, and re-layouts  87.4 us (3%)
    reduce_scatter x1, waiting for transfers between devices, body(): lax.psum_scatter(jnp.concatenate([jnp.concatenate([lax.dot_general(first_...  2050 us
    all_gather x1, waiting for transfers between devices, body(): lax.all_gather(up_weight, ('seq', 'batch'), axis=0, tiled=True)  139 us
    all_gather x1, waiting for transfers between devices, body(): lax.all_gather(down_weight, ('seq', 'batch'), axis=0, tiled=True)  133 us
    all_gather x1, waiting for transfers between devices, body(): lax.all_gather(gate_weight, ('seq', 'batch'), axis=0, tiled=True)  133 us
    all_gather x1, waiting for transfers between devices, body(): lax.all_gather(joint_weight, ('seq', 'batch'), axis=0, tiled=True)  109 us
    unnamed x2, blocking collectives  96.9 us
    all_gather x1, waiting for transfers between devices, body(): lax.all_gather(key_flat, 'seq', axis=1, tiled=True)  68.2 us
  transfers between devices with their start and end apart: 10, of which 8 were waited for; matrix products, arithmetic and copies ran while one was open for 7% of the time, Pallas kernels for 0%

commit v1 on v0

v1 whole, which is shorter than its diff:
```python
import math

import numpy as np

import jax
import jax.numpy as jnp
from jax import lax
from jax.experimental import pallas as pl
from jax.experimental.pallas import tpu as pltpu
from jax.sharding import PartitionSpec as P

HEADS = 32
HEAD_DIM = 64
ROT_DIMS = 16
LANGS = 7

EPSILON = 1e-05
THETA_BASE = 10000.0
NEGATIVE = -1e30
VMEM_BYTES = 56 * 1024 * 1024

bf16 = jnp.bfloat16
f32 = jnp.float32


def swap(value, axis, number, bit):
    return lax.ppermute(value, axis, [(i, i ^ bit) for i in range(number)])


def bits_of(number):
    return [1 << i for i in range(number.bit_length() - 1)]


def tie(*values):
    return lax.optimization_barrier(values)


def after(value, *others):
    return tie(value, *others)[0]


def exchange_near(blocks, number):
    if number != 8:
        return blocks
    mine = lax.axis_index("seq") % 2
    pairs = blocks.reshape((number // 2, 2) + blocks.shape[1:])
    got = swap(lax.dynamic_slice_in_dim(pairs, 1 - mine, 1, 1), "seq", number, 1)
    return lax.dynamic_update_slice_in_dim(pairs, got, 1 - mine, 1).reshape(blocks.shape)


def exchange_far(blocks, number):
    low = 2 if number == 8 else 1
    place = lax.axis_index("seq") // low
    out = blocks.reshape((number // low, low) + blocks.shape[1:])
    parts = [
        swap(lax.dynamic_slice_in_dim(out, place ^ k, 1, 0), "seq", number, k * low)
        for k in range(1, number // low)
    ]
    for k, part in enumerate(parts):
        out = lax.dynamic_update_slice_in_dim(out, part, place ^ (k + 1), 0)
    return out.reshape(blocks.shape)


def gather_far(value, number):
    held = [(0, value)]
    for bit in reversed(bits_of(number)[1:]):
        held = held + [(k ^ bit, swap(v, "batch", number, bit)) for k, v in held]
    return held


def gather_near(held, number):
    me = lax.axis_index("batch")
    held = held + [(k ^ 1, swap(v, "batch", number, 1)) for k, v in held]
    own = held[0][1]
    out = jnp.broadcast_to(own[:, None], own.shape[:1] + (number,) + own.shape[1:])
    for k, v in held[1:]:
        out = lax.dynamic_update_slice_in_dim(out, v[:, None], me ^ k, 1)
    return out


def scatter_stage(value, number, bit):
    n, _, r, c = value.shape
    pairs = value.reshape(n, -1, 2, r, c)
    mine = (lax.axis_index("batch") // bit) % 2
    keep = lax.dynamic_index_in_dim(pairs, mine, 2, False)
    send = lax.dynamic_index_in_dim(pairs, 1 - mine, 2, False).astype(bf16)
    return keep.astype(f32) + swap(send, "batch", number, bit).astype(f32)


def scatter_near(value, number):
    return scatter_stage(value, number, 1)


def scatter_far(value, number):
    for bit in bits_of(number)[1:]:
        value = scatter_stage(value, number, bit)
    return value[:, 0].astype(bf16)


RING = (0, 2, 4, 6, 7, 5, 3, 1)


def ring_place():
    s = lax.axis_index("seq")
    return jnp.where(s % 2 == 0, s // 2, 7 - s // 2)


def ring_index(place):
    place = (place + 16) % 8
    return jnp.where(place < 4, 2 * place, 15 - 2 * place)


def ring_step(value, way):
    return lax.ppermute(value, "seq", [(RING[i], RING[(i + way) % 8]) for i in range(8)])


class Ring:
    ahead = behind = None
    taken = 0

    def tie(self, *others):
        if self.number != 8:
            return others
        self.ahead, self.behind, *others = tie(self.ahead, self.behind, *others)
        return others


class Gather(Ring):
    def __init__(self, value, number):
        self.number = number
        if number != 8:
            every = lax.all_gather(value, "seq", axis=0, tiled=False)
            self.pieces = [(i, every[i]) for i in range(number)]
            return
        self.pieces = [(lax.axis_index("seq"), value)]
        self.ahead = self.behind = value
        self.place = ring_place()

    def step(self):
        if self.number != 8:
            return
        self.taken += 1
        k = self.taken
        self.ahead = ring_step(self.ahead, 1)
        if k < 4:
            self.behind = ring_step(self.behind, -1)
            self.pieces.append((ring_index(self.place + k), self.behind))
        self.pieces.append((ring_index(self.place - k), self.ahead))


class Scatter(Ring):
    def __init__(self, block, number):
        self.number = number
        self.block = block
        self.place = ring_place()

    def step(self):
        if self.number != 8:
            return
        k = 4 - self.taken
        self.taken += 1
        part = self.block(ring_index(self.place + k))
        if self.ahead is not None:
            part = (part.astype(f32) + self.ahead.astype(f32)).astype(bf16)
        self.ahead = ring_step(part, 1)
        if k > 1:
            part = self.block(ring_index(self.place - k + 1))
            if self.behind is not None:
                part = (part.astype(f32) + self.behind.astype(f32)).astype(bf16)
            self.behind = ring_step(part, -1)

    def total(self):
        if self.number != 8:
            every = jnp.stack([self.block(i) for i in range(self.number)])
            return lax.psum_scatter(every, "seq", scatter_dimension=0, tiled=False).astype(f32)
        own = self.block(lax.axis_index("seq"))
        return own.astype(f32) + self.ahead.astype(f32) + self.behind.astype(f32)


def join(pieces, number, axis):
    at, first = pieces[0]
    size = first.shape[axis]
    shape = first.shape[:axis] + (number * size,) + first.shape[axis + 1 :]
    out = jnp.zeros(shape, first.dtype)
    for at, piece in pieces:
        out = lax.dynamic_update_slice_in_dim(out, piece, at * size, axis)
    return out


def turn_tables(length):
    half = ROT_DIMS // 2
    frequency = THETA_BASE ** (-np.arange(half, dtype=np.float32) / np.float32(half))
    angle = (np.arange(length, dtype=np.float32)[:, None] * frequency.astype(np.float32)[None]).astype(
        np.float32
    )
    cosine = np.ones((length, HEAD_DIM), np.float32)
    left = np.zeros((length, HEAD_DIM), np.float32)
    right = np.zeros((length, HEAD_DIM), np.float32)
    cosine[:, :half] = np.cos(angle)
    cosine[:, half:ROT_DIMS] = np.cos(angle)
    left[:, :half] = -np.sin(angle)
    right[:, half:ROT_DIMS] = np.sin(angle)
    return [np.concatenate([t, t], 1) for t in (cosine, left, right)]


def wide(table, columns):
    if columns < table.shape[1]:
        return table[:, :columns]
    return jnp.concatenate([table] * (columns // table.shape[1]), axis=1)


def lane_roll(value, amount):
    columns = value.shape[1]
    if columns % 128 == 0:
        return pltpu.roll(value, amount % columns, 1)
    amount = amount % columns
    return jnp.concatenate([value[:, columns - amount :], value[:, : columns - amount]], axis=1)


def turn(value, cosine, left, right):
    half = ROT_DIMS // 2
    return value * cosine + lane_roll(value, -half) * left + lane_roll(value, half) * right


def turn_back(value, cosine, left, right):
    half = ROT_DIMS // 2
    return value * cosine - lane_roll(value, -half) * left - lane_roll(value, half) * right


def head_mask(columns, head):
    lane = lax.broadcasted_iota(jnp.int32, (1, columns), 1)
    return (lane >= head * HEAD_DIM) & (lane < (head + 1) * HEAD_DIM)


def block_of(length):
    return math.gcd(length, 256)


def attend_kernel(joint_ref, cos_ref, left_ref, right_ref, low_ref, context_ref, mixed_ref, lse_ref):
    length, total = joint_ref.shape
    columns = total // 3
    heads = columns // HEAD_DIM
    block = block_of(length)
    scale = 1.0 / math.sqrt(HEAD_DIM)
    for i in range(length // block):
        rows = pl.ds(i * block, block)
        tables = [wide(t[rows, :], columns) for t in (cos_ref, left_ref, right_ref)]
        low_ref[rows, 0:columns] = (
            turn(joint_ref[rows, 0:columns], *tables).astype(bf16) * scale
        ).astype(bf16)
        low_ref[rows, columns : 2 * columns] = turn(
            joint_ref[rows, columns : 2 * columns], *tables
        ).astype(bf16)
        low_ref[rows, 2 * columns :] = joint_ref[rows, 2 * columns :].astype(bf16)
    for i in range(length // block):
        rows = pl.ds(i * block, block)
        reach = (i + 1) * block
        query = low_ref[rows, 0:columns]
        key = low_ref[0:reach, columns : 2 * columns]
        value = low_ref[0:reach, 2 * columns :]
        total_out = jnp.zeros((block, columns), f32)
        lse_all = jnp.zeros((block, 128), f32)
        lane = lax.broadcasted_iota(jnp.int32, (block, 128), 1)
        ahead = lax.broadcasted_iota(jnp.int32, (block, reach), 1) > (
            i * block + lax.broadcasted_iota(jnp.int32, (block, reach), 0)
        )
        for h in range(heads):
            mask = head_mask(columns, h)
            scores = lax.dot_general(
                jnp.where(mask, query, jnp.zeros_like(query)),
                key,
                (((1,), (1,)), ((), ())),
                preferred_element_type=f32,
            )
            scores = jnp.where(ahead, NEGATIVE, scores)
            top = jnp.max(scores, axis=1, keepdims=True)
            weight = jnp.exp(scores - top)
            denominator = jnp.sum(weight, axis=1, keepdims=True)
            probs = (weight * (1.0 / denominator)).astype(bf16)
            total_out += jnp.dot(
                probs, jnp.where(mask, value, jnp.zeros_like(value)), preferred_element_type=f32
            )
            lse_all = jnp.where(lane == h, top + jnp.log(denominator), lse_all)
        context_ref[rows, :] = total_out
        mixed_ref[rows, :] = total_out.astype(bf16)
        lse_ref[rows, :] = lse_all


def attend(joint, tables):
    length, total = joint.shape
    columns = total // 3
    return pl.pallas_call(
        attend_kernel,
        out_shape=(
            jax.ShapeDtypeStruct((length, total), bf16),
            jax.ShapeDtypeStruct((length, columns), f32),
            jax.ShapeDtypeStruct((length, columns), bf16),
            jax.ShapeDtypeStruct((length, 128), f32),
        ),
        compiler_params=pltpu.CompilerParams(vmem_limit_bytes=VMEM_BYTES),
        cost_estimate=pl.CostEstimate(
            flops=4 * length * length * columns * 2,
            bytes_accessed=16 * length * total,
            transcendentals=length * length * columns // HEAD_DIM,
        ),
        name="attend",
    )(joint, *tables)


def attend_back_kernel(
    low_ref, grad_ref, context_ref, lse_ref, cos_ref, left_ref, right_ref, out_ref, dq_ref, dk_ref, dv_ref
):
    length, total = low_ref.shape
    columns = total // 3
    heads = columns // HEAD_DIM
    block = block_of(length)
    scale = 1.0 / math.sqrt(HEAD_DIM)
    dk_ref[...] = jnp.zeros_like(dk_ref)
    dv_ref[...] = jnp.zeros_like(dv_ref)
    for i in range(length // block):
        rows = pl.ds(i * block, block)
        reach = (i + 1) * block
        query = low_ref[rows, 0:columns]
        grad = grad_ref[rows, :]
        grad_wide = grad.astype(f32)
        query_t = query.astype(f32).T.astype(bf16)
        grad_t = grad_wide.T.astype(bf16)
        product = grad_wide * context_ref[rows, :]
        key = low_ref[0:reach, columns : 2 * columns]
        value = low_ref[0:reach, 2 * columns :]
        dq = jnp.zeros((block, columns), f32)
        ahead = lax.broadcasted_iota(jnp.int32, (block, reach), 1) > (
            i * block + lax.broadcasted_iota(jnp.int32, (block, reach), 0)
        )
        for h in range(heads):
            mask = head_mask(columns, h)
            span = slice(h * HEAD_DIM, (h + 1) * HEAD_DIM)
            scores = lax.dot_general(
                jnp.where(mask, query, jnp.zeros_like(query)),
                key,
                (((1,), (1,)), ((), ())),
                preferred_element_type=f32,
            )
            scores = jnp.where(ahead, NEGATIVE, scores)
            probs = jnp.exp(scores - lse_ref[rows, h : h + 1])
            dots = lax.dot_general(
                jnp.where(mask, grad, jnp.zeros_like(grad)),
                value,
                (((1,), (1,)), ((), ())),
                preferred_element_type=f32,
            )
            balance = jnp.sum(jnp.where(mask, product, 0.0), axis=1, keepdims=True)
            score_grad = (probs * (dots - balance)).astype(bf16)
            dq += jnp.dot(
                score_grad, jnp.where(mask, key, jnp.zeros_like(key)), preferred_element_type=f32
            )
            dk_ref[span, 0:reach] += jnp.dot(query_t[span], score_grad, preferred_element_type=f32)
            dv_ref[span, 0:reach] += jnp.dot(
                grad_t[span], probs.astype(bf16), preferred_element_type=f32
            )
        dq_ref[rows, :] = dq
    for i in range(length // block):
        rows = pl.ds(i * block, block)
        tables = [wide(t[rows, :], columns) for t in (cos_ref, left_ref, right_ref)]
        out_ref[rows, 0:columns] = turn_back(dq_ref[rows, :] * scale, *tables).astype(bf16)
        out_ref[rows, columns : 2 * columns] = turn_back(dk_ref[:, rows].T, *tables).astype(bf16)
        out_ref[rows, 2 * columns :] = dv_ref[:, rows].T.astype(bf16)


def attend_back(low, grad, context, lse, tables):
    length, total = low.shape
    columns = total // 3
    return pl.pallas_call(
        attend_back_kernel,
        out_shape=jax.ShapeDtypeStruct((length, total), bf16),
        scratch_shapes=[
            pltpu.VMEM((length, columns), f32),
            pltpu.VMEM((columns, length), f32),
            pltpu.VMEM((columns, length), f32),
        ],
        compiler_params=pltpu.CompilerParams(vmem_limit_bytes=VMEM_BYTES),
        cost_estimate=pl.CostEstimate(
            flops=10 * length * length * columns * 2,
            bytes_accessed=16 * length * total,
            transcendentals=length * length * columns // HEAD_DIM,
        ),
        name="attend_back",
    )(low, grad, context, lse, *tables)


def mean_of(values):
    return jnp.mean(values, axis=-1, keepdims=True)


def unit_of(values):
    center = values - mean_of(values)
    inverse_std = lax.rsqrt(mean_of(center * center) + EPSILON)
    return center * inverse_std, inverse_std


def norm_back(incoming, unit_rows, inverse_std, gain_values):
    inner = incoming * gain_values
    return inverse_std * (inner - mean_of(inner) - unit_rows * mean_of(inner * unit_rows))


def dot(left, right, contract):
    return lax.dot_general(left, right, (contract, ((), ())), preferred_element_type=f32)


def make_body(n_seq, n_batch):
    def body(
        tokens,
        language,
        language_weight,
        output_grad,
        attention_gain,
        attention_shift,
        joint_weight,
        joint_bias,
        output_weight,
        feedfwd_gain,
        feedfwd_shift,
        gate_weight,
        up_weight,
        down_weight,
    ):
        _, local, width = tokens.shape
        rows, ff_width = gate_weight.shape
        length = local * n_seq
        columns = width // n_seq
        tiles = -(-ff_width // (128 * n_seq))
        ff_local = 128 * tiles
        seq_at = lax.axis_index("seq")
        first_row = seq_at * local
        values = tokens[0]
        tables = [jnp.asarray(t) for t in turn_tables(length)]

        center_own = values - mean_of(values)
        inverse_one = lax.rsqrt(mean_of(center_own * center_own) + EPSILON)
        unit_own = center_own * inverse_one
        ring = Gather(center_own.astype(bf16), n_seq)

        small = jnp.concatenate(
            [attention_gain, attention_shift, feedfwd_gain, feedfwd_shift, joint_bias]
        )
        extra = -(-small.shape[0] // (3 * columns))
        small = jnp.pad(small, (0, 8 * 3 * columns - small.shape[0])).reshape(8, 3 * columns)
        blocks = jnp.transpose(joint_weight.reshape(rows, 3, n_seq, columns), (2, 0, 1, 3))
        blocks = blocks.reshape(n_seq, rows, 3 * columns)
        blocks = jnp.concatenate(
            [blocks, jnp.broadcast_to(small[None], (n_seq,) + small.shape)], axis=1
        )
        ff_blocks = [
            jnp.pad(w, ((0, 0), (0, n_seq * ff_local - ff_width))).reshape(rows, tiles, n_seq, 128)
            for w in (gate_weight, up_weight, down_weight)
        ]
        ff_blocks = jnp.transpose(jnp.stack(ff_blocks, 1), (3, 0, 1, 2, 4))
        ff_blocks = ff_blocks.reshape(n_seq, rows, 3 * ff_local)

        ring.step()
        blocks = exchange_near(blocks, n_seq)
        ff_blocks = after(ff_blocks, blocks)
        ff_blocks = exchange_near(ff_blocks, n_seq)
        (blocks,) = ring.tie(blocks)
        ring.step()
        blocks = exchange_far(blocks, n_seq)
        blocks, ff_blocks = ring.tie(blocks, ff_blocks)
        ring.step()
        held = gather_far(blocks, n_batch)
        ff_blocks = exchange_far(ff_blocks, n_seq)
        (tied,) = ring.tie(held[-1][1])
        held[-1] = (held[-1][0], tied)
        ring.step()
        joint_all = gather_near(held, n_batch)
        center = join(ring.pieces, n_seq, 0)
        joint_all, center, ff_blocks = tie(joint_all, center, ff_blocks)
        ff_held = gather_far(ff_blocks, n_batch)
        small = joint_all[:, :, rows : rows + extra].reshape(n_seq, n_batch, -1)
        joint_all = joint_all[:, :, :rows].reshape(width, 3 * columns)
        piece = width // (n_seq * n_batch)

        def small_part(start, size):
            return small[:, :, start : start + size].reshape(1, -1).astype(f32)

        gain_one = small_part(0, piece)
        shift_one = small_part(piece, piece)
        gain_two = small_part(2 * piece, piece)
        shift_two = small_part(3 * piece, piece)
        bias_all = small_part(4 * piece, 3 * piece).reshape(3, n_seq, columns)
        bias = lax.dynamic_slice_in_dim(bias_all, seq_at, 1, 1).reshape(1, 3 * columns)

        output_all = lax.all_gather(output_weight, ("seq", "batch"), axis=0, tiled=True)

        def output_rows(at):
            return lax.dynamic_slice_in_dim(output_all, at * columns, columns, 0)

        chosen = language[:, None] == jnp.arange(LANGS, dtype=jnp.int32)[None, :]
        row_scale = jnp.sum(jnp.where(chosen, language_weight[None, :], 0.0), axis=1)
        cotangent = output_grad[0] * row_scale[:, None]
        down_grad = after(cotangent.astype(bf16), center)
        down_grad = lax.all_gather(down_grad, "seq", axis=0, tiled=True)

        unit_one, _ = unit_of(center.astype(f32))
        first_input = (unit_one * gain_one + shift_one).astype(bf16)
        joint = dot(first_input, joint_all, ((1,), (0,))) + bias
        low, context, mixed, lse = attend(joint, tables)

        ring = Gather(mixed, n_seq)
        ring.step()
        ring.tie()
        ring.step()
        ring.tie()
        ring.step()
        (tied,) = ring.tie(ff_held[-1][1])
        ff_held[-1] = (ff_held[-1][0], tied)
        ring.step()
        ff_all = gather_near(ff_held, n_batch)
        if n_seq == 8:
            at, last = ring.pieces[-1]
            early = join(ring.pieces[:-1] + [(at, jnp.zeros_like(last))], n_seq, 1)
            projected = dot(early, output_all, ((1,), (0,)))
            projected, last, ff_all = tie(projected, last, ff_all)
            projected = projected + dot(last, output_rows(at), ((1,), (0,)))
            mixed_all = lax.dynamic_update_slice_in_dim(early, last, at * columns, 1)
        else:
            mixed_all = join(ring.pieces, n_seq, 1)
            projected = dot(mixed_all, output_all, ((1,), (0,)))
        ff_all = ff_all.reshape(width, 3 * ff_local)
        gate_all = ff_all[:, :ff_local]
        up_all = ff_all[:, ff_local : 2 * ff_local]
        down_all = ff_all[:, 2 * ff_local :]
        middle_own = values + lax.dynamic_slice_in_dim(projected, first_row, local, 0)
        unit_two, inverse_two = unit_of(center.astype(f32) + projected)
        second_input = (unit_two * gain_two + shift_two).astype(bf16)

        gate = dot(second_input, gate_all, ((1,), (0,)))
        upper = dot(second_input, up_all, ((1,), (0,)))
        sigmoid = jax.nn.sigmoid(gate)
        activated = gate * sigmoid
        hidden = (activated * upper).astype(bf16)
        result_part = dot(hidden, down_all, ((1,), (1,))).astype(bf16)
        result_sum = lax.psum_scatter(result_part, "seq", scatter_dimension=0, tiled=True)

        def split(grad, *shape):
            return grad.astype(bf16).reshape((n_seq, n_batch, rows) + shape)

        grad_down = scatter_near(split(dot(down_grad, hidden, ((0,), (0,))), ff_local), n_batch)
        hidden_grad = dot(down_grad, down_all, ((1,), (0,)))
        hidden_grad, result_part = tie(hidden_grad, result_part)
        gate_grad = (hidden_grad * upper * sigmoid * (1.0 + gate * (1.0 - sigmoid))).astype(bf16)
        up_grad = (hidden_grad * activated).astype(bf16)
        second_part = dot(gate_grad, gate_all, ((1,), (1,))) + dot(up_grad, up_all, ((1,), (1,)))
        second_part, grad_down = tie(second_part, grad_down)
        grad_down = scatter_far(grad_down, n_batch)

        scaled = second_part * (gain_two * inverse_two)
        scaled_low = scaled.astype(bf16)
        sums = jnp.stack([jnp.mean(scaled, axis=-1), jnp.mean(scaled * unit_two, axis=-1)])
        sums = sums.astype(bf16).reshape(-1, columns)
        if n_seq == 8:

            def through_block(at):
                part = dot(scaled_low, output_rows(at), ((1,), (1,))).astype(bf16)
                return jnp.concatenate([part, sums], axis=0)

        else:
            through = dot(scaled_low, output_all, ((1,), (1,))).astype(bf16)

            def through_block(at):
                return jnp.concatenate([through[:, at * columns : (at + 1) * columns], sums], axis=0)

        heads_weight = output_rows(seq_at)
        ring = Scatter(through_block, n_seq)
        ring.step()
        grad_both = [split(dot(second_input, g, ((0,), (0,))), ff_local) for g in (gate_grad, up_grad)]
        grad_both = jnp.concatenate(grad_both, axis=3)
        grad_down, grad_both = ring.tie(grad_down, grad_both)
        ring.step()
        grad_both = scatter_near(grad_both, n_batch)
        grad_down = exchange_near(grad_down, n_seq)
        grad_both, grad_down = ring.tie(grad_both, grad_down)
        ring.step()
        grad_both = scatter_far(grad_both, n_batch)
        from_cot = dot(down_grad, heads_weight, ((1,), (1,)))
        from_unit = dot(unit_two.astype(bf16), heads_weight, ((1,), (1,)))
        from_cot, from_unit, result_sum = ring.tie(from_cot, from_unit, result_sum)
        ring.step()
        grad_output = dot(mixed_all, scaled_low, ((0,), (0,))).astype(bf16)
        (grad_output,) = ring.tie(grad_output)
        through = ring.total()
        through, grad_both, grad_down = tie(through, grad_both, grad_down)
        grad_both = exchange_near(grad_both, n_seq)
        grad_down = exchange_far(grad_down, n_seq)
        result = middle_own + result_sum.astype(f32)
        weight_sums = jnp.sum(heads_weight.astype(f32), axis=1)[None, :]
        means = through[length:].reshape(2, length)
        mean_one, mean_two = means[0][:, None], means[1][:, None]
        context_grad = (
            through[:length] + from_cot - mean_one * weight_sums - mean_two * from_unit
        ).astype(bf16)
        joint_grad = attend_back(low, context_grad, context, lse, tables)

        rest = down_grad.astype(f32) - mean_one - unit_two * mean_two
        rest = dot(mixed, rest.astype(bf16), ((0,), (0,)))
        rest = rest + lax.dynamic_slice_in_dim(grad_output, seq_at * columns, columns, 0)
        grad_output = lax.dynamic_update_slice_in_dim(
            grad_output, rest.astype(bf16), seq_at * columns, 0
        )
        joint_grad, grad_both, grad_down, grad_output = tie(
            joint_grad, grad_both, grad_down, grad_output
        )
        grad_joint = dot(first_input, joint_grad, ((0,), (0,)))
        first_part = dot(joint_grad, joint_all, ((1,), (1,)))

        bias_part = jnp.sum(joint_grad.astype(f32), axis=0).reshape(3, 1, columns)
        bias_part = lax.dynamic_update_slice_in_dim(
            jnp.zeros((3, n_seq, columns), f32), bias_part, seq_at, 1
        )
        vectors = [
            jnp.sum(first_part * unit_one, axis=0),
            jnp.sum(first_part, axis=0),
            jnp.sum(second_part * unit_two, axis=0),
            jnp.sum(second_part, axis=0),
            bias_part,
        ]
        vectors = jnp.concatenate([v.reshape(n_seq, n_batch, -1) for v in vectors], axis=2)
        vectors = jnp.pad(vectors, ((0, 0), (0, 0), (0, 8 * 3 * columns - vectors.shape[2])))
        vectors = vectors.reshape(n_seq, n_batch, 8, 3 * columns).astype(bf16)
        grad_joint = jnp.concatenate([split(grad_joint, 3 * columns), vectors], axis=2)
        grad_joint = scatter_near(grad_joint, n_batch)

        inner = first_part * (gain_one * lax.rsqrt(mean_of(center.astype(f32) ** 2) + EPSILON))
        first_sums = jnp.stack([jnp.mean(inner, axis=-1), jnp.mean(inner * unit_one, axis=-1)])
        both = (scaled + inner).astype(bf16)
        both, grad_joint = tie(both, grad_joint)

        def both_block(at):
            part = lax.dynamic_slice_in_dim(both, at * local, local, 0)
            below = lax.dynamic_slice_in_dim(first_sums, at * local, local, 1)
            below = jnp.pad(below.reshape(-1), (0, 8 * width - 2 * local)).reshape(8, width)
            return jnp.concatenate([part, below.astype(bf16)], axis=0)

        ring = Scatter(both_block, n_seq)
        ring.step()
        grad_joint = scatter_far(grad_joint, n_batch)
        grad_output = scatter_near(split(grad_output, width), n_batch)
        grad_joint, grad_output = ring.tie(grad_joint, grad_output)
        ring.step()
        grad_joint = exchange_near(grad_joint, n_seq)
        grad_output = scatter_far(grad_output, n_batch)
        (grad_joint,) = ring.tie(grad_joint)
        ring.step()
        grad_joint = exchange_far(grad_joint, n_seq)
        grad_joint, grad_both, grad_output = ring.tie(grad_joint, grad_both, grad_output)
        ring.step()
        grad_both = exchange_far(grad_both, n_seq)
        grad_output = lax.psum_scatter(
            grad_output, "seq", scatter_dimension=0, tiled=False
        ).astype(f32)
        both_own = ring.total()
        first_sums = both_own[local].reshape(-1)[: 2 * local].reshape(2, local)

        def own(array):
            return lax.dynamic_slice_in_dim(array, first_row, local, 0)

        token_grad = (
            cotangent
            - own(mean_one)
            - own(unit_two) * own(mean_two)
            + both_own[:local]
            - first_sums[0][:, None]
            - unit_own * first_sums[1][:, None]
        )

        def unsplit(grad):
            grad = grad.reshape(n_seq, rows, tiles, 128).astype(f32)
            return jnp.transpose(grad, (1, 2, 0, 3)).reshape(rows, n_seq * ff_local)[:, :ff_width]

        grad_gate = unsplit(grad_both[:, :, :ff_local])
        grad_up = unsplit(grad_both[:, :, ff_local:])
        grad_down = unsplit(grad_down)
        grad_joint = grad_joint.astype(f32)
        vectors = jnp.sum(grad_joint[:, rows : rows + extra], axis=0).reshape(-1)
        grad_joint = grad_joint[:, :rows].reshape(n_seq, rows, 3, columns)
        grad_joint = jnp.transpose(grad_joint, (1, 2, 0, 3)).reshape(rows, 3 * width)
        return (
            result[None],
            token_grad[None],
            vectors[:piece],
            vectors[piece : 2 * piece],
            grad_joint,
            vectors[4 * piece : 7 * piece],
            grad_output,
            vectors[2 * piece : 3 * piece],
            vectors[3 * piece : 4 * piece],
            grad_gate,
            grad_up,
            grad_down,
        )

    return body


def solution(mesh):
    rows = P(("seq", "batch"))
    matrix = P(("seq", "batch"), None)
    data = P("batch", "seq", None)
    return jax.shard_map(
        make_body(mesh.shape["seq"], mesh.shape["batch"]),
        mesh=mesh,
        in_specs=(
            data,
            P("batch"),
            P(),
            data,
            rows,
            rows,
            matrix,
            rows,
            matrix,
            rows,
            rows,
            matrix,
            matrix,
            matrix,
        ),
        out_specs=(data, data, rows, rows, matrix, rows, matrix, rows, rows, matrix, matrix, matrix),
        check_vma=False,
    )
```

time: 3330 us -> 806 us (0.24)
  waiting for transfers between devices: 2750 us -> 275 us
  blocking collectives: 158 us -> 0 us
  matrix products: 290 us -> 151 us
  starting transfers between devices: 0.61 us -> 100 us
  other arithmetic: 26 us -> 106 us
  local copies, waits for them, and re-layouts: 87.4 us -> 121 us
    reduce_scatter x1 -> x2, waiting for transfers between devices: 2050 us -> 24.3 us  [the longest x1 24.3 us: body(): lax.psum_scatter(grad_output, 'seq', scatter_dimension=0, tiled=False)]
    all_gather x8 -> x1, waiting for transfers between devices: 645 us -> 0.01 us  [body(): down_grad = lax.all_gather(down_grad, 'seq', axis=0, tiled=True)]
    ppermute x0 -> x62, waiting for transfers between devices: none -> 250 us  [the longest x34 193 us: swap(): return lax.ppermute(value, axis, [(i, i ^ bit) for i in range(number)])]
    dot_general x29 -> x26, matrix products: 290 us -> 151 us  [dot(): lax.dot_general(left, right, (contract, ((), ())), preferred_element_type...]
    ppermute x0 -> x62, starting transfers between devices: none -> 99.6 us  [the longest x34 52.4 us: swap(): return lax.ppermute(value, axis, [(i, i ^ bit) for i in range(number)])]
    unnamed x2 -> x0, blocking collectives: 96.9 us -> none
    all_gather x2 -> x0, blocking collectives: 61.2 us -> none  [the longest x1 31.2 us: body(): lax.all_gather(balance, 'seq', axis=1, tiled=True)]
    all_gather x1, waiting for transfers between devices: 49.4 us -> 0.01 us  [body(): lax.all_gather(output_weight, ('seq', 'batch'), axis=0, tiled=True)]
  transfers between devices with their start and end apart: 10 -> 66, of which waited for: 8 -> 32; matrix products, arithmetic and copies ran while one was open for 7% -> 40% of each run, Pallas kernels for 0% -> 3%
where the time goes in v1:
time: 806 us; the launch traced here: 794 us
  waiting for transfers between devices  275 us (34%)
  matrix products  151 us (19%)
  local copies, waits for them, and re-layouts  121 us (15%)
  other arithmetic  106 us (13%)
  starting transfers between devices  100 us (12%)
  Pallas kernels  25.2 us (3%)
  between operations  16.5 us (2%)
    ppermute x34, waiting for transfers between devices, swap(): return lax.ppermute(value, axis, [(i, i ^ bit) for i in range(number)])  193 us
    dot_general x26, matrix products, dot(): lax.dot_general(left, right, (contract, ((), ())), preferred_element_type...  151 us
    ppermute x28, waiting for transfers between devices, ring_step(): lax.ppermute(value, 'seq', [(RING[i], RING[(i + way) % 8]) for i in range...  57.1 us
    ppermute x34, starting transfers between devices, swap(): return lax.ppermute(value, axis, [(i, i ^ bit) for i in range(number)])  52.4 us
    ppermute x28, starting transfers between devices, ring_step(): lax.ppermute(value, 'seq', [(RING[i], RING[(i + way) % 8]) for i in range...  47.1 us
    reduce_sum x6, other arithmetic, mean_of(): return jnp.mean(values, axis=-1, keepdims=True)  25.4 us
    reduce_scatter x1, waiting for transfers between devices, body(): lax.psum_scatter(grad_output, 'seq', scatter_dimension=0, tiled=False)  24.3 us
    dynamic_update_slice x15, local copies, waits for them, and re-layouts, join(): out = lax.dynamic_update_slice_in_dim(out, piece, at * size, axis)  23.4 us
  transfers between devices with their start and end apart: 66, of which 32 were waited for; matrix products, arithmetic and copies ran while one was open for 40% of the time, Pallas kernels for 3%

profile of v1, /device:TPU:8, one launch (start us, length us, event | category | flops | bytes accessed | tf_op | source)
XLA Modules:
  0.0 794.3 jit_solution(2356786304449961698)
XLA Ops:
  53.7 18.6 %collective-permute-done.5 = bf16[1,2,72,768]{3,1,0,2:T(2,128)(2,1)S(1)} collective-permute-done((bf16[1,2,72,768]{3,1,0,2:T(2,128)(2,1)S(1)}, bf16[1,2,72,768]{3,1,0,2:T(2,128)(2,1)S(1)}, u32[]{:S(2)}, u32[]{:S(2)}) %collective-permute-start.5) | collective-permute-done | bytes 221216 | tf_op jit(solution)/shard_map/ppermute | solution.py:27
  75.5 18.2 %collective-permute-done.7 = bf16[1,2,72,768]{3,1,0,2:T(2,128)(2,1)S(1)} collective-permute-done((bf16[1,2,72,768]{3,1,0,2:T(2,128)(2,1)S(1)}, bf16[1,2,72,768]{3,1,0,2:T(2,128)(2,1)S(1)}, u32[]{:S(2)}, u32[]{:S(2)}) %collective-permute-start.7) | collective-permute-done | bytes 221216 | tf_op jit(solution)/shard_map/ppermute | solution.py:27
  105.6 11.3 %collective-permute-done.10 = bf16[128,2048]{1,0:T(8,128)(2,1)S(1)} collective-permute-done((bf16[128,2048]{1,0:T(8,128)(2,1)}, bf16[128,2048]{1,0:T(8,128)(2,1)S(1)}, u32[]{:S(2)}, u32[]{:S(2)}) %collective-permute-start.10) | collective-permute-done | bytes 524320 | tf_op jit(solution)/shard_map/ppermute | solution.py:114
  117.8 10.6 %collective-permute-done.15 = bf16[1,2,64,2304]{3,2,1,0:T(8,128)(2,1)S(1)} collective-permute-done((bf16[1,2,64,2304]{3,2,1,0:T(8,128)(2,1)S(1)}, bf16[1,2,64,2304]{3,2,1,0:T(8,128)(2,1)S(1)}, u32[]{:S(2)}, u32[]{:S(2)}) %collective-permute-start.15) | collective-permute-done | bytes 589856 | tf_op jit(solution)/shard_map/ppermute | solution.py:27
  134.8 33.8 %collective-permute-done.16 = bf16[1,2,64,2304]{3,2,1,0:T(8,128)(2,1)S(1)} collective-permute-done((bf16[1,2,64,2304]{3,2,1,0:T(8,128)(2,1)S(1)}, bf16[1,2,64,2304]{3,2,1,0:T(8,128)(2,1)S(1)}, u32[]{:S(2)}, u32[]{:S(2)}) %collective-permute-start.16) | collective-permute-done | bytes 589856 | tf_op jit(solution)/shard_map/ppermute | solution.py:27
  168.6 13.6 %collective-permute-done.17 = bf16[1,2,64,2304]{3,2,1,0:T(8,128)(2,1)S(1)} collective-permute-done((bf16[1,2,64,2304]{3,2,1,0:T(8,128)(2,1)S(1)}, bf16[1,2,64,2304]{3,2,1,0:T(8,128)(2,1)S(1)}, u32[]{:S(2)}, u32[]{:S(2)}) %collective-permute-start.17) | collective-permute-done | bytes 589856 | tf_op jit(solution)/shard_map/ppermute | solution.py:27
  182.2 8.1 %collective-permute-done.14 = bf16[128,2048]{1,0:T(8,128)(2,1)S(1)} collective-permute-done((bf16[128,2048]{1,0:T(8,128)(2,1)S(1)}, bf16[128,2048]{1,0:T(8,128)(2,1)S(1)}, u32[]{:S(2)}, u32[]{:S(2)}) %collective-permute-start.14) | collective-permute-done | bytes 524320 | tf_op jit(solution)/shard_map/ppermute | solution.py:114
  202.6 7.7 convolution_add_fusion.1.joint_ref
  210.4 11.7 %attend.1 = (bf16[1024,768]{1,0:T(8,128)(2,1)}, f32[1024,256]{1,0:T(8,128)}, bf16[1024,256]{1,0:T(8,128)(2,1)}, f32[1024,128]{1,0:T(8,128)}) custom-call(f32[1024,768]{1,0:T(8,128)} %convolution_add_fusion.1.joint_ref, f32[1024,128]{1,0:T(8,128)} %constant.333.clone.cos_ref, f32[1024,128]{1,0:T(8,128)} %constant.334.clone.left_ref, ...), custom_call_target="tpu_custom_call" | custom-call | flops 2147483648 | bytes 12582912 | tf_op jit(solution)/shard_map/attend/pallas_call | solution.py:292
  224.5 10.1 %collective-permute-done.18 = bf16[1024,256]{1,0:T(8,128)(2,1)} collective-permute-done((bf16[1024,256]{1,0:T(8,128)(2,1)}, bf16[1024,256]{1,0:T(8,128)(2,1)}, u32[]{:S(2)}, u32[]{:S(2)}) %collective-permute-start.18) | collective-permute-done | bytes 524320 | tf_op jit(solution)/shard_map/ppermute | solution.py:114
  238.0 8.7 %collective-permute-done.20 = bf16[1024,256]{1,0:T(8,128)(2,1)} collective-permute-done((bf16[1024,256]{1,0:T(8,128)(2,1)}, bf16[1024,256]{1,0:T(8,128)(2,1)}, u32[]{:S(2)}, u32[]{:S(2)}) %collective-permute-start.20) | collective-permute-done | bytes 524320 | tf_op jit(solution)/shard_map/ppermute | solution.py:114
  282.3 14.5 %fusion.104 = f32[1024,2048]{1,0:T(8,128)} fusion(bf16[1024,2048]{1,0:T(8,128)(2,1)} %broadcast_dynamic-update-slice_fusion, bf16[2048,2048]{1,0:T(8,128)(2,1)} %all-gather.3.cloned.1.call-done), kind=kOutput, calls=%fused_computation.323 | convolution fusion | flops 8589934592 | bytes 20971520 | tf_op jit(solution)/shard_map/dot_general | solution.py:407
  302.8 11.4 %fusion.19 = (f32[1024]{0:T(1024)S(1)}, f32[1024,2048]{1,0:T(8,128)}) fusion(bf16[1024,2048]{1,0:T(8,128)(2,1)} %constant_dynamic-update-slice_fusion.23, f32[1024,2048]{1,0:T(8,128)} %fusion.104, f32[1024,2048]{1,0:T(8,128)} %fusion.51), kind=kLoop, calls=%fused_computation.51 | loop fusion | flops 8387584 | bytes 29364224 | tf_op jit(solution)/shard_map/reduce_sum | solution.py:392
  321.4 7.0 add_convert_fusion.1
  352.2 7.7 fusion.24
  394.6 7.1 convolution_add_fusion
  428.5 10.2 %collective-permute-done.31 = bf16[8,1,64,768]{3,2,1,0:T(8,128)(2,1)S(1)} collective-permute-done((bf16[8,1,64,768]{3,2,1,0:T(8,128)(2,1)S(1)}, bf16[8,1,64,768]{3,2,1,0:T(8,128)(2,1)S(1)}, u32[]{:S(2)}, u32[]{:S(2)}) %collective-permute-start.31) | collective-permute-done | bytes 786464 | tf_op jit(solution)/shard_map/ppermute | solution.py:27
  442.0 13.5 %convolution_convert_fusion = bf16[2048,2048]{1,0:T(8,128)(2,1)} fusion(bf16[1024,2048]{1,0:T(8,128)(2,1)} %constant_dynamic-update-slice_fusion.11, bf16[1024,2048]{1,0:T(8,128)(2,1)S(1)} %copy-done.19), kind=kOutput, calls=%fused_computation.25 | convolution fusion | flops 8594128896 | bytes 16777216 | tf_op jit(solution)/shard_map/dot_general | solution.py:407
  459.1 8.0 %collective-permute-done.35 = bf16[4,1,64,768]{3,2,1,0:T(8,128)(2,1)S(1)} collective-permute-done((bf16[4,1,64,768]{3,2,1,0:T(8,128)(2,1)S(1)}, bf16[4,1,64,768]{3,2,1,0:T(8,128)(2,1)S(1)}, u32[]{:S(2)}, u32[]{:S(2)}) %collective-permute-start.35) | collective-permute-done | bytes 393248 | tf_op jit(solution)/shard_map/ppermute | solution.py:27
  475.8 6.8 collective-permute-start.37
  498.9 9.0 %collective-permute-done.39 = bf16[8,1,64,1536]{3,2,1,0:T(8,128)(2,1)S(1)} collective-permute-done((bf16[8,1,64,1536]{3,2,1,0:T(8,128)(2,1)S(1)}, bf16[8,1,64,1536]{3,2,1,0:T(8,128)(2,1)S(1)}, u32[]{:S(2)}, u32[]{:S(2)}) %collective-permute-start.39) | collective-permute-done | bytes 1572896 | tf_op jit(solution)/shard_map/ppermute | solution.py:27
  512.9 8.3 %collective-permute-start.41 = (bf16[1,2,64,768]{3,2,1,0:T(8,128)(2,1)S(1)}, bf16[1,2,64,768]{3,2,1,0:T(8,128)(2,1)S(1)}, u32[]{:S(2)}, u32[]{:S(2)}) collective-permute-start(bf16[1,2,64,768]{3,2,1,0:T(8,128)(2,1)S(1)} %constant_dynamic-slice_fusion.35), channel_id=1, source_target_pairs={{0,8},{4,12},{8,0},{12,4},{16,24},{20,28},{24,16},{28,20},{1,9},{5... | collective-permute-start | bytes 589832 | tf_op jit(solution)/shard_map/ppermute | solution.py:27
  530.5 13.5 %attend_back.1 = bf16[1024,768]{1,0:T(8,128)(2,1)} custom-call(bf16[1024,768]{1,0:T(8,128)(2,1)} %get-tuple-element.120.low_ref, bf16[1024,256]{1,0:T(8,128)(2,1)} %subtract_convert_fusion.2.grad_ref, f32[1024,256]{1,0:T(8,128)} %get-tuple-element.123.context_ref, f32[1024,128]{1,0:T(8,128)} %get-tuple-element.124.lse_ref, ...), custom_call_target="tpu_custom_call" | custom-call | flops 5368709120 | bytes 12582912 | tf_op jit(solution)/shard_map/attend_back/pallas_call | solution.py:373
  548.3 11.4 %fusion.7 = (bf16[2048]{0:T(1024)(128)(2,1)S(1)}, f32[1024]{0:T(1024)S(1)}, f32[1024]{0:T(1024)}, bf16[2048]{0:T(1024)(128)(2,1)S(1)}, bf16[1024,2048]{1,0:T(8,128)(2,1)}) fusion(bf16[1024,2048]{1,0:T(8,128)(2,1)} %constant_dynamic-update-slice_fusion.23, f32[1024]{0:T(1024)S(1)} %copy-done.53, f32[1024]{0:T(1024)S(1)} %copy-done.45, ...), kind=kOutput, calls=%fused_computation.11 | convolution fusion | flops 3252676608 | bytes 21544960 | tf_op jit(solution)/shard_map/dot_general | solution.py:407
  561.3 6.8 constant_dynamic-slice_fusion.17
  603.7 7.9 collective-permute-done.47
  636.5 9.5 %collective-permute-start.54 = (bf16[1,2,72,768]{3,2,1,0:T(8,128)(2,1)S(1)}, bf16[1,2,72,768]{3,2,1,0:T(8,128)(2,1)S(1)}, u32[]{:S(2)}, u32[]{:S(2)}) collective-permute-start(bf16[1,2,72,768]{3,2,1,0:T(8,128)(2,1)S(1)} %constant_dynamic-slice_fusion.10), channel_id=1, source_target_pairs={{0,8},{4,12},{8,0},{12,4},{16,24},{20,28},{24,16},{28,20},{1,9},{5... | collective-permute-start | bytes 663560 | tf_op jit(solution)/shard_map/ppermute | solution.py:27
  660.6 17.7 %collective-permute-done.55 = bf16[1,2,72,768]{3,2,1,0:T(8,128)(2,1)S(1)} collective-permute-done((bf16[1,2,72,768]{3,2,1,0:T(8,128)(2,1)S(1)}, bf16[1,2,72,768]{3,2,1,0:T(8,128)(2,1)S(1)}, u32[]{:S(2)}, u32[]{:S(2)}) %collective-permute-start.55) | collective-permute-done | bytes 221216 | tf_op jit(solution)/shard_map/ppermute | solution.py:27
  705.0 7.2 collective-permute-done.58
  717.6 23.6 %collective-permute-done.60 = bf16[1,2,64,1536]{3,2,1,0:T(8,128)(2,1)S(1)} collective-permute-done((bf16[1,2,64,1536]{3,2,1,0:T(8,128)(2,1)S(1)}, bf16[1,2,64,1536]{3,2,1,0:T(8,128)(2,1)S(1)}, u32[]{:S(2)}, u32[]{:S(2)}) %collective-permute-start.60) | collective-permute-done | bytes 393248 | tf_op jit(solution)/shard_map/ppermute | solution.py:27
  741.2 11.4 %collective-permute-done.61 = bf16[1,2,64,1536]{3,2,1,0:T(8,128)(2,1)S(1)} collective-permute-done((bf16[1,2,64,1536]{3,2,1,0:T(8,128)(2,1)S(1)}, bf16[1,2,64,1536]{3,2,1,0:T(8,128)(2,1)S(1)}, u32[]{:S(2)}, u32[]{:S(2)}) %collective-permute-start.61) | collective-permute-done | bytes 393248 | tf_op jit(solution)/shard_map/ppermute | solution.py:27
  761.2 24.3 %reduce-scatter.5.cloned.1.call-done = bf16[1,64,2048]{2,1,0:T(8,128)(2,1)} async-done(((bf16[8,64,2048]{2,1,0:T(8,128)(2,1)}), bf16[1,64,2048]{2,1,0:T(8,128)(2,1)}) %reduce-scatter.5.cloned.1.call-update) | async-done | bytes 262160 | tf_op jit(solution)/shard_map/reduce_scatter | solution.py:657
  (500 shorter events, 388.6 us)
Async XLA Ops:
  7.2 275.1 %all-gather.3.cloned.1.call-start = ((), (), s32[]{:S(2)}) async-start(), calls=%async_computation.2 | async-start | bytes 8650752 | tf_op jit(solution)/shard_map/all_gather | solution.py:492
  7.9 335.5 %all-gather.5.cloned.1.call-start = ((), (), s32[]{:S(2)}) async-start(), calls=%async_computation.3 | async-start | bytes 4718592 | tf_op jit(solution)/shard_map/all_gather | solution.py:501
  34.2 60.9 %collective-permute-start.8 = (bf16[4,1,64,2304]{3,2,1,0:T(8,128)(2,1)}, bf16[4,1,64,2304]{3,2,1,0:T(8,128)(2,1)}, u32[]{:S(2)}, u32[]{:S(2)}) collective-permute-start(bf16[4,1,64,2304]{3,2,1,0:T(8,128)(2,1)} %constant_dynamic-slice_fusion.44), channel_id=1, source_target_pairs={{0,4},{4,0},{8,12},{12,8},{16,20},{20,16},{24,28},{28,24},{1,5},{5... | collective-permute-start | bytes 3538952 | tf_op jit(solution)/shard_map/ppermute | solution.py:27
  35.6 60.9 %collective-permute-start.3 = (bf16[128,2048]{1,0:T(8,128)(2,1)}, bf16[128,2048]{1,0:T(8,128)(2,1)}, u32[]{:S(2)}, u32[]{:S(2)}) collective-permute-start(bf16[128,2048]{1,0:T(8,128)(2,1)} %collective-permute-done), channel_id=1, source_target_pairs={{0,8},{8,16},{16,24},{24,28},{28,20},{20,12},{12,4},{4,0},{1,9},{9... | collective-permute-start | bytes 1572872 | tf_op jit(solution)/shard_map/ppermute | solution.py:114
  37.3 59.3 %collective-permute-start.4 = (bf16[128,2048]{1,0:T(8,128)(2,1)}, bf16[128,2048]{1,0:T(8,128)(2,1)}, u32[]{:S(2)}, u32[]{:S(2)}) collective-permute-start(bf16[128,2048]{1,0:T(8,128)(2,1)} %collective-permute-done.1), channel_id=1, source_target_pairs={{0,4},{8,0},{16,8},{24,16},{28,24},{20,28},{12,20},{4,12},{1,5},{9... | collective-permute-start | bytes 1572872 | tf_op jit(solution)/shard_map/ppermute | solution.py:114
  45.8 26.5 %collective-permute-start.5 = (bf16[1,2,72,768]{3,1,0,2:T(2,128)(2,1)S(1)}, bf16[1,2,72,768]{3,1,0,2:T(2,128)(2,1)S(1)}, u32[]{:S(2)}, u32[]{:S(2)}) collective-permute-start(bf16[1,2,72,768]{3,1,0,2:T(2,128)(2,1)S(1)} %get-tuple-element.197), channel_id=1, source_target_pairs={{0,8},{4,12},{8,0},{12,4},{16,24},{20,28},{24,16},{28,20},{1,9},{5... | collective-permute-start | bytes 663560 | tf_op jit(solution)/shard_map/ppermute | solution.py:27
  47.9 27.4 %collective-permute-start.6 = (bf16[1,2,72,768]{3,1,0,2:T(2,128)(2,1)S(1)}, bf16[1,2,72,768]{3,1,0,2:T(2,128)(2,1)S(1)}, u32[]{:S(2)}, u32[]{:S(2)}) collective-permute-start(bf16[1,2,72,768]{3,1,0,2:T(2,128)(2,1)S(1)} %get-tuple-element.196), channel_id=1, source_target_pairs={{0,16},{4,20},{8,24},{12,28},{16,0},{20,4},{24,8},{28,12},{1,17},{... | collective-permute-start | bytes 663560 | tf_op jit(solution)/shard_map/ppermute | solution.py:27
  96.7 31.7 %collective-permute-start.15 = (bf16[1,2,64,2304]{3,2,1,0:T(8,128)(2,1)S(1)}, bf16[1,2,64,2304]{3,2,1,0:T(8,128)(2,1)S(1)}, u32[]{:S(2)}, u32[]{:S(2)}) collective-permute-start(bf16[1,2,64,2304]{3,2,1,0:T(8,128)(2,1)S(1)} %constant_dynamic-slice_fusion.43), channel_id=1, source_target_pairs={{0,8},{4,12},{8,0},{12,4},{16,24},{20,28},{24,16},{28,20},{1,9},{5... | collective-permute-start | bytes 1769480 | tf_op jit(solution)/shard_map/ppermute | solution.py:27
  98.9 34.5 %collective-permute-start.11 = (bf16[8,72,768]{2,0,1:T(8,128)(2,1)S(1)}, bf16[8,72,768]{2,0,1:T(8,128)(2,1)S(1)}, u32[]{:S(2)}, u32[]{:S(2)}) collective-permute-start(bf16[8,72,768]{2,0,1:T(8,128)(2,1)S(1)} %copy-done.21), channel_id=1, source_target_pairs={{0,2},{1,3},{2,0},{3,1},{4,6},{5,7},{6,4},{7,5},{8,10},{9,11},{10,... | collective-permute-start | bytes 2654216 | tf_op jit(solution)/shard_map/ppermute | solution.py:27
  102.6 32.1 %collective-permute-start.12 = (bf16[8,72,768]{2,0,1:T(8,128)(2,1)S(1)}, bf16[8,72,768]{2,0,1:T(8,128)(2,1)S(1)}, u32[]{:S(2)}, u32[]{:S(2)}) collective-permute-start(bf16[8,72,768]{2,0,1:T(8,128)(2,1)S(1)} %copy-done.21), channel_id=1, source_target_pairs={{0,1},{1,0},{2,3},{3,2},{4,5},{5,4},{6,7},{7,6},{8,9},{9,8},{10,11... | collective-permute-start | bytes 2654216 | tf_op jit(solution)/shard_map/ppermute | solution.py:27
  102.6 28.7 %collective-permute-start.9 = (bf16[128,2048]{1,0:T(8,128)(2,1)}, bf16[128,2048]{1,0:T(8,128)(2,1)S(1)}, u32[]{:S(2)}, u32[]{:S(2)}) collective-permute-start(bf16[128,2048]{1,0:T(8,128)(2,1)} %collective-permute-done.3), channel_id=1, source_target_pairs={{0,8},{8,16},{16,24},{24,28},{28,20},{20,12},{12,4},{4,0},{1,9},{9... | collective-permute-start | bytes 1572872 | tf_op jit(solution)/shard_map/ppermute | solution.py:114
  128.5 40.1 %collective-permute-start.16 = (bf16[1,2,64,2304]{3,2,1,0:T(8,128)(2,1)S(1)}, bf16[1,2,64,2304]{3,2,1,0:T(8,128)(2,1)S(1)}, u32[]{:S(2)}, u32[]{:S(2)}) collective-permute-start(bf16[1,2,64,2304]{3,2,1,0:T(8,128)(2,1)S(1)} %get-tuple-element.177), channel_id=1, source_target_pairs={{0,16},{4,20},{8,24},{12,28},{16,0},{20,4},{24,8},{28,12},{1,17},{... | collective-permute-start | bytes 1769480 | tf_op jit(solution)/shard_map/ppermute | solution.py:27
  132.1 50.0 %collective-permute-start.17 = (bf16[1,2,64,2304]{3,2,1,0:T(8,128)(2,1)S(1)}, bf16[1,2,64,2304]{3,2,1,0:T(8,128)(2,1)S(1)}, u32[]{:S(2)}, u32[]{:S(2)}) collective-permute-start(bf16[1,2,64,2304]{3,2,1,0:T(8,128)(2,1)S(1)} %get-tuple-element.176), channel_id=1, source_target_pairs={{0,24},{4,28},{8,16},{12,20},{16,8},{20,12},{24,0},{28,4},{1,25},{... | collective-permute-start | bytes 1769480 | tf_op jit(solution)/shard_map/ppermute | solution.py:27
  133.4 57.9 %collective-permute-start.13 = (bf16[8,72,768]{2,0,1:T(8,128)(2,1)S(1)}, bf16[8,72,768]{2,0,1:T(8,128)(2,1)S(1)}, u32[]{:S(2)}, u32[]{:S(2)}) collective-permute-start(bf16[8,72,768]{2,0,1:T(8,128)(2,1)S(1)} %collective-permute-done.11), channel_id=1, source_target_pairs={{0,1},{1,0},{2,3},{3,2},{4,5},{5,4},{6,7},{7,6},{8,9},{9,8},{10,11... | collective-permute-start | bytes 2654216 | tf_op jit(solution)/shard_map/ppermute | solution.py:27
  133.4 57.0 %collective-permute-start.14 = (bf16[128,2048]{1,0:T(8,128)(2,1)S(1)}, bf16[128,2048]{1,0:T(8,128)(2,1)S(1)}, u32[]{:S(2)}, u32[]{:S(2)}) collective-permute-start(bf16[128,2048]{1,0:T(8,128)(2,1)S(1)} %collective-permute-done.9), channel_id=1, source_target_pairs={{0,8},{8,16},{16,24},{24,28},{28,20},{20,12},{12,4},{4,0},{1,9},{9... | collective-permute-start | bytes 1572872 | tf_op jit(solution)/shard_map/ppermute | solution.py:114
  194.3 64.0 %collective-permute-start.24 = (bf16[8,64,2304]{2,1,0:T(8,128)(2,1)S(1)}, bf16[8,64,2304]{2,1,0:T(8,128)(2,1)}, u32[]{:S(2)}, u32[]{:S(2)}) collective-permute-start(bf16[8,64,2304]{2,1,0:T(8,128)(2,1)S(1)} %bitcast.244), channel_id=1, source_target_pairs={{0,2},{1,3},{2,0},{3,1},{4,6},{5,7},{6,4},{7,5},{8,10},{9,11},{10,... | collective-permute-start | bytes 7077896 | tf_op jit(solution)/shard_map/ppermute | solution.py:27
  237.3 40.1 %collective-permute-start.26 = (bf16[8,64,2304]{2,1,0:T(8,128)(2,1)S(1)}, bf16[8,64,2304]{2,1,0:T(8,128)(2,1)}, u32[]{:S(2)}, u32[]{:S(2)}) collective-permute-start(bf16[8,64,2304]{2,1,0:T(8,128)(2,1)S(1)} %bitcast.245), channel_id=1, source_target_pairs={{0,1},{1,0},{2,3},{3,2},{4,5},{5,4},{6,7},{7,6},{8,9},{9,8},{10,11... | collective-permute-start | bytes 7077896 | tf_op jit(solution)/shard_map/ppermute | solution.py:27
  251.0 244.3 %reduce-scatter.3.cloned.1.call-start = ((), (), s32[]{:S(2)}) async-start(), calls=%async_computation.4 | async-start | bytes 4718592 | tf_op jit(solution)/shard_map/reduce_scatter | solution.py:542
  268.8 28.0 %collective-permute-start.25 = (bf16[1024,256]{1,0:T(8,128)(2,1)}, bf16[1024,256]{1,0:T(8,128)(2,1)S(1)}, u32[]{:S(2)}, u32[]{:S(2)}) collective-permute-start(bf16[1024,256]{1,0:T(8,128)(2,1)} %collective-permute-done.23), channel_id=1, source_target_pairs={{0,8},{8,16},{16,24},{24,28},{28,20},{20,12},{12,4},{4,0},{1,9},{9... | collective-permute-start | bytes 1572872 | tf_op jit(solution)/shard_map/ppermute | solution.py:114
  363.7 421.8 %reduce-scatter.5.cloned.1.call-start = ((), (), s32[]{:S(2)}) async-start(), calls=%async_computation.5 | async-start | bytes 2359296 | tf_op jit(solution)/shard_map/reduce_scatter | solution.py:657
  373.8 27.9 %collective-permute-start.28 = (bf16[8,2,64,768]{3,2,1,0:T(8,128)(2,1)}, bf16[8,2,64,768]{3,2,1,0:T(8,128)(2,1)}, u32[]{:S(2)}, u32[]{:S(2)}) collective-permute-start(bf16[8,2,64,768]{3,2,1,0:T(8,128)(2,1)} %dynamic-slice_bitcast_fusion.1), channel_id=1, source_target_pairs={{0,1},{1,0},{2,3},{3,2},{4,5},{5,4},{6,7},{7,6},{8,9},{9,8},{10,11... | collective-permute-start | bytes 4718600 | tf_op jit(solution)/shard_map/ppermute | solution.py:27
  439.3 27.8 %collective-permute-start.34 = (bf16[8,2,64,1536]{3,2,1,0:T(8,128)(2,1)S(1)}, bf16[8,2,64,1536]{3,2,1,0:T(8,128)(2,1)S(1)}, u32[]{:S(2)}, u32[]{:S(2)}) collective-permute-start(bf16[8,2,64,1536]{3,2,1,0:T(8,128)(2,1)S(1)} %dynamic-slice_bitcast_fusion), channel_id=1, source_target_pairs={{0,1},{1,0},{2,3},{3,2},{4,5},{5,4},{6,7},{7,6},{8,9},{9,8},{10,11... | collective-permute-start | bytes 9437192 | tf_op jit(solution)/shard_map/ppermute | solution.py:27
  472.4 35.5 %collective-permute-start.39 = (bf16[8,1,64,1536]{3,2,1,0:T(8,128)(2,1)S(1)}, bf16[8,1,64,1536]{3,2,1,0:T(8,128)(2,1)S(1)}, u32[]{:S(2)}, u32[]{:S(2)}) collective-permute-start(bf16[8,1,64,1536]{3,2,1,0:T(8,128)(2,1)S(1)} %dynamic-slice_convert_fusion.1), channel_id=1, source_target_pairs={{0,2},{1,3},{2,0},{3,1},{4,6},{5,7},{6,4},{7,5},{8,10},{9,11},{10,... | collective-permute-start | bytes 4718600 | tf_op jit(solution)/shard_map/ppermute | solution.py:27
  511.9 34.6 %collective-permute-start.40 = (bf16[4,1,64,1536]{3,2,1,0:T(8,128)(2,1)S(1)}, bf16[4,1,64,1536]{3,2,1,0:T(8,128)(2,1)S(1)}, u32[]{:S(2)}, u32[]{:S(2)}) collective-permute-start(bf16[4,1,64,1536]{3,2,1,0:T(8,128)(2,1)S(1)} %constant_dynamic-slice_fusion.36), channel_id=1, source_target_pairs={{0,4},{4,0},{8,12},{12,8},{16,20},{20,16},{24,28},{28,24},{1,5},{5... | collective-permute-start | bytes 2359304 | tf_op jit(solution)/shard_map/ppermute | solution.py:27
  570.4 42.5 %collective-permute-start.48 = (bf16[8,2,64,2048]{3,2,0,1:T(8,128)(2,1)}, bf16[8,2,64,2048]{3,2,0,1:T(8,128)(2,1)}, u32[]{:S(2)}, u32[]{:S(2)}) collective-permute-start(bf16[8,2,64,2048]{3,2,0,1:T(8,128)(2,1)} %bitcast.230), channel_id=1, source_target_pairs={{0,1},{1,0},{2,3},{3,2},{4,5},{5,4},{6,7},{7,6},{8,9},{9,8},{10,11... | collective-permute-start | bytes 12582920 | tf_op jit(solution)/shard_map/ppermute | solution.py:27
  626.5 54.2 %collective-permute-start.57 = (bf16[8,1,64,2048]{3,2,0,1:T(8,128)(2,1)}, bf16[8,1,64,2048]{3,2,0,1:T(8,128)(2,1)}, u32[]{:S(2)}, u32[]{:S(2)}) collective-permute-start(bf16[8,1,64,2048]{3,2,0,1:T(8,128)(2,1)} %dynamic-slice_convert_fusion), channel_id=1, source_target_pairs={{0,2},{1,3},{2,0},{3,1},{4,6},{5,7},{6,4},{7,5},{8,10},{9,11},{10,... | collective-permute-start | bytes 6291464 | tf_op jit(solution)/shard_map/ppermute | solution.py:27
  648.2 37.4 %collective-permute-start.52 = (bf16[136,2048]{1,0:T(8,128)(2,1)}, bf16[136,2048]{1,0:T(8,128)(2,1)}, u32[]{:S(2)}, u32[]{:S(2)}) collective-permute-start(bf16[136,2048]{1,0:T(8,128)(2,1)} %add_convert_fusion.9), channel_id=1, source_target_pairs={{0,8},{8,16},{16,24},{24,28},{28,20},{20,12},{12,4},{4,0},{1,9},{9... | collective-permute-start | bytes 1671176 | tf_op jit(solution)/shard_map/ppermute | solution.py:114
  651.4 26.9 %collective-permute-start.55 = (bf16[1,2,72,768]{3,2,1,0:T(8,128)(2,1)S(1)}, bf16[1,2,72,768]{3,2,1,0:T(8,128)(2,1)S(1)}, u32[]{:S(2)}, u32[]{:S(2)}) collective-permute-start(bf16[1,2,72,768]{3,2,1,0:T(8,128)(2,1)S(1)} %get-tuple-element.193), channel_id=1, source_target_pairs={{0,16},{4,20},{8,24},{12,28},{16,0},{20,4},{24,8},{28,12},{1,17},{... | collective-permute-start | bytes 663560 | tf_op jit(solution)/shard_map/ppermute | solution.py:27
  657.1 23.6 %collective-permute-start.56 = (bf16[1,2,72,768]{3,2,1,0:T(8,128)(2,1)S(1)}, bf16[1,2,72,768]{3,2,1,0:T(8,128)(2,1)S(1)}, u32[]{:S(2)}, u32[]{:S(2)}) collective-permute-start(bf16[1,2,72,768]{3,2,1,0:T(8,128)(2,1)S(1)} %get-tuple-element.192), channel_id=1, source_target_pairs={{0,24},{4,28},{8,16},{12,20},{16,8},{20,12},{24,0},{28,4},{1,25},{... | collective-permute-start | bytes 663560 | tf_op jit(solution)/shard_map/ppermute | solution.py:27
  659.1 26.5 %collective-permute-start.53 = (bf16[136,2048]{1,0:T(8,128)(2,1)}, bf16[136,2048]{1,0:T(8,128)(2,1)}, u32[]{:S(2)}, u32[]{:S(2)}) collective-permute-start(bf16[136,2048]{1,0:T(8,128)(2,1)} %add_convert_fusion.8), channel_id=1, source_target_pairs={{0,4},{8,0},{16,8},{24,16},{28,24},{20,28},{12,20},{4,12},{1,5},{9... | collective-permute-start | bytes 1671176 | tf_op jit(solution)/shard_map/ppermute | solution.py:114
  702.8 38.4 %collective-permute-start.60 = (bf16[1,2,64,1536]{3,2,1,0:T(8,128)(2,1)S(1)}, bf16[1,2,64,1536]{3,2,1,0:T(8,128)(2,1)S(1)}, u32[]{:S(2)}, u32[]{:S(2)}) collective-permute-start(bf16[1,2,64,1536]{3,2,1,0:T(8,128)(2,1)S(1)} %get-tuple-element.182), channel_id=1, source_target_pairs={{0,16},{4,20},{8,24},{12,28},{16,0},{20,4},{24,8},{28,12},{1,17},{... | collective-permute-start | bytes 1179656 | tf_op jit(solution)/shard_map/ppermute | solution.py:27
  704.4 48.3 %collective-permute-start.61 = (bf16[1,2,64,1536]{3,2,1,0:T(8,128)(2,1)S(1)}, bf16[1,2,64,1536]{3,2,1,0:T(8,128)(2,1)S(1)}, u32[]{:S(2)}, u32[]{:S(2)}) collective-permute-start(bf16[1,2,64,1536]{3,2,1,0:T(8,128)(2,1)S(1)} %get-tuple-element.181), channel_id=1, source_target_pairs={{0,24},{4,28},{8,16},{12,20},{16,8},{20,12},{24,0},{28,4},{1,25},{... | collective-permute-start | bytes 1179656 | tf_op jit(solution)/shard_map/ppermute | solution.py:27
  (109 other events, 1172.8 us)
Sparse Core Ops, SparseCore 0:
  10.9 113.3 all-gather.2
  251.2 80.1 all-gather.4
  363.8 89.7 reduce-scatter.2
  701.2 84.2 reduce-scatter.4

commit v2 on v1

--- a/solution.py
+++ b/solution.py
@@ -39,26 +39,43 @@
     return tie(value, *others)[0]
 
 
-def exchange_near(blocks, number):
+def exchange_begin(blocks, number, bit):
+    mine = (lax.axis_index("seq") // bit) % 2
+    pairs = blocks.reshape((number // (2 * bit), 2, bit) + blocks.shape[1:])
+    return pairs, swap(lax.dynamic_slice_in_dim(pairs, 1 - mine, 1, 1), "seq", number, bit)
+
+
+def exchange_end(state, number, bit):
+    pairs, got = state
+    mine = (lax.axis_index("seq") // bit) % 2
+    out = lax.dynamic_update_slice_in_dim(pairs, got, 1 - mine, 1)
+    return out.reshape((number,) + pairs.shape[3:])
+
+
+def exchange(blocks, number, bit):
+    return exchange_end(exchange_begin(blocks, number, bit), number, bit)
+
+
+def exchange_far(blocks, number):
     if number != 8:
+        for bit in bits_of(number)[1:]:
+            blocks = exchange(blocks, number, bit)
         return blocks
-    mine = lax.axis_index("seq") % 2
-    pairs = blocks.reshape((number // 2, 2) + blocks.shape[1:])
-    got = swap(lax.dynamic_slice_in_dim(pairs, 1 - mine, 1, 1), "seq", number, 1)
-    return lax.dynamic_update_slice_in_dim(pairs, got, 1 - mine, 1).reshape(blocks.shape)
-
-
-def exchange_far(blocks, number):
-    low = 2 if number == 8 else 1
-    place = lax.axis_index("seq") // low
-    out = blocks.reshape((number // low, low) + blocks.shape[1:])
+    place = lax.axis_index("seq") // 2
+    out = blocks.reshape((4, 2) + blocks.shape[1:])
     parts = [
-        swap(lax.dynamic_slice_in_dim(out, place ^ k, 1, 0), "seq", number, k * low)
-        for k in range(1, number // low)
+        swap(lax.dynamic_slice_in_dim(out, place ^ k, 1, 0), "seq", number, k * 2)
+        for k in range(1, 4)
     ]
     for k, part in enumerate(parts):
         out = lax.dynamic_update_slice_in_dim(out, part, place ^ (k + 1), 0)
     return out.reshape(blocks.shape)
+
+
+def rest_of_exchange(blocks, number):
+    for bit in bits_of(number)[3:]:
+        blocks = exchange(blocks, number, bit)
+    return blocks
 
 
 def gather_far(value, number):
@@ -69,13 +86,8 @@
 
 
 def gather_near(held, number):
-    me = lax.axis_index("batch")
-    held = held + [(k ^ 1, swap(v, "batch", number, 1)) for k, v in held]
-    own = held[0][1]
-    out = jnp.broadcast_to(own[:, None], own.shape[:1] + (number,) + own.shape[1:])
-    for k, v in held[1:]:
-        out = lax.dynamic_update_slice_in_dim(out, v[:, None], me ^ k, 1)
-    return out
+    held = dict(held + [(k ^ 1, swap(v, "batch", number, 1)) for k, v in held])
+    return [held[k] for k in range(number)]
 
 
 def scatter_stage(value, number, bit):
@@ -84,7 +96,7 @@
     mine = (lax.axis_index("batch") // bit) % 2
     keep = lax.dynamic_index_in_dim(pairs, mine, 2, False)
     send = lax.dynamic_index_in_dim(pairs, 1 - mine, 2, False).astype(bf16)
-    return keep.astype(f32) + swap(send, "batch", number, bit).astype(f32)
+    return (keep.astype(f32) + swap(send, "batch", number, bit).astype(f32)).astype(bf16)
 
 
 def scatter_near(value, number):
@@ -94,7 +106,7 @@
 def scatter_far(value, number):
     for bit in bits_of(number)[1:]:
         value = scatter_stage(value, number, bit)
-    return value[:, 0].astype(bf16)
+    return value[:, 0]
 
 
 RING = (0, 2, 4, 6, 7, 5, 3, 1)
@@ -108,6 +120,15 @@
 def ring_index(place):
     place = (place + 16) % 8
     return jnp.where(place < 4, 2 * place, 15 - 2 * place)
+
+
+ARRIVAL = (0, 1, -1, 2, -2, 3, -3, -4)
+
+
+def arrival(number):
+    if number != 8:
+        return list(range(number))
+    return [ring_index(ring_place() + step) for step in ARRIVAL]
 
 
 def ring_step(value, way):
@@ -236,22 +257,11 @@
     return math.gcd(length, 256)
 
 
-def attend_kernel(joint_ref, cos_ref, left_ref, right_ref, low_ref, context_ref, mixed_ref, lse_ref):
-    length, total = joint_ref.shape
+def attend_kernel(low_ref, context_ref, mixed_ref, lse_ref):
+    length, total = low_ref.shape
     columns = total // 3
     heads = columns // HEAD_DIM
     block = block_of(length)
-    scale = 1.0 / math.sqrt(HEAD_DIM)
-    for i in range(length // block):
-        rows = pl.ds(i * block, block)
-        tables = [wide(t[rows, :], columns) for t in (cos_ref, left_ref, right_ref)]
-        low_ref[rows, 0:columns] = (
-            turn(joint_ref[rows, 0:columns], *tables).astype(bf16) * scale
-        ).astype(bf16)
-        low_ref[rows, columns : 2 * columns] = turn(
-            joint_ref[rows, columns : 2 * columns], *tables
-        ).astype(bf16)
-        low_ref[rows, 2 * columns :] = joint_ref[rows, 2 * columns :].astype(bf16)
     for i in range(length // block):
         rows = pl.ds(i * block, block)
         reach = (i + 1) * block
@@ -286,13 +296,12 @@
         lse_ref[rows, :] = lse_all
 
 
-def attend(joint, tables):
-    length, total = joint.shape
+def attend(low):
+    length, total = low.shape
     columns = total // 3
     return pl.pallas_call(
         attend_kernel,
         out_shape=(
-            jax.ShapeDtypeStruct((length, total), bf16),
             jax.ShapeDtypeStruct((length, columns), f32),
             jax.ShapeDtypeStruct((length, columns), bf16),
             jax.ShapeDtypeStruct((length, 128), f32),
@@ -304,7 +313,7 @@
             transcendentals=length * length * columns // HEAD_DIM,
         ),
         name="attend",
-    )(joint, *tables)
+    )(low)
 
 
 def attend_back_kernel(
@@ -407,6 +416,403 @@
     return lax.dot_general(left, right, (contract, ((), ())), preferred_element_type=f32)
 
 
+def block_spec(block, columns):
+    return pl.BlockSpec((block, columns), lambda i: (i, 0))
+
+
+def whole_spec(rows, columns):
+    return pl.BlockSpec((rows, columns), lambda i: (0, 0))
+
+
+def once_spec(rows, columns):
+    return pl.BlockSpec((rows, columns), lambda i: (0, 0), pipeline_mode=pl.Buffered(1))
+
+
+def any_specs(number):
+    return [pl.BlockSpec(memory_space=pl.ANY)] * number
+
+
+def run_copies(copies, sems):
+    copies = [pltpu.make_async_copy(*pair, sems.at[i]) for i, pair in enumerate(copies)]
+    for copy in copies:
+        copy.start()
+    for copy in copies:
+        copy.wait()
+
+
+def weight_copies(piece_refs, weight_ref):
+    me = lax.axis_index("batch")
+    rows = weight_ref.shape[2]
+    return [
+        (ref.at[:, pl.ds(0, rows), :], weight_ref.at[:, me ^ k])
+        for k, ref in enumerate(piece_refs)
+    ]
+
+
+def load_pieces(piece_refs, weight_ref, sems):
+    @pl.when(pl.program_id(0) == 0)
+    def _():
+        run_copies(weight_copies(piece_refs, weight_ref), sems)
+
+
+def weight_of(weight_ref, start, size):
+    part = weight_ref[:, :, :, start : start + size]
+    return part.reshape(-1, size)
+
+
+def call_kernel(kernel, length, in_specs, out, scratch, args, name, flops):
+    block = block_of(length)
+    return pl.pallas_call(
+        kernel,
+        grid=(length // block,),
+        in_specs=in_specs,
+        out_specs=[spec for _, spec in out],
+        out_shape=[shape for shape, _ in out],
+        scratch_shapes=scratch,
+        compiler_params=pltpu.CompilerParams(
+            vmem_limit_bytes=VMEM_BYTES, dimension_semantics=("arbitrary",)
+        ),
+        cost_estimate=pl.CostEstimate(
+            flops=flops, bytes_accessed=flops // 500, transcendentals=0
+        ),
+        name=name,
+    )(*args)
+
+
+def rows_out(length, columns, kind):
+    return (jax.ShapeDtypeStruct((length, columns), kind), block_spec(block_of(length), columns))
+
+
+def sums_out(columns):
+    return (jax.ShapeDtypeStruct((8, columns), f32), whole_spec(8, columns))
+
+
+def add_sums(ref, *rows):
+    @pl.when(pl.program_id(0) == 0)
+    def _():
+        ref[...] = jnp.zeros_like(ref)
+
+    for i, row in enumerate(rows):
+        ref[i : i + 1, :] += jnp.sum(row, axis=0, keepdims=True)
+
+
+def heads_kernel(n, n_seq, *refs):
+    gain_ref, shift_ref, bias_ref, cos_ref, left_ref, right_ref = refs[:6]
+    pieces = refs[6 : 6 + n]
+    center_pieces = refs[6 + n : 6 + n + n_seq]
+    low_ref, input_ref, center_ref, weight_ref, all_ref, sems = refs[6 + n + n_seq :]
+    local = all_ref.shape[1]
+
+    @pl.when(pl.program_id(0) == 0)
+    def _():
+        copies = [
+            (ref.at[pl.ds(0, local), :], all_ref.at[at])
+            for at, ref in zip(arrival(n_seq), center_pieces)
+        ]
+        run_copies(copies + weight_copies(pieces, weight_ref), sems)
+
+    total = low_ref.shape[1]
+    columns = total // 3
+    block, width = center_ref.shape
+    many = block // local
+    center = all_ref[pl.ds(pl.program_id(0) * many, many)].reshape(block, width)
+    center_ref[...] = center
+    unit, _ = unit_of(center.astype(f32))
+    first_input = (unit * gain_ref[...] + shift_ref[...]).astype(bf16)
+    input_ref[...] = first_input
+    joint = dot(first_input, weight_of(weight_ref, 0, total), ((1,), (0,))) + bias_ref[...]
+    tables = [wide(t[...], columns) for t in (cos_ref, left_ref, right_ref)]
+    scale = 1.0 / math.sqrt(HEAD_DIM)
+    query = turn(joint[:, :columns], *tables).astype(bf16)
+    low_ref[:, :columns] = (query.astype(f32) * scale).astype(bf16)
+    low_ref[:, columns : 2 * columns] = turn(joint[:, columns : 2 * columns], *tables).astype(bf16)
+    low_ref[:, 2 * columns :] = joint[:, 2 * columns :].astype(bf16)
+
+
+def make_heads(center_pieces, gain, shift, bias, tables, pieces, rows, local):
+    n_seq, n = len(center_pieces), len(pieces)
+    length, width = local * n_seq, gain.shape[1]
+    total = bias.shape[1]
+    block = block_of(length)
+    return call_kernel(
+        lambda *refs: heads_kernel(n, n_seq, *refs),
+        length,
+        [whole_spec(1, width), whole_spec(1, width), whole_spec(1, total)]
+        + [block_spec(block, 128)] * 3
+        + any_specs(n + n_seq),
+        [
+            rows_out(length, total, bf16),
+            rows_out(length, width, bf16),
+            rows_out(length, width, bf16),
+        ],
+        [
+            pltpu.VMEM((n_seq, n, rows, total), bf16),
+            pltpu.VMEM((n_seq, local, width), bf16),
+            pltpu.SemaphoreType.DMA((n + n_seq,)),
+        ],
+        (gain, shift, bias, *tables, *pieces, *center_pieces),
+        "make_heads",
+        2 * length * width * total,
+    )
+
+
+def middle_kernel(n, n_seq, many, *refs):
+    center_ref, gain_ref, shift_ref = refs[:3]
+    pieces, mixed_pieces = refs[3 : 3 + n], refs[3 + n : 3 + n + many]
+    input_ref, unit_ref, inverse_ref, mixed_ref, out_ref = refs[3 + n + many : 8 + n + many]
+    weight_ref, all_ref, sems, out_sem = refs[8 + n + many :]
+    rows, width = weight_ref.shape[2:]
+    columns = width // n_seq
+    step = pl.program_id(0)
+    give = pltpu.make_async_copy(weight_ref, out_ref, out_sem)
+
+    @pl.when(step == 0)
+    def _():
+        me = lax.axis_index("batch")
+        places = arrival(n_seq)
+        copies = [
+            (ref.at[pl.ds(j * rows, rows), :], weight_ref.at[at, me ^ k])
+            for k, ref in enumerate(pieces)
+            for j, at in enumerate(places)
+        ]
+        if many == 1:
+            copies.append((mixed_pieces[0], all_ref))
+        else:
+            for at, ref in zip(places, mixed_pieces):
+                span = pl.ds(pl.multiple_of(at * columns, columns), columns)
+                copies.append((ref, all_ref.at[:, span]))
+        run_copies(copies, sems)
+        give.start()
+
+    block = center_ref.shape[0]
+    mixed = all_ref[pl.ds(pl.multiple_of(step * block, block), block), :]
+    mixed_ref[...] = mixed
+    projected = dot(mixed, weight_ref[...].reshape(width, width), ((1,), (0,)))
+    unit, inverse = unit_of(center_ref[...].astype(f32) + projected)
+    input_ref[...] = (unit * gain_ref[...] + shift_ref[...]).astype(bf16)
+    unit_ref[...] = unit.astype(bf16)
+    inverse_ref[...] = jnp.broadcast_to(inverse, inverse_ref.shape)
+
+    @pl.when(step == pl.num_programs(0) - 1)
+    def _():
+        give.wait()
+
+
+def make_middle(mixed_pieces, pieces, center, gain, shift, n_seq, rows):
+    length, width = center.shape
+    n, many = len(pieces), len(mixed_pieces)
+    block = block_of(length)
+    row = whole_spec(1, width)
+    weight_shape = (n_seq, n, rows, width)
+    return call_kernel(
+        lambda *refs: middle_kernel(n, n_seq, many, *refs),
+        length,
+        [block_spec(block, width), row, row] + any_specs(n + many),
+        [
+            rows_out(length, width, bf16),
+            rows_out(length, width, bf16),
+            rows_out(length, 128, f32),
+            rows_out(length, width, bf16),
+            (jax.ShapeDtypeStruct(weight_shape, bf16), pl.BlockSpec(memory_space=pl.ANY)),
+        ],
+        [
+            pltpu.VMEM(weight_shape, bf16),
+            pltpu.VMEM((length, width), bf16),
+            pltpu.SemaphoreType.DMA((n * n_seq + many,)),
+            pltpu.SemaphoreType.DMA,
+        ],
+        (center, gain, shift, *pieces, *mixed_pieces),
+        "make_middle",
+        2 * length * width * width,
+    )
+
+
+def feed_kernel(n, *refs):
+    input_ref, grad_ref, unit_ref, inverse_ref, gain_ref, output_ref = refs[:6]
+    pieces = refs[6 : 6 + n]
+    hidden_ref, grads_ref, result_ref, back_ref, through_ref, sums_ref = refs[6 + n : 12 + n]
+    weight_ref, sems = refs[12 + n :]
+    load_pieces(pieces, weight_ref, sems)
+    size = hidden_ref.shape[1]
+    second_input = input_ref[...]
+    gate = dot(second_input, weight_of(weight_ref, 0, size), ((1,), (0,)))
+    upper = dot(second_input, weight_of(weight_ref, size, size), ((1,), (0,)))
+    hidden_grad = dot(grad_ref[...], weight_of(weight_ref, 2 * size, size), ((1,), (0,)))
+    sigmoid = jax.nn.sigmoid(gate)
+    activated = gate * sigmoid
+    hidden = (activated * upper).astype(bf16)
+    hidden_ref[...] = hidden
+    gate_grad = (hidden_grad * upper * sigmoid * (1.0 + gate * (1.0 - sigmoid))).astype(bf16)
+    grads_ref[:, :size] = gate_grad
+    up_grad = (hidden_grad * activated).astype(bf16)
+    grads_ref[:, size:] = up_grad
+    result_ref[...] = dot(hidden, weight_of(weight_ref, 2 * size, size), ((1,), (1,))).astype(bf16)
+    second = dot(gate_grad, weight_of(weight_ref, 0, size), ((1,), (1,)))
+    second += dot(up_grad, weight_of(weight_ref, size, size), ((1,), (1,)))
+    unit = unit_ref[...].astype(f32)
+    add_sums(sums_ref, second * unit, second)
+    back = norm_back(second, unit, inverse_ref[:, 0:1], gain_ref[...]).astype(bf16)
+    back_ref[...] = back
+    through = dot(back, output_ref[...], ((1,), (1,))).astype(bf16)
+    columns = through_ref.shape[2]
+    for i in range(through_ref.shape[0]):
+        through_ref[i] = through[:, i * columns : (i + 1) * columns]
+
+
+def feed(second_input, down_grad, unit, inverse, gain, output_all, pieces, rows, n_seq):
+    length, width = second_input.shape
+    size = pieces[0].shape[2] // 3
+    n = len(pieces)
+    block = block_of(length)
+    full = block_spec(block, width)
+    return call_kernel(
+        lambda *refs: feed_kernel(n, *refs),
+        length,
+        [full, full, full, block_spec(block, 128), whole_spec(1, width), once_spec(width, width)]
+        + any_specs(n),
+        [rows_out(length, size, bf16), rows_out(length, 2 * size, bf16)]
+        + [rows_out(length, width, bf16)] * 2
+        + [
+            (
+                jax.ShapeDtypeStruct((n_seq, length, width // n_seq), bf16),
+                pl.BlockSpec((n_seq, block, width // n_seq), lambda i: (0, i, 0)),
+            ),
+            sums_out(width),
+        ],
+        [
+            pltpu.VMEM((pieces[0].shape[0], n, rows, 3 * size), bf16),
+            pltpu.SemaphoreType.DMA((n,)),
+        ],
+        (second_input, down_grad, unit, inverse, gain, output_all, *pieces),
+        "feed",
+        12 * length * width * size + 2 * length * width * width,
+    )
+
+
+def first_kernel(n, *refs):
+    grad_ref, center_ref, gain_ref, back_ref = refs[:4]
+    pieces = refs[4 : 4 + n]
+    both_ref, sums_ref, bias_ref, weight_ref, sems = refs[4 + n :]
+    load_pieces(pieces, weight_ref, sems)
+    grad = grad_ref[...]
+    first = dot(grad, weight_of(weight_ref, 0, grad.shape[1]), ((1,), (1,)))
+    unit, inverse = unit_of(center_ref[...].astype(f32))
+    add_sums(sums_ref, first * unit, first)
+    add_sums(bias_ref, grad.astype(f32))
+    both = back_ref[...].astype(f32) + norm_back(first, unit, inverse, gain_ref[...])
+    both_ref[...] = both.astype(bf16)
+
+
+def first_back(joint_grad, center, gain, back, pieces, rows):
+    length, width = center.shape
+    total = joint_grad.shape[1]
+    n = len(pieces)
+    block = block_of(length)
+    full = block_spec(block, width)
+    return call_kernel(
+        lambda *refs: first_kernel(n, *refs),
+        length,
+        [block_spec(block, total), full, whole_spec(1, width), full] + any_specs(n),
+        [rows_out(length, width, bf16), sums_out(width), sums_out(total)],
+        [
+            pltpu.VMEM((pieces[0].shape[0], n, rows, total), bf16),
+            pltpu.SemaphoreType.DMA((n,)),
+        ],
+        (joint_grad, center, gain, back, *pieces),
+        "first_back",
+        2 * length * width * total,
+    )
+
+
+def grad_kernel(rows, has_rest, has_below, *refs):
+    left_ref, right_ref = refs[:2]
+    refs = refs[2:]
+    part = dot(left_ref[...], right_ref[...], ((0,), (0,)))
+    if has_rest:
+        rest_ref, refs = refs[0], refs[1:]
+        local = rest_ref.shape[0]
+        first = pl.multiple_of(lax.axis_index("seq") * local, local)
+        part += dot(left_ref[pl.ds(first, local), :], rest_ref[...], ((0,), (0,)))
+    if has_below:
+        below_ref, refs = refs[0], refs[1:]
+    keep_ref, send_ref, part_ref = refs
+    me = lax.axis_index("batch")
+    part_ref[...] = part.astype(bf16).reshape(part_ref.shape)
+    for far in range(2):
+        for near, ref in enumerate((keep_ref, send_ref)):
+            batch_at = me ^ (2 * far + near)
+            ref[far, 0, :rows] = part_ref[batch_at]
+            if has_below:
+                ref[far, 0, rows:] = below_ref[0, batch_at]
+
+
+def weight_grad(left, right, n_seq, n_batch, rest=None, below=None):
+    length, width = left.shape
+    c = right.shape[1]
+    rows = width // (n_seq * n_batch)
+    if n_seq != 8 or n_batch != 4:
+        if rest is not None:
+            first = lax.axis_index("seq") * rest.shape[0]
+            mine = lax.dynamic_slice_in_dim(right, first, rest.shape[0], 0) + rest
+            right = lax.dynamic_update_slice_in_dim(right, mine, first, 0)
+        part = dot(left, right, ((0,), (0,))).astype(bf16).reshape(n_seq, n_batch, rows, c)
+        if below is not None:
+            part = jnp.concatenate([part, below], axis=2)
+        return part, None
+    args = [left, right]
+    specs = [pl.BlockSpec((length, width // n_seq), lambda i: (0, i)), once_spec(length, c)]
+    high = rows
+    if rest is not None:
+        args.append(rest)
+        specs.append(once_spec(*rest.shape))
+    if below is not None:
+        high += below.shape[2]
+        args.append(below)
+        specs.append(pl.BlockSpec((1,) + below.shape[1:], lambda i: (i, 0, 0, 0)))
+    shape = jax.ShapeDtypeStruct((2, n_seq, high, c), bf16)
+    spec = pl.BlockSpec((2, 1, high, c), lambda i: (0, i, 0, 0))
+    return pl.pallas_call(
+        lambda *refs: grad_kernel(rows, rest is not None, below is not None, *refs),
+        grid=(n_seq,),
+        in_specs=specs,
+        out_specs=[spec, spec],
+        out_shape=[shape, shape],
+        scratch_shapes=[pltpu.VMEM((n_batch, rows, c), bf16)],
+        compiler_params=pltpu.CompilerParams(
+            vmem_limit_bytes=VMEM_BYTES, dimension_semantics=("arbitrary",)
+        ),
+        cost_estimate=pl.CostEstimate(
+            flops=2 * length * width * c,
+            bytes_accessed=2 * (length * width + length * c + 2 * width * c),
+            transcendentals=0,
+        ),
+        name="weight_grad",
+    )(*args)
+
+
+def grad_near(halves, n_batch):
+    keep, send = halves
+    if send is None:
+        return scatter_near(keep, n_batch), None
+    return keep, swap(send, "batch", n_batch, 1)
+
+
+def grad_far_begin(halves, n_batch):
+    keep, got = halves
+    if got is None:
+        return scatter_far(keep, n_batch), None
+    keep, got = keep.astype(f32), got.astype(f32)
+    other = swap((keep[1] + got[1]).astype(bf16), "batch", n_batch, 2)
+    return (keep[0] + got[0]).astype(bf16), other
+
+
+def grad_far_end(state):
+    keep, other = state
+    if other is None:
+        return keep
+    return (keep.astype(f32) + other.astype(f32)).astype(bf16)
+
+
 def make_body(n_seq, n_batch):
     def body(
         tokens,
@@ -436,15 +842,12 @@
         tables = [jnp.asarray(t) for t in turn_tables(length)]
 
         center_own = values - mean_of(values)
-        inverse_one = lax.rsqrt(mean_of(center_own * center_own) + EPSILON)
-        unit_own = center_own * inverse_one
-        ring = Gather(center_own.astype(bf16), n_seq)
+        ring = Gather(jnp.concatenate([center_own.astype(bf16), output_weight]), n_seq)
 
         small = jnp.concatenate(
             [attention_gain, attention_shift, feedfwd_gain, feedfwd_shift, joint_bias]
         )
-        extra = -(-small.shape[0] // (3 * columns))
-        small = jnp.pad(small, (0, 8 * 3 * columns - small.shape[0])).reshape(8, 3 * columns)
+        small = jnp.pad(small[None], ((0, 15), (0, 3 * columns - small.shape[0])))
         blocks = jnp.transpose(joint_weight.reshape(rows, 3, n_seq, columns), (2, 0, 1, 3))
         blocks = blocks.reshape(n_seq, rows, 3 * columns)
         blocks = jnp.concatenate(
@@ -458,25 +861,37 @@
         ff_blocks = ff_blocks.reshape(n_seq, rows, 3 * ff_local)
 
         ring.step()
-        blocks = exchange_near(blocks, n_seq)
-        ff_blocks = after(ff_blocks, blocks)
-        ff_blocks = exchange_near(ff_blocks, n_seq)
-        (blocks,) = ring.tie(blocks)
-        ring.step()
-        blocks = exchange_far(blocks, n_seq)
-        blocks, ff_blocks = ring.tie(blocks, ff_blocks)
+        flight = exchange_begin(blocks, n_seq, 1)
+        ff_flight = exchange_begin(ff_blocks, n_seq, 4)
+        (flight,) = ring.tie(flight)
+        blocks = exchange_end(flight, n_seq, 1)
+        ring.step()
+        flight = exchange_begin(blocks, n_seq, 2)
+        flight, ff_flight = ring.tie(flight, ff_flight)
+        blocks = exchange_end(flight, n_seq, 2)
+        ff_blocks = rest_of_exchange(exchange_end(ff_flight, n_seq, 4), n_seq)
+        ring.step()
+        flight = exchange_begin(blocks, n_seq, 4)
+        ff_flight = exchange_begin(ff_blocks, n_seq, 1)
+        flight, ff_flight = ring.tie(flight, ff_flight)
+        blocks = rest_of_exchange(exchange_end(flight, n_seq, 4), n_seq)
+        ff_blocks = exchange_end(ff_flight, n_seq, 1)
         ring.step()
         held = gather_far(blocks, n_batch)
-        ff_blocks = exchange_far(ff_blocks, n_seq)
-        (tied,) = ring.tie(held[-1][1])
-        held[-1] = (held[-1][0], tied)
-        ring.step()
-        joint_all = gather_near(held, n_batch)
-        center = join(ring.pieces, n_seq, 0)
-        joint_all, center, ff_blocks = tie(joint_all, center, ff_blocks)
-        ff_held = gather_far(ff_blocks, n_batch)
-        small = joint_all[:, :, rows : rows + extra].reshape(n_seq, n_batch, -1)
-        joint_all = joint_all[:, :, :rows].reshape(width, 3 * columns)
+        ff_flight = exchange_begin(ff_blocks, n_seq, 2)
+        (held_last,) = ring.tie(held[-1][1])
+        held[-1] = (held[-1][0], held_last)
+        pieces = gather_near(held, n_batch)
+        center_pieces = [v for _, v in ring.pieces]
+        output_held = jnp.concatenate([v[local:] for v in center_pieces])
+        output_held, *pieces = tie(output_held, *pieces)
+        output_held = gather_far(output_held, n_batch)
+
+        small = jnp.stack([v[:, rows] for v in pieces], axis=1)
+        batch_at = lax.axis_index("batch")
+        for bit in bits_of(n_batch):
+            flipped = small.reshape(n_seq, -1, 2, bit, small.shape[2])[:, :, ::-1]
+            small = jnp.where((batch_at & bit) == 0, small, flipped.reshape(small.shape))
         piece = width // (n_seq * n_batch)
 
         def small_part(start, size):
@@ -489,188 +904,120 @@
         bias_all = small_part(4 * piece, 3 * piece).reshape(3, n_seq, columns)
         bias = lax.dynamic_slice_in_dim(bias_all, seq_at, 1, 1).reshape(1, 3 * columns)
 
-        output_all = lax.all_gather(output_weight, ("seq", "batch"), axis=0, tiled=True)
-
-        def output_rows(at):
-            return lax.dynamic_slice_in_dim(output_all, at * columns, columns, 0)
-
         chosen = language[:, None] == jnp.arange(LANGS, dtype=jnp.int32)[None, :]
         row_scale = jnp.sum(jnp.where(chosen, language_weight[None, :], 0.0), axis=1)
         cotangent = output_grad[0] * row_scale[:, None]
-        down_grad = after(cotangent.astype(bf16), center)
+        down_grad = after(cotangent.astype(bf16), pieces[0])
         down_grad = lax.all_gather(down_grad, "seq", axis=0, tiled=True)
 
-        unit_one, _ = unit_of(center.astype(f32))
-        first_input = (unit_one * gain_one + shift_one).astype(bf16)
-        joint = dot(first_input, joint_all, ((1,), (0,))) + bias
-        low, context, mixed, lse = attend(joint, tables)
-
+        low, first_input, center = make_heads(
+            center_pieces, gain_one, shift_one, bias, tables, pieces, rows, local
+        )
+        context, mixed, lse = attend(low)
+
+        mixed, held_last, ff_flight = tie(mixed, output_held[-1][1], ff_flight)
+        output_held[-1] = (output_held[-1][0], held_last)
         ring = Gather(mixed, n_seq)
         ring.step()
+        held = gather_far(exchange_end(ff_flight, n_seq, 2), n_batch)
         ring.tie()
         ring.step()
+        output_pieces = gather_near(output_held, n_batch)
+        output_pieces = ring.tie(*output_pieces)
+        ring.step()
         ring.tie()
         ring.step()
-        (tied,) = ring.tie(ff_held[-1][1])
-        ff_held[-1] = (ff_held[-1][0], tied)
-        ring.step()
-        ff_all = gather_near(ff_held, n_batch)
-        if n_seq == 8:
-            at, last = ring.pieces[-1]
-            early = join(ring.pieces[:-1] + [(at, jnp.zeros_like(last))], n_seq, 1)
-            projected = dot(early, output_all, ((1,), (0,)))
-            projected, last, ff_all = tie(projected, last, ff_all)
-            projected = projected + dot(last, output_rows(at), ((1,), (0,)))
-            mixed_all = lax.dynamic_update_slice_in_dim(early, last, at * columns, 1)
-        else:
-            mixed_all = join(ring.pieces, n_seq, 1)
-            projected = dot(mixed_all, output_all, ((1,), (0,)))
-        ff_all = ff_all.reshape(width, 3 * ff_local)
-        gate_all = ff_all[:, :ff_local]
-        up_all = ff_all[:, ff_local : 2 * ff_local]
-        down_all = ff_all[:, 2 * ff_local :]
-        middle_own = values + lax.dynamic_slice_in_dim(projected, first_row, local, 0)
-        unit_two, inverse_two = unit_of(center.astype(f32) + projected)
-        second_input = (unit_two * gain_two + shift_two).astype(bf16)
-
-        gate = dot(second_input, gate_all, ((1,), (0,)))
-        upper = dot(second_input, up_all, ((1,), (0,)))
-        sigmoid = jax.nn.sigmoid(gate)
-        activated = gate * sigmoid
-        hidden = (activated * upper).astype(bf16)
-        result_part = dot(hidden, down_all, ((1,), (1,))).astype(bf16)
+        (held_last,) = ring.tie(held[-1][1])
+        held[-1] = (held[-1][0], held_last)
+        ff_pieces = gather_near(held, n_batch)
+        mixed_pieces = [v for _, v in ring.pieces]
+        if columns % 128:
+            mixed_pieces = [join(ring.pieces, n_seq, 1)]
+        second_input, unit_two, inverse_two, mixed_all, output_all = make_middle(
+            mixed_pieces, output_pieces, center, gain_two, shift_two, n_seq, rows
+        )
+        output_all = output_all.reshape(width, width)
+
+        hidden, middle_grads, result_part, back, through, second_sums = feed(
+            second_input,
+            down_grad,
+            unit_two,
+            inverse_two,
+            gain_two,
+            output_all,
+            ff_pieces,
+            rows,
+            n_seq,
+        )
         result_sum = lax.psum_scatter(result_part, "seq", scatter_dimension=0, tiled=True)
-
-        def split(grad, *shape):
-            return grad.astype(bf16).reshape((n_seq, n_batch, rows) + shape)
-
-        grad_down = scatter_near(split(dot(down_grad, hidden, ((0,), (0,))), ff_local), n_batch)
-        hidden_grad = dot(down_grad, down_all, ((1,), (0,)))
-        hidden_grad, result_part = tie(hidden_grad, result_part)
-        gate_grad = (hidden_grad * upper * sigmoid * (1.0 + gate * (1.0 - sigmoid))).astype(bf16)
-        up_grad = (hidden_grad * activated).astype(bf16)
-        second_part = dot(gate_grad, gate_all, ((1,), (1,))) + dot(up_grad, up_all, ((1,), (1,)))
-        second_part, grad_down = tie(second_part, grad_down)
-        grad_down = scatter_far(grad_down, n_batch)
-
-        scaled = second_part * (gain_two * inverse_two)
-        scaled_low = scaled.astype(bf16)
-        sums = jnp.stack([jnp.mean(scaled, axis=-1), jnp.mean(scaled * unit_two, axis=-1)])
-        sums = sums.astype(bf16).reshape(-1, columns)
-        if n_seq == 8:
-
-            def through_block(at):
-                part = dot(scaled_low, output_rows(at), ((1,), (1,))).astype(bf16)
-                return jnp.concatenate([part, sums], axis=0)
-
-        else:
-            through = dot(scaled_low, output_all, ((1,), (1,))).astype(bf16)
-
-            def through_block(at):
-                return jnp.concatenate([through[:, at * columns : (at + 1) * columns], sums], axis=0)
-
-        heads_weight = output_rows(seq_at)
-        ring = Scatter(through_block, n_seq)
-        ring.step()
-        grad_both = [split(dot(second_input, g, ((0,), (0,))), ff_local) for g in (gate_grad, up_grad)]
-        grad_both = jnp.concatenate(grad_both, axis=3)
-        grad_down, grad_both = ring.tie(grad_down, grad_both)
-        ring.step()
-        grad_both = scatter_near(grad_both, n_batch)
-        grad_down = exchange_near(grad_down, n_seq)
-        grad_both, grad_down = ring.tie(grad_both, grad_down)
-        ring.step()
-        grad_both = scatter_far(grad_both, n_batch)
-        from_cot = dot(down_grad, heads_weight, ((1,), (1,)))
-        from_unit = dot(unit_two.astype(bf16), heads_weight, ((1,), (1,)))
-        from_cot, from_unit, result_sum = ring.tie(from_cot, from_unit, result_sum)
-        ring.step()
-        grad_output = dot(mixed_all, scaled_low, ((0,), (0,))).astype(bf16)
-        (grad_output,) = ring.tie(grad_output)
-        through = ring.total()
-        through, grad_both, grad_down = tie(through, grad_both, grad_down)
-        grad_both = exchange_near(grad_both, n_seq)
-        grad_down = exchange_far(grad_down, n_seq)
-        result = middle_own + result_sum.astype(f32)
-        weight_sums = jnp.sum(heads_weight.astype(f32), axis=1)[None, :]
-        means = through[length:].reshape(2, length)
-        mean_one, mean_two = means[0][:, None], means[1][:, None]
-        context_grad = (
-            through[:length] + from_cot - mean_one * weight_sums - mean_two * from_unit
-        ).astype(bf16)
-        joint_grad = attend_back(low, context_grad, context, lse, tables)
-
-        rest = down_grad.astype(f32) - mean_one - unit_two * mean_two
-        rest = dot(mixed, rest.astype(bf16), ((0,), (0,)))
-        rest = rest + lax.dynamic_slice_in_dim(grad_output, seq_at * columns, columns, 0)
-        grad_output = lax.dynamic_update_slice_in_dim(
-            grad_output, rest.astype(bf16), seq_at * columns, 0
-        )
-        joint_grad, grad_both, grad_down, grad_output = tie(
-            joint_grad, grad_both, grad_down, grad_output
-        )
-        grad_joint = dot(first_input, joint_grad, ((0,), (0,)))
-        first_part = dot(joint_grad, joint_all, ((1,), (1,)))
-
-        bias_part = jnp.sum(joint_grad.astype(f32), axis=0).reshape(3, 1, columns)
-        bias_part = lax.dynamic_update_slice_in_dim(
-            jnp.zeros((3, n_seq, columns), f32), bias_part, seq_at, 1
-        )
-        vectors = [
-            jnp.sum(first_part * unit_one, axis=0),
-            jnp.sum(first_part, axis=0),
-            jnp.sum(second_part * unit_two, axis=0),
-            jnp.sum(second_part, axis=0),
-            bias_part,
-        ]
-        vectors = jnp.concatenate([v.reshape(n_seq, n_batch, -1) for v in vectors], axis=2)
-        vectors = jnp.pad(vectors, ((0, 0), (0, 0), (0, 8 * 3 * columns - vectors.shape[2])))
-        vectors = vectors.reshape(n_seq, n_batch, 8, 3 * columns).astype(bf16)
-        grad_joint = jnp.concatenate([split(grad_joint, 3 * columns), vectors], axis=2)
-        grad_joint = scatter_near(grad_joint, n_batch)
-
-        inner = first_part * (gain_one * lax.rsqrt(mean_of(center.astype(f32) ** 2) + EPSILON))
-        first_sums = jnp.stack([jnp.mean(inner, axis=-1), jnp.mean(inner * unit_one, axis=-1)])
-        both = (scaled + inner).astype(bf16)
-        both, grad_joint = tie(both, grad_joint)
-
-        def both_block(at):
-            part = lax.dynamic_slice_in_dim(both, at * local, local, 0)
-            below = lax.dynamic_slice_in_dim(first_sums, at * local, local, 1)
-            below = jnp.pad(below.reshape(-1), (0, 8 * width - 2 * local)).reshape(8, width)
-            return jnp.concatenate([part, below.astype(bf16)], axis=0)
-
-        ring = Scatter(both_block, n_seq)
-        ring.step()
-        grad_joint = scatter_far(grad_joint, n_batch)
-        grad_output = scatter_near(split(grad_output, width), n_batch)
-        grad_joint, grad_output = ring.tie(grad_joint, grad_output)
-        ring.step()
-        grad_joint = exchange_near(grad_joint, n_seq)
-        grad_output = scatter_far(grad_output, n_batch)
-        (grad_joint,) = ring.tie(grad_joint)
-        ring.step()
-        grad_joint = exchange_far(grad_joint, n_seq)
-        grad_joint, grad_both, grad_output = ring.tie(grad_joint, grad_both, grad_output)
-        ring.step()
-        grad_both = exchange_far(grad_both, n_seq)
-        grad_output = lax.psum_scatter(
-            grad_output, "seq", scatter_dimension=0, tiled=False
-        ).astype(f32)
-        both_own = ring.total()
-        first_sums = both_own[local].reshape(-1)[: 2 * local].reshape(2, local)
 
         def own(array):
             return lax.dynamic_slice_in_dim(array, first_row, local, 0)
 
-        token_grad = (
-            cotangent
-            - own(mean_one)
-            - own(unit_two) * own(mean_two)
-            + both_own[:local]
-            - first_sums[0][:, None]
-            - unit_own * first_sums[1][:, None]
+        ring = Scatter(lambda at: lax.dynamic_index_in_dim(through, at, 0, False), n_seq)
+        ring.step()
+        grad_down = grad_near(weight_grad(down_grad, hidden, n_seq, n_batch), n_batch)
+        (grad_down,) = ring.tie(grad_down)
+        ring.step()
+        grad_down = grad_far_begin(grad_down, n_batch)
+        grad_both = weight_grad(second_input, middle_grads, n_seq, n_batch)
+        grad_both, grad_down = ring.tie(grad_both, grad_down)
+        ring.step()
+        grad_both = grad_near(grad_both, n_batch)
+        grad_down = exchange_begin(grad_far_end(grad_down), n_seq, 4)
+        grad_output = weight_grad(
+            mixed_all, back, n_seq, n_batch, rest=cotangent.astype(bf16)
         )
+        grad_both, grad_output = ring.tie(grad_both, grad_output)
+        ring.step()
+        grad_both = grad_far_begin(grad_both, n_batch)
+        grad_output = grad_near(grad_output, n_batch)
+        heads_weight = lax.dynamic_slice_in_dim(output_all, seq_at * columns, columns, 0)
+        from_cot = dot(down_grad, heads_weight, ((1,), (1,)))
+        from_cot, grad_output, grad_down = ring.tie(from_cot, grad_output, grad_down)
+        context_grad = (ring.total() + from_cot).astype(bf16)
+        grad_down = rest_of_exchange(exchange_end(grad_down, n_seq, 4), n_seq)
+        grad_down = exchange_begin(grad_down, n_seq, 1)
+        joint_grad = attend_back(low, context_grad, context, lse, tables)
+        joint_grad, grad_both, grad_down = tie(joint_grad, grad_both, grad_down)
+        grad_output = grad_far_begin(grad_output, n_batch)
+        grad_both = exchange_begin(grad_far_end(grad_both), n_seq, 4)
+        grad_down = exchange_begin(exchange_end(grad_down, n_seq, 1), n_seq, 2)
+        both, first_sums, bias_sums = first_back(joint_grad, center, gain_one, back, pieces, rows)
+
+        ring = Scatter(lambda at: lax.dynamic_slice_in_dim(both, at * local, local, 0), n_seq)
+        ring.step()
+        bias_part = lax.dynamic_update_slice_in_dim(
+            jnp.zeros((3, n_seq, columns), f32), bias_sums[:1].reshape(3, 1, columns), seq_at, 1
+        )
+        vectors = [first_sums[0], first_sums[1], second_sums[0], second_sums[1], bias_part]
+        vectors = [v.reshape(n_seq, n_batch, 1, -1).astype(bf16) for v in vectors]
+        vectors = jnp.concatenate(vectors, axis=3)
+        vectors = jnp.pad(vectors, ((0, 0), (0, 0), (0, 15), (0, 3 * columns - 7 * piece)))
+        grad_joint = weight_grad(first_input, joint_grad, n_seq, n_batch, below=vectors)
+        grad_joint, grad_both, grad_down = ring.tie(grad_joint, grad_both, grad_down)
+        ring.step()
+        grad_joint = grad_near(grad_joint, n_batch)
+        grad_both = rest_of_exchange(exchange_end(grad_both, n_seq, 4), n_seq)
+        grad_both = exchange_begin(grad_both, n_seq, 1)
+        grad_down = exchange_end(grad_down, n_seq, 2)
+        projected_own = dot(own(mixed_all), output_all, ((1,), (0,)))
+        result = values + projected_own + result_sum.astype(f32)
+        grad_joint, grad_output, result = ring.tie(grad_joint, grad_output, result)
+        grad_output = lax.psum_scatter(
+            grad_far_end(grad_output), "seq", scatter_dimension=0, tiled=False
+        )
+        ring.step()
+        grad_joint = grad_far_begin(grad_joint, n_batch)
+        grad_joint, grad_both = ring.tie(grad_joint, grad_both)
+        ring.step()
+        grad_joint = exchange_begin(grad_far_end(grad_joint), n_seq, 1)
+        grad_both = exchange_begin(exchange_end(grad_both, n_seq, 1), n_seq, 2)
+        (grad_joint,) = ring.tie(grad_joint)
+        grad_joint = exchange_far(exchange_end(grad_joint, n_seq, 1), n_seq)
+        grad_both = exchange_end(grad_both, n_seq, 2)
+        token_grad = cotangent + ring.total()
+        grad_output = grad_output.astype(f32)
 
         def unsplit(grad):
             grad = grad.reshape(n_seq, rows, tiles, 128).astype(f32)
@@ -680,7 +1027,7 @@
         grad_up = unsplit(grad_both[:, :, ff_local:])
         grad_down = unsplit(grad_down)
         grad_joint = grad_joint.astype(f32)
-        vectors = jnp.sum(grad_joint[:, rows : rows + extra], axis=0).reshape(-1)
+        vectors = jnp.sum(grad_joint[:, rows], axis=0)
         grad_joint = grad_joint[:, :rows].reshape(n_seq, rows, 3, columns)
         grad_joint = jnp.transpose(grad_joint, (1, 2, 0, 3)).reshape(rows, 3 * width)
         return (

time: 806 us -> 751 us (0.932)
  matrix products: 151 us -> 11.9 us
  Pallas kernels: 25.2 us -> 162 us
  waiting for transfers between devices: 275 us -> 334 us
  other arithmetic: 106 us -> 58.5 us
  local copies, waits for them, and re-layouts: 121 us -> 80 us
  starting transfers between devices: 100 us -> 80.9 us
    dot_general x26 -> x2, matrix products: 151 us -> 11.9 us  [dot(): lax.dot_general(left, right, (contract, ((), ())), preferred_element_type...]
    pallas_call x1 -> x9, Pallas kernels: 11.7 us -> 148 us  [the longest x4 91.8 us: call_kernel(): pl.pallas_call(kernel, grid=(length // block,), in_specs=in_specs, out_sp...]
    ppermute x28, waiting for transfers between devices: 57.1 us -> 177 us  [ring_step(): lax.ppermute(value, 'seq', [(RING[i], RING[(i + way) % 8]) for i in range...]
    ppermute x34 -> x33, waiting for transfers between devices: 193 us -> 157 us  [swap(): return lax.ppermute(value, axis, [(i, i ^ bit) for i in range(number)])]
    dynamic_update_slice x27 -> x13, local copies, waits for them, and re-layouts: 38.1 us -> 10.9 us  [exchange_end(): out = lax.dynamic_update_slice_in_dim(pairs, got, 1 - mine, 1)]
    reduce_scatter x1, waiting for transfers between devices: 24.3 us -> 0.01 us  [body(): lax.psum_scatter(grad_far_end(grad_output), 'seq', scatter_dimension=0, t...]
    reduce_sum x6 -> x1, other arithmetic: 25.4 us -> 1.44 us  [mean_of(): return jnp.mean(values, axis=-1, keepdims=True)]
    ppermute x28, starting transfers between devices: 47.1 us -> 33.2 us  [ring_step(): lax.ppermute(value, 'seq', [(RING[i], RING[(i + way) % 8]) for i in range...]
  transfers between devices with their start and end apart: 66 -> 64, of which waited for: 32 -> 31; matrix products, arithmetic and copies ran while one was open for 40% -> 18% of each run, Pallas kernels for 3% -> 15%
where the time goes in v2:
time: 751 us; the launch traced here: 743 us
  waiting for transfers between devices  334 us (44%)
  Pallas kernels  162 us (22%)
  starting transfers between devices  80.9 us (11%)
  local copies, waits for them, and re-layouts  80 us (11%)
  other arithmetic  58.5 us (8%)
  between operations  16.1 us (2%)
  matrix products  11.9 us (2%)
    ppermute x28, waiting for transfers between devices, ring_step(): lax.ppermute(value, 'seq', [(RING[i], RING[(i + way) % 8]) for i in range...  177 us
    ppermute x33, waiting for transfers between devices, swap(): return lax.ppermute(value, axis, [(i, i ^ bit) for i in range(number)])  157 us
    pallas_call x4, Pallas kernels, call_kernel(): pl.pallas_call(kernel, grid=(length // block,), in_specs=in_specs, out_sp...  91.8 us
    pallas_call x4, Pallas kernels, weight_grad(): pl.pallas_call(lambda *refs: grad_kernel(rows, rest is not None, below is...  48.2 us
    ppermute x33, starting transfers between devices, swap(): return lax.ppermute(value, axis, [(i, i ^ bit) for i in range(number)])  47.4 us
    ppermute x28, starting transfers between devices, ring_step(): lax.ppermute(value, 'seq', [(RING[i], RING[(i + way) % 8]) for i in range...  33.2 us
    unnamed x127, local copies, waits for them, and re-layouts  23.6 us
  transfers between devices with their start and end apart: 64, of which 31 were waited for; matrix products, arithmetic and copies ran while one was open for 18% of the time, Pallas kernels for 15%

profile of v2, /device:TPU:8, one launch (start us, length us, event | category | flops | bytes accessed | tf_op | source)
XLA Modules:
  0.0 743.5 jit_solution(62904550103155941)
XLA Ops:
  30.2 25.7 %collective-permute-done.refs_11_ = bf16[192,2048]{1,0:T(8,128)(2,1)} collective-permute-done((bf16[192,2048]{1,0:T(8,128)(2,1)}, bf16[192,2048]{1,0:T(8,128)(2,1)}, u32[]{:S(2)}, u32[]{:S(2)}) %collective-permute-start) | collective-permute-done | bytes 786464 | tf_op jit(solution)/shard_map/ppermute | solution.py:135
  60.4 20.3 %collective-permute-done.6 = bf16[1,1,4,64,2304]{4,3,2,1,0:T(8,128)(2,1)} collective-permute-done((bf16[1,1,4,64,2304]{4,3,2,1,0:T(8,128)(2,1)}, bf16[1,1,4,64,2304]{4,3,2,1,0:T(8,128)(2,1)}, u32[]{:S(2)}, u32[]{:S(2)}) %collective-permute-start.6) | collective-permute-done | bytes 1179680 | tf_op jit(solution)/shard_map/ppermute | solution.py:27
  80.7 13.0 %collective-permute-done.5 = bf16[2,1,2,80,768]{4,3,2,1,0:T(8,128)(2,1)S(1)} collective-permute-done((bf16[2,1,2,80,768]{4,3,2,1,0:T(8,128)(2,1)S(1)}, bf16[2,1,2,80,768]{4,3,2,1,0:T(8,128)(2,1)S(1)}, u32[]{:S(2)}, u32[]{:S(2)}) %collective-permute-start.5) | collective-permute-done | bytes 491552 | tf_op jit(solution)/shard_map/ppermute | solution.py:27
  111.2 32.1 %collective-permute-done.9 = bf16[1,1,4,80,768]{4,3,2,1,0:T(8,128)(2,1)} collective-permute-done((bf16[1,1,4,80,768]{4,3,2,1,0:T(8,128)(2,1)}, bf16[1,1,4,80,768]{4,3,2,1,0:T(8,128)(2,1)}, u32[]{:S(2)}, u32[]{:S(2)}) %collective-permute-start.9) | collective-permute-done | bytes 491552 | tf_op jit(solution)/shard_map/ppermute | solution.py:27
  151.3 13.6 %collective-permute-done.11.refs_17_ = bf16[192,2048]{1,0:T(8,128)(2,1)S(1)} collective-permute-done((bf16[192,2048]{1,0:T(8,128)(2,1)}, bf16[192,2048]{1,0:T(8,128)(2,1)S(1)}, u32[]{:S(2)}, u32[]{:S(2)}) %collective-permute-start.11) | collective-permute-done | bytes 786464 | tf_op jit(solution)/shard_map/ppermute | solution.py:135
  184.1 12.2 %make_heads.1 = (bf16[1024,768]{1,0:T(8,128)(2,1)}, bf16[1024,2048]{1,0:T(8,128)(2,1)}, bf16[1024,2048]{1,0:T(8,128)(2,1)}) custom-call(f32[1,2048]{1,0:T(1,128)} %reshape.318.refs_0_.refs_2_, f32[1,2048]{1,0:T(1,128)} %reshape.319.refs_1_, f32[1,768]{1,0:T(1,128)} %bitcast.190, f32[1024,128]{1,0:T(8,128)} %constant.286.clone.refs_3_.cos_ref, ...), custom_call_target="tpu_custom_call" | custom-call | flops 3221225472 | bytes 6442450 | tf_op jit(solution)/shard_map/make_heads/pallas_call | solution.py:465
  196.3 8.3 %attend.1 = (f32[1024,256]{1,0:T(8,128)}, bf16[1024,256]{1,0:T(8,128)(2,1)}, f32[1024,128]{1,0:T(8,128)}) custom-call(bf16[1024,768]{1,0:T(8,128)(2,1)} %get-tuple-element.147.low_ref), custom_call_target="tpu_custom_call" | custom-call | flops 2147483648 | bytes 12582912 | tf_op jit(solution)/shard_map/attend/pallas_call | solution.py:302
  204.6 16.9 %collective-permute-done.16 = bf16[2,1,2,64,2304]{4,3,2,1,0:T(8,128)(2,1)} collective-permute-done((bf16[2,1,2,64,2304]{4,3,2,1,0:T(8,128)(2,1)}, bf16[2,1,2,64,2304]{4,3,2,1,0:T(8,128)(2,1)}, u32[]{:S(2)}, u32[]{:S(2)}) %collective-permute-start.16) | collective-permute-done | bytes 1179680 | tf_op jit(solution)/shard_map/ppermute | solution.py:27
  225.6 31.6 %collective-permute-done.17.refs_9_ = bf16[1024,256]{1,0:T(8,128)(2,1)S(1)} collective-permute-done((bf16[1024,256]{1,0:T(8,128)(2,1)S(1)}, bf16[1024,256]{1,0:T(8,128)(2,1)S(1)}, u32[]{:S(2)}, u32[]{:S(2)}) %collective-permute-start.17) | collective-permute-done | bytes 524320 | tf_op jit(solution)/shard_map/ppermute | solution.py:135
  262.4 21.3 %collective-permute-done.19.refs_11_ = bf16[1024,256]{1,0:T(8,128)(2,1)S(1)} collective-permute-done((bf16[1024,256]{1,0:T(8,128)(2,1)S(1)}, bf16[1024,256]{1,0:T(8,128)(2,1)S(1)}, u32[]{:S(2)}, u32[]{:S(2)}) %collective-permute-start.19) | collective-permute-done | bytes 524320 | tf_op jit(solution)/shard_map/ppermute | solution.py:135
  287.3 8.3 %collective-permute-done.23.refs_12_ = bf16[1024,256]{1,0:T(8,128)(2,1)S(1)} collective-permute-done((bf16[1024,256]{1,0:T(8,128)(2,1)S(1)}, bf16[1024,256]{1,0:T(8,128)(2,1)S(1)}, u32[]{:S(2)}, u32[]{:S(2)}) %collective-permute-start.23) | collective-permute-done | bytes 524320 | tf_op jit(solution)/shard_map/ppermute | solution.py:135
  298.3 11.8 %collective-permute-done.25.refs_14_ = bf16[1024,256]{1,0:T(8,128)(2,1)S(1)} collective-permute-done((bf16[1024,256]{1,0:T(8,128)(2,1)S(1)}, bf16[1024,256]{1,0:T(8,128)(2,1)S(1)}, u32[]{:S(2)}, u32[]{:S(2)}) %collective-permute-start.25) | collective-permute-done | bytes 524320 | tf_op jit(solution)/shard_map/ppermute | solution.py:135
  312.2 20.1 %make_middle.1 = (bf16[1024,2048]{1,0:T(8,128)(2,1)}, bf16[1024,2048]{1,0:T(8,128)(2,1)}, f32[1024,128]{1,0:T(8,128)}, bf16[1024,2048]{1,0:T(8,128)(2,1)}, bf16[8,4,64,2048]{3,2,1,0:T(8,128)(2,1)}) custom-call(bf16[1024,2048]{1,0:T(8,128)(2,1)} %get-tuple-element.148.refs_0_.refs_1_, f32[1,2048]{1,0:T(1,128)} %reshape.321.refs_1_.refs_4_, ...), custom_call_target="tpu_custom_call" | custom-call | flops 8589934592 | bytes 17179868 | tf_op jit(solution)/shard_map/make_middle/pallas_call | solution.py:465
  332.3 43.9 %feed.1 = (bf16[1024,768]{1,0:T(8,128)(2,1)}, bf16[1024,1536]{1,0:T(8,128)(2,1)}, bf16[1024,2048]{1,0:T(8,128)(2,1)}, bf16[1024,2048]{1,0:T(8,128)(2,1)}, bf16[8...) custom-call(bf16[1024,2048]{1,0:T(8,128)(2,1)} %get-tuple-element.164.refs_0_, ...), custom_call_target="tpu_custom_call" | custom-call | flops 27917287424 | bytes 55834576 | tf_op jit(solution)/shard_map/feed/pallas_call | solution.py:465
  376.3 9.4 %weight_grad.4 = (bf16[2,8,64,768]{3,2,1,0:T(8,128)(2,1)}, bf16[2,8,64,768]{3,2,1,0:T(8,128)(2,1)}) custom-call(bf16[1024,2048]{1,0:T(8,128)(2,1)} %all-gather.2.cloned.1.call-done.refs_1_.refs_0_, bf16[1024,768]{1,0:T(8,128)(2,1)} %get-tuple-element.173.refs_1_), custom_call_target="tpu_custom_call" | custom-call | flops 3221225472 | bytes 12058624 | tf_op jit(solution)/shard_map/weight_grad/pallas_call | solution.py:774
  392.9 12.3 %collective-permute-done.29 = bf16[1024,256]{1,0:T(8,128)(2,1)} collective-permute-done((bf16[1024,256]{1,0:T(8,128)(2,1)}, bf16[1024,256]{1,0:T(8,128)(2,1)}, u32[]{:S(2)}, u32[]{:S(2)}) %collective-permute-start.29) | collective-permute-done | bytes 524320 | tf_op jit(solution)/shard_map/ppermute | solution.py:135
  413.0 12.4 %weight_grad.5 = (bf16[2,8,64,1536]{3,2,1,0:T(8,128)(2,1)}, bf16[2,8,64,1536]{3,2,1,0:T(8,128)(2,1)}) custom-call(bf16[1024,2048]{1,0:T(8,128)(2,1)} %get-tuple-element.164.refs_0_, bf16[1024,1536]{1,0:T(8,128)(2,1)} %get-tuple-element.178.refs_1_), custom_call_target="tpu_custom_call" | custom-call | flops 6442450944 | bytes 19922944 | tf_op jit(solution)/shard_map/weight_grad/pallas_call | solution.py:774
  431.5 16.6 %weight_grad.6 = (bf16[2,8,64,2048]{3,2,1,0:T(8,128)(2,1)}, bf16[2,8,64,2048]{3,2,1,0:T(8,128)(2,1)}) custom-call(bf16[1024,2048]{1,0:T(8,128)(2,1)} %get-tuple-element.187.refs_0_, bf16[1024,2048]{1,0:T(8,128)(2,1)} %get-tuple-element.188.refs_1_.refs_3_, bf16[128,2048]{1,0:T(8,128)(2,1)} %bitcast_convert_fusion.refs_2_), custom_call_target="tpu_custom_call" | custom-call | flops 8589934592 | bytes 25165824 | tf_op jit(solution)/shard_map/weight_grad/pallas_call | solution.py:774
  448.1 9.8 %collective-permute-done.35 = bf16[1024,256]{1,0:T(8,128)(2,1)S(1)} collective-permute-done((bf16[1024,256]{1,0:T(8,128)(2,1)S(1)}, bf16[1024,256]{1,0:T(8,128)(2,1)S(1)}, u32[]{:S(2)}, u32[]{:S(2)}) %collective-permute-start.35) | collective-permute-done | bytes 524320 | tf_op jit(solution)/shard_map/ppermute | solution.py:135
  478.0 16.2 %collective-permute-done.40 = bf16[1,1,4,64,768]{4,3,2,1,0:T(8,128)(2,1)S(1)} collective-permute-done((bf16[1,1,4,64,768]{4,3,2,1,0:T(8,128)(2,1)}, bf16[1,1,4,64,768]{4,3,2,1,0:T(8,128)(2,1)S(1)}, u32[]{:S(2)}, u32[]{:S(2)}) %collective-permute-start.40) | collective-permute-done | bytes 393248 | tf_op jit(solution)/shard_map/ppermute | solution.py:27
  494.2 11.0 %collective-permute-done.38 = bf16[1024,256]{1,0:T(8,128)(2,1)S(1)} collective-permute-done((bf16[1024,256]{1,0:T(8,128)(2,1)S(1)}, bf16[1024,256]{1,0:T(8,128)(2,1)S(1)}, u32[]{:S(2)}, u32[]{:S(2)}) %collective-permute-start.38) | collective-permute-done | bytes 524320 | tf_op jit(solution)/shard_map/ppermute | solution.py:135
  519.3 13.5 %attend_back.1.refs_0_.refs_1_ = bf16[1024,768]{1,0:T(8,128)(2,1)} custom-call(bf16[1024,768]{1,0:T(8,128)(2,1)} %get-tuple-element.147.low_ref, bf16[1024,256]{1,0:T(8,128)(2,1)} %fusion.20.grad_ref, f32[1024,256]{1,0:T(8,128)} %get-tuple-element.200.context_ref, f32[1024,128]{1,0:T(8,128)} %get-tuple-element.201.lse_ref, ...), custom_call_target="tpu_custom_call" | custom-call | flops 5368709120 | bytes 12582912 | tf_op jit(solution)/shard_map/attend_back/pallas_call | solution.py:382
  535.6 15.6 %first_back.1 = (bf16[1024,2048]{1,0:T(8,128)(2,1)}, f32[8,2048]{1,0:T(8,128)}, f32[8,768]{1,0:T(8,128)}) custom-call(bf16[1024,768]{1,0:T(8,128)(2,1)} %attend_back.1.refs_0_.refs_1_, bf16[1024,2048]{1,0:T(8,128)(2,1)} %get-tuple-element.148.refs_0_.refs_1_, f32[1,2048]{1,0:T(1,128)} %reshape.318.refs_0_.refs_2_, ...), custom_call_target="tpu_custom_call" | custom-call | flops 3221225472 | bytes 6442450 | tf_op jit(solution)/shard_map/first_back/pallas_call | solution.py:465
  559.7 9.8 %weight_grad.7 = (bf16[2,8,80,768]{3,2,1,0:T(8,128)(2,1)}, bf16[2,8,80,768]{3,2,1,0:T(8,128)(2,1)}) custom-call(bf16[1024,2048]{1,0:T(8,128)(2,1)} %get-tuple-element.208.refs_0_, bf16[1024,768]{1,0:T(8,128)(2,1)} %attend_back.1.refs_0_.refs_1_, bf16[8,4,16,768]{3,2,1,0:T(8,128)(2,1)} %pad.22.refs_2_), custom_call_target="tpu_custom_call" | custom-call | flops 3221225472 | bytes 12058624 | tf_op jit(solution)/shard_map/weight_grad/pallas_call | solution.py:774
  569.5 21.4 %collective-permute-done.46 = bf16[2,1,2,64,768]{4,3,2,1,0:T(8,128)(2,1)} collective-permute-done((bf16[2,1,2,64,768]{4,3,2,1,0:T(8,128)(2,1)}, bf16[2,1,2,64,768]{4,3,2,1,0:T(8,128)(2,1)}, u32[]{:S(2)}, u32[]{:S(2)}) %collective-permute-start.46) | collective-permute-done | bytes 393248 | tf_op jit(solution)/shard_map/ppermute | solution.py:27
  591.1 6.0 fusion.4
  609.1 6.1 collective-permute-done.47
  630.2 7.9 %collective-permute-done.51 = bf16[128,2048]{1,0:T(8,128)(2,1)} collective-permute-done((bf16[128,2048]{1,0:T(8,128)(2,1)}, bf16[128,2048]{1,0:T(8,128)(2,1)}, u32[]{:S(2)}, u32[]{:S(2)}) %collective-permute-start.51) | collective-permute-done | bytes 524320 | tf_op jit(solution)/shard_map/ppermute | solution.py:135
  654.9 10.9 %collective-permute-done.56 = bf16[4,1,1,80,768]{4,3,0,2,1:T(8,128)(2,1)S(1)} collective-permute-done((bf16[4,1,1,80,768]{4,3,0,2,1:T(8,128)(2,1)S(1)}, bf16[4,1,1,80,768]{4,3,0,2,1:T(8,128)(2,1)S(1)}, u32[]{:S(2)}, u32[]{:S(2)}) %collective-permute-start.56) | collective-permute-done | bytes 491552 | tf_op jit(solution)/shard_map/ppermute | solution.py:27
  670.8 11.3 %collective-permute-start.57 = (bf16[1,2,80,768]{3,2,1,0:T(8,128)(2,1)S(1)}, bf16[1,2,80,768]{3,2,1,0:T(8,128)(2,1)S(1)}, u32[]{:S(2)}, u32[]{:S(2)}) collective-permute-start(bf16[1,2,80,768]{3,2,1,0:T(8,128)(2,1)S(1)} %constant_dynamic-slice_fusion.3), channel_id=1, source_target_pairs={{0,8},{4,12},{8,0},{12,4},{16,24},{20,28},{24,16},{28,20},{1,9},{5... | collective-permute-start | bytes 737288 | tf_op jit(solution)/shard_map/ppermute | solution.py:27
  685.2 8.2 %collective-permute-done.57 = bf16[1,2,80,768]{3,2,1,0:T(8,128)(2,1)S(1)} collective-permute-done((bf16[1,2,80,768]{3,2,1,0:T(8,128)(2,1)S(1)}, bf16[1,2,80,768]{3,2,1,0:T(8,128)(2,1)S(1)}, u32[]{:S(2)}, u32[]{:S(2)}) %collective-permute-start.57) | collective-permute-done | bytes 245792 | tf_op jit(solution)/shard_map/ppermute | solution.py:27
  710.5 6.4 collective-permute-done.58
  (364 shorter events, 243.6 us)
Async XLA Ops:
  7.2 325.1 %all-gather.2.cloned.1.call-start = ((), (), s32[]{:S(2)}) async-start(), calls=%async_computation.2 | async-start | bytes 4718592 | tf_op jit(solution)/shard_map/all_gather | solution.py:911
  11.0 45.0 %collective-permute-start = (bf16[192,2048]{1,0:T(8,128)(2,1)}, bf16[192,2048]{1,0:T(8,128)(2,1)}, u32[]{:S(2)}, u32[]{:S(2)}) collective-permute-start(bf16[192,2048]{1,0:T(8,128)(2,1)} %pad_maximum_fusion.1.refs_10_), channel_id=1, source_target_pairs={{0,4},{8,0},{16,8},{24,16},{28,24},{20,28},{12,20},{4,12},{1,5},{9... | collective-permute-start | bytes 2359304 | tf_op jit(solution)/shard_map/ppermute | solution.py:135
  11.0 45.0 %collective-permute-start.1 = (bf16[192,2048]{1,0:T(8,128)(2,1)}, bf16[192,2048]{1,0:T(8,128)(2,1)}, u32[]{:S(2)}, u32[]{:S(2)}) collective-permute-start(bf16[192,2048]{1,0:T(8,128)(2,1)} %pad_maximum_fusion.1.refs_10_), channel_id=1, source_target_pairs={{0,8},{8,16},{16,24},{24,28},{28,20},{20,12},{12,4},{4,0},{1,9},{9... | collective-permute-start | bytes 2359304 | tf_op jit(solution)/shard_map/ppermute | solution.py:135
  27.5 53.2 %collective-permute-start.6 = (bf16[1,1,4,64,2304]{4,3,2,1,0:T(8,128)(2,1)}, bf16[1,1,4,64,2304]{4,3,2,1,0:T(8,128)(2,1)}, u32[]{:S(2)}, u32[]{:S(2)}) collective-permute-start(bf16[1,1,4,64,2304]{4,3,2,1,0:T(8,128)(2,1)} %constant_dynamic-slice_fusion.15), channel_id=1, source_target_pairs={{0,16},{4,20},{8,24},{12,28},{16,0},{20,4},{24,8},{28,12},{1,17},{... | collective-permute-start | bytes 3538952 | tf_op jit(solution)/shard_map/ppermute | solution.py:27
  55.9 42.1 %collective-permute-start.3 = (bf16[192,2048]{1,0:T(8,128)(2,1)}, bf16[192,2048]{1,0:T(8,128)(2,1)}, u32[]{:S(2)}, u32[]{:S(2)}) collective-permute-start(bf16[192,2048]{1,0:T(8,128)(2,1)} %collective-permute-done.refs_11_), channel_id=1, source_target_pairs={{0,4},{8,0},{16,8},{24,16},{28,24},{20,28},{12,20},{4,12},{1,5},{9... | collective-permute-start | bytes 2359304 | tf_op jit(solution)/shard_map/ppermute | solution.py:135
  56.0 42.1 %collective-permute-start.4 = (bf16[192,2048]{1,0:T(8,128)(2,1)}, bf16[192,2048]{1,0:T(8,128)(2,1)}, u32[]{:S(2)}, u32[]{:S(2)}) collective-permute-start(bf16[192,2048]{1,0:T(8,128)(2,1)} %collective-permute-done.1.refs_12_), channel_id=1, source_target_pairs={{0,8},{8,16},{16,24},{24,28},{28,20},{20,12},{12,4},{4,0},{1,9},{9... | collective-permute-start | bytes 2359304 | tf_op jit(solution)/shard_map/ppermute | solution.py:135
  59.1 34.6 %collective-permute-start.5 = (bf16[2,1,2,80,768]{4,3,2,1,0:T(8,128)(2,1)S(1)}, bf16[2,1,2,80,768]{4,3,2,1,0:T(8,128)(2,1)S(1)}, u32[]{:S(2)}, u32[]{:S(2)}) collective-permute-start(bf16[2,1,2,80,768]{4,3,2,1,0:T(8,128)(2,1)S(1)} %constant_dynamic-slice_fusion.16), channel_id=1, source_target_pairs={{0,8},{4,12},{8,0},{12,4},{16,24},{20,28},{24,16},{28,20},{1,9},{5... | collective-permute-start | bytes 1474568 | tf_op jit(solution)/shard_map/ppermute | solution.py:27
  100.5 42.8 %collective-permute-start.10 = (bf16[4,1,1,64,2304]{4,3,1,0,2:T(8,128)(2,1)}, bf16[4,1,1,64,2304]{4,3,1,0,2:T(8,128)(2,1)}, u32[]{:S(2)}, u32[]{:S(2)}) collective-permute-start(bf16[4,1,1,64,2304]{4,3,1,0,2:T(8,128)(2,1)} %constant_dynamic-slice_fusion.13), channel_id=1, source_target_pairs={{0,4},{4,0},{8,12},{12,8},{16,20},{20,16},{24,28},{28,24},{1,5},{5... | collective-permute-start | bytes 3538952 | tf_op jit(solution)/shard_map/ppermute | solution.py:27
  104.8 38.5 %collective-permute-start.7 = (bf16[192,2048]{1,0:T(8,128)(2,1)}, bf16[192,2048]{1,0:T(8,128)(2,1)}, u32[]{:S(2)}, u32[]{:S(2)}) collective-permute-start(bf16[192,2048]{1,0:T(8,128)(2,1)} %collective-permute-done.3.refs_13_), channel_id=1, source_target_pairs={{0,4},{8,0},{16,8},{24,16},{28,24},{20,28},{12,20},{4,12},{1,5},{9... | collective-permute-start | bytes 2359304 | tf_op jit(solution)/shard_map/ppermute | solution.py:135
  104.9 38.5 %collective-permute-start.8 = (bf16[192,2048]{1,0:T(8,128)(2,1)}, bf16[192,2048]{1,0:T(8,128)(2,1)}, u32[]{:S(2)}, u32[]{:S(2)}) collective-permute-start(bf16[192,2048]{1,0:T(8,128)(2,1)} %collective-permute-done.4.refs_14_), channel_id=1, source_target_pairs={{0,8},{8,16},{16,24},{24,28},{28,20},{20,12},{12,4},{4,0},{1,9},{9... | collective-permute-start | bytes 2359304 | tf_op jit(solution)/shard_map/ppermute | solution.py:135
  108.8 34.5 %collective-permute-start.9 = (bf16[1,1,4,80,768]{4,3,2,1,0:T(8,128)(2,1)}, bf16[1,1,4,80,768]{4,3,2,1,0:T(8,128)(2,1)}, u32[]{:S(2)}, u32[]{:S(2)}) collective-permute-start(bf16[1,1,4,80,768]{4,3,2,1,0:T(8,128)(2,1)} %constant_dynamic-slice_fusion.14), channel_id=1, source_target_pairs={{0,16},{4,20},{8,24},{12,28},{16,0},{20,4},{24,8},{28,12},{1,17},{... | collective-permute-start | bytes 1474568 | tf_op jit(solution)/shard_map/ppermute | solution.py:27
  171.5 50.1 %collective-permute-start.15 = (bf16[512,2048]{1,0:T(8,128)(2,1)}, bf16[512,2048]{1,0:T(8,128)(2,1)}, u32[]{:S(2)}, u32[]{:S(2)}) collective-permute-start(bf16[512,2048]{1,0:T(8,128)(2,1)} %slice_dynamic-update-slice_fusion.refs_3_), channel_id=1, source_target_pairs={{0,2},{1,3},{2,0},{3,1},{4,6},{5,7},{6,4},{7,5},{8,10},{9,11},{10,... | collective-permute-start | bytes 6291464 | tf_op jit(solution)/shard_map/ppermute | solution.py:27
  174.4 416.7 %reduce-scatter.3.cloned.1.call-start = ((), (), s32[]{:S(2)}) async-start(), calls=%async_computation.3 | async-start | bytes 4718592 | tf_op jit(solution)/shard_map/reduce_scatter | solution.py:952
  175.7 45.8 %collective-permute-start.16 = (bf16[2,1,2,64,2304]{4,3,2,1,0:T(8,128)(2,1)}, bf16[2,1,2,64,2304]{4,3,2,1,0:T(8,128)(2,1)}, u32[]{:S(2)}, u32[]{:S(2)}) collective-permute-start(bf16[2,1,2,64,2304]{4,3,2,1,0:T(8,128)(2,1)} %constant_dynamic-slice_fusion.11), channel_id=1, source_target_pairs={{0,8},{4,12},{8,0},{12,4},{16,24},{20,28},{24,16},{28,20},{1,9},{5... | collective-permute-start | bytes 3538952 | tf_op jit(solution)/shard_map/ppermute | solution.py:27
  181.1 81.3 %collective-permute-start.21 = (bf16[512,2048]{1,0:T(8,128)(2,1)}, bf16[512,2048]{1,0:T(8,128)(2,1)}, u32[]{:S(2)}, u32[]{:S(2)}) collective-permute-start(bf16[512,2048]{1,0:T(8,128)(2,1)} %slice_dynamic-update-slice_fusion.refs_3_), channel_id=1, source_target_pairs={{0,1},{1,0},{2,3},{3,2},{4,5},{5,4},{6,7},{7,6},{8,9},{9,8},{10,11... | collective-permute-start | bytes 6291464 | tf_op jit(solution)/shard_map/ppermute | solution.py:27
  221.5 62.2 %collective-permute-start.22 = (bf16[512,2048]{1,0:T(8,128)(2,1)}, bf16[512,2048]{1,0:T(8,128)(2,1)S(1)}, u32[]{:S(2)}, u32[]{:S(2)}) collective-permute-start(bf16[512,2048]{1,0:T(8,128)(2,1)} %collective-permute-done.15.refs_5_), channel_id=1, source_target_pairs={{0,1},{1,0},{2,3},{3,2},{4,5},{5,4},{6,7},{7,6},{8,9},{9,8},{10,11... | collective-permute-start | bytes 6291464 | tf_op jit(solution)/shard_map/ppermute | solution.py:27
  222.9 75.3 %collective-permute-start.27 = (bf16[8,64,2304]{2,1,0:T(8,128)(2,1)S(1)}, bf16[8,64,2304]{2,1,0:T(8,128)(2,1)}, u32[]{:S(2)}, u32[]{:S(2)}) collective-permute-start(bf16[8,64,2304]{2,1,0:T(8,128)(2,1)S(1)} %bitcast.150), channel_id=1, source_target_pairs={{0,2},{1,3},{2,0},{3,1},{4,6},{5,7},{6,4},{7,5},{8,10},{9,11},{10,... | collective-permute-start | bytes 7077896 | tf_op jit(solution)/shard_map/ppermute | solution.py:27
  223.6 33.6 %collective-permute-start.17 = (bf16[1024,256]{1,0:T(8,128)(2,1)S(1)}, bf16[1024,256]{1,0:T(8,128)(2,1)S(1)}, u32[]{:S(2)}, u32[]{:S(2)}) collective-permute-start(bf16[1024,256]{1,0:T(8,128)(2,1)S(1)} %copy-done.45), channel_id=1, source_target_pairs={{0,8},{8,16},{16,24},{24,28},{28,20},{20,12},{12,4},{4,0},{1,9},{9... | collective-permute-start | bytes 1572872 | tf_op jit(solution)/shard_map/ppermute | solution.py:135
  225.0 34.8 %collective-permute-start.18 = (bf16[1024,256]{1,0:T(8,128)(2,1)S(1)}, bf16[1024,256]{1,0:T(8,128)(2,1)S(1)}, u32[]{:S(2)}, u32[]{:S(2)}) collective-permute-start(bf16[1024,256]{1,0:T(8,128)(2,1)S(1)} %copy-done.45), channel_id=1, source_target_pairs={{0,4},{8,0},{16,8},{24,16},{28,24},{20,28},{12,20},{4,12},{1,5},{9... | collective-permute-start | bytes 1572872 | tf_op jit(solution)/shard_map/ppermute | solution.py:135
  298.2 34.0 %collective-permute-start.26 = (bf16[8,64,2304]{2,1,0:T(8,128)(2,1)S(1)}, bf16[8,64,2304]{2,1,0:T(8,128)(2,1)}, u32[]{:S(2)}, u32[]{:S(2)}) collective-permute-start(bf16[8,64,2304]{2,1,0:T(8,128)(2,1)S(1)} %bitcast.151), channel_id=1, source_target_pairs={{0,1},{1,0},{2,3},{3,2},{4,5},{5,4},{6,7},{7,6},{8,9},{9,8},{10,11... | collective-permute-start | bytes 7077896 | tf_op jit(solution)/shard_map/ppermute | solution.py:27
  427.3 30.5 %collective-permute-start.37 = (bf16[2,8,64,1536]{3,2,1,0:T(8,128)(2,1)}, bf16[2,8,64,1536]{3,2,1,0:T(8,128)(2,1)S(1)}, u32[]{:S(2)}, u32[]{:S(2)}) collective-permute-start(bf16[2,8,64,1536]{3,2,1,0:T(8,128)(2,1)} %get-tuple-element.186), channel_id=1, source_target_pairs={{0,1},{1,0},{2,3},{3,2},{4,5},{5,4},{6,7},{7,6},{8,9},{9,8},{10,11... | collective-permute-start | bytes 9437192 | tf_op jit(solution)/shard_map/ppermute | solution.py:27
  427.4 307.3 %reduce-scatter.5.cloned.1.call-start = ((), (), s32[]{:S(2)}) async-start(), calls=%async_computation.4 | async-start | bytes 2359296 | tf_op jit(solution)/shard_map/reduce_scatter | solution.py:1007
  429.3 28.6 %collective-permute-start.35 = (bf16[1024,256]{1,0:T(8,128)(2,1)S(1)}, bf16[1024,256]{1,0:T(8,128)(2,1)S(1)}, u32[]{:S(2)}, u32[]{:S(2)}) collective-permute-start(bf16[1024,256]{1,0:T(8,128)(2,1)S(1)} %get-tuple-element.265), channel_id=1, source_target_pairs={{0,8},{8,16},{16,24},{24,28},{28,20},{20,12},{12,4},{4,0},{1,9},{9... | collective-permute-start | bytes 1572872 | tf_op jit(solution)/shard_map/ppermute | solution.py:135
  458.8 46.4 %collective-permute-start.39 = (bf16[2,8,64,2048]{3,2,1,0:T(8,128)(2,1)}, bf16[2,8,64,2048]{3,2,1,0:T(8,128)(2,1)}, u32[]{:S(2)}, u32[]{:S(2)}) collective-permute-start(bf16[2,8,64,2048]{3,2,1,0:T(8,128)(2,1)} %get-tuple-element.194), channel_id=1, source_target_pairs={{0,1},{1,0},{2,3},{3,2},{4,5},{5,4},{6,7},{7,6},{8,9},{9,8},{10,11... | collective-permute-start | bytes 12582920 | tf_op jit(solution)/shard_map/ppermute | solution.py:27
  471.2 34.0 %collective-permute-start.38 = (bf16[1024,256]{1,0:T(8,128)(2,1)S(1)}, bf16[1024,256]{1,0:T(8,128)(2,1)S(1)}, u32[]{:S(2)}, u32[]{:S(2)}) collective-permute-start(bf16[1024,256]{1,0:T(8,128)(2,1)S(1)} %fusion.17), channel_id=1, source_target_pairs={{0,8},{8,16},{16,24},{24,28},{28,20},{20,12},{12,4},{4,0},{1,9},{9... | collective-permute-start | bytes 1572872 | tf_op jit(solution)/shard_map/ppermute | solution.py:135
  476.5 56.3 %collective-permute-start.41 = (bf16[8,64,1536]{2,1,0:T(8,128)(2,1)}, bf16[8,64,1536]{2,1,0:T(8,128)(2,1)}, u32[]{:S(2)}, u32[]{:S(2)}) collective-permute-start(bf16[8,64,1536]{2,1,0:T(8,128)(2,1)} %get-tuple-element.252), channel_id=1, source_target_pairs={{0,2},{1,3},{2,0},{3,1},{4,6},{5,7},{6,4},{7,5},{8,10},{9,11},{10,... | collective-permute-start | bytes 4718600 | tf_op jit(solution)/shard_map/ppermute | solution.py:27
  515.7 101.4 %collective-permute-start.50 = (bf16[8,64,2048]{2,1,0:T(8,128)(2,1)}, bf16[8,64,2048]{2,1,0:T(8,128)(2,1)}, u32[]{:S(2)}, u32[]{:S(2)}) collective-permute-start(bf16[8,64,2048]{2,1,0:T(8,128)(2,1)} %get-tuple-element.250), channel_id=1, source_target_pairs={{0,2},{1,3},{2,0},{3,1},{4,6},{5,7},{6,4},{7,5},{8,10},{9,11},{10,... | collective-permute-start | bytes 6291464 | tf_op jit(solution)/shard_map/ppermute | solution.py:27
  535.6 55.3 %collective-permute-start.45 = (bf16[1,1,4,64,1536]{4,3,2,1,0:T(8,128)(2,1)}, bf16[1,1,4,64,1536]{4,3,2,1,0:T(8,128)(2,1)}, u32[]{:S(2)}, u32[]{:S(2)}) collective-permute-start(bf16[1,1,4,64,1536]{4,3,2,1,0:T(8,128)(2,1)} %constant_dynamic-slice_fusion.6), channel_id=1, source_target_pairs={{0,16},{4,20},{8,24},{12,28},{16,0},{20,4},{24,8},{28,12},{1,17},{... | collective-permute-start | bytes 2359304 | tf_op jit(solution)/shard_map/ppermute | solution.py:27
  553.6 37.4 %collective-permute-start.43 = (bf16[128,2048]{1,0:T(8,128)(2,1)}, bf16[128,2048]{1,0:T(8,128)(2,1)}, u32[]{:S(2)}, u32[]{:S(2)}) collective-permute-start(bf16[128,2048]{1,0:T(8,128)(2,1)} %get-tuple-element.263), channel_id=1, source_target_pairs={{0,8},{8,16},{16,24},{24,28},{28,20},{20,12},{12,4},{4,0},{1,9},{9... | collective-permute-start | bytes 1572872 | tf_op jit(solution)/shard_map/ppermute | solution.py:135
  553.6 37.4 %collective-permute-start.44 = (bf16[128,2048]{1,0:T(8,128)(2,1)}, bf16[128,2048]{1,0:T(8,128)(2,1)}, u32[]{:S(2)}, u32[]{:S(2)}) collective-permute-start(bf16[128,2048]{1,0:T(8,128)(2,1)} %get-tuple-element.262), channel_id=1, source_target_pairs={{0,4},{8,0},{16,8},{24,16},{28,24},{20,28},{12,20},{4,12},{1,5},{9... | collective-permute-start | bytes 1572872 | tf_op jit(solution)/shard_map/ppermute | solution.py:135
  556.4 34.5 %collective-permute-start.46 = (bf16[2,1,2,64,768]{4,3,2,1,0:T(8,128)(2,1)}, bf16[2,1,2,64,768]{4,3,2,1,0:T(8,128)(2,1)}, u32[]{:S(2)}, u32[]{:S(2)}) collective-permute-start(bf16[2,1,2,64,768]{4,3,2,1,0:T(8,128)(2,1)} %constant_dynamic-slice_fusion.5), channel_id=1, source_target_pairs={{0,8},{4,12},{8,0},{12,4},{16,24},{20,28},{24,16},{28,20},{1,9},{5... | collective-permute-start | bytes 1179656 | tf_op jit(solution)/shard_map/ppermute | solution.py:27
  654.5 45.6 %collective-permute-start.60 = (bf16[2,1,2,64,1536]{4,3,2,1,0:T(8,128)(2,1)S(1)}, bf16[2,1,2,64,1536]{4,3,2,1,0:T(8,128)(2,1)S(1)}, u32[]{:S(2)}, u32[]{:S(2)}) collective-permute-start(bf16[2,1,2,64,1536]{4,3,2,1,0:T(8,128)(2,1)S(1)} %constant_dynamic-slice_fusion), channel_id=1, source_target_pairs={{0,8},{4,12},{8,0},{12,4},{16,24},{20,28},{24,16},{28,20},{1,9},{5... | collective-permute-start | bytes 2359304 | tf_op jit(solution)/shard_map/ppermute | solution.py:27
  (86 other events, 1276.7 us)
Sparse Core Ops, SparseCore 0:
  174.5 109.9 all-gather.1
  427.6 129.6 reduce-scatter.2
  630.3 83.4 reduce-scatter.4

commit v3 on v2

--- a/solution.py
+++ b/solution.py
@@ -18,6 +18,7 @@
 THETA_BASE = 10000.0
 NEGATIVE = -1e30
 VMEM_BYTES = 56 * 1024 * 1024
+GRAD_BLOCKS = 2
 
 bf16 = jnp.bfloat16
 f32 = jnp.float32
@@ -57,19 +58,18 @@
 
 
 def exchange_far(blocks, number):
-    if number != 8:
-        for bit in bits_of(number)[1:]:
-            blocks = exchange(blocks, number, bit)
-        return blocks
+    for bit in bits_of(number)[1:]:
+        blocks = exchange(blocks, number, bit)
+    return blocks
+
+
+def exchange_parts(blocks):
     place = lax.axis_index("seq") // 2
-    out = blocks.reshape((4, 2) + blocks.shape[1:])
-    parts = [
-        swap(lax.dynamic_slice_in_dim(out, place ^ k, 1, 0), "seq", number, k * 2)
+    pairs = blocks.reshape((4, 2) + blocks.shape[1:])
+    return [
+        swap(lax.dynamic_slice_in_dim(pairs, place ^ k, 1, 0), "seq", 8, k * 2)[0]
         for k in range(1, 4)
     ]
-    for k, part in enumerate(parts):
-        out = lax.dynamic_update_slice_in_dim(out, part, place ^ (k + 1), 0)
-    return out.reshape(blocks.shape)
 
 
 def rest_of_exchange(blocks, number):
@@ -407,6 +407,11 @@
     return center * inverse_std, inverse_std
 
 
+def unit_of_centered(center):
+    inverse_std = lax.rsqrt(mean_of(center * center) + EPSILON)
+    return center * inverse_std, inverse_std
+
+
 def norm_back(incoming, unit_rows, inverse_std, gain_values):
     inner = incoming * gain_values
     return inverse_std * (inner - mean_of(inner) - unit_rows * mean_of(inner * unit_rows))
@@ -517,7 +522,7 @@
     many = block // local
     center = all_ref[pl.ds(pl.program_id(0) * many, many)].reshape(block, width)
     center_ref[...] = center
-    unit, _ = unit_of(center.astype(f32))
+    unit, _ = unit_of_centered(center.astype(f32))
     first_input = (unit * gain_ref[...] + shift_ref[...]).astype(bf16)
     input_ref[...] = first_input
     joint = dot(first_input, weight_of(weight_ref, 0, total), ((1,), (0,))) + bias_ref[...]
@@ -628,25 +633,55 @@
 
 
 def feed_kernel(n, *refs):
-    input_ref, grad_ref, unit_ref, inverse_ref, gain_ref, output_ref = refs[:6]
-    pieces = refs[6 : 6 + n]
-    hidden_ref, grads_ref, result_ref, back_ref, through_ref, sums_ref = refs[6 + n : 12 + n]
-    weight_ref, sems = refs[12 + n :]
+    input_ref = refs[0]
+    pieces = refs[1 : 1 + n]
+    gate_ref, upper_ref, hidden_ref, result_ref, weight_ref, sems = refs[1 + n :]
     load_pieces(pieces, weight_ref, sems)
     size = hidden_ref.shape[1]
     second_input = input_ref[...]
     gate = dot(second_input, weight_of(weight_ref, 0, size), ((1,), (0,)))
     upper = dot(second_input, weight_of(weight_ref, size, size), ((1,), (0,)))
+    gate_ref[...] = gate
+    upper_ref[...] = upper
+    hidden = (gate * jax.nn.sigmoid(gate) * upper).astype(bf16)
+    hidden_ref[...] = hidden
+    result_ref[...] = dot(hidden, weight_of(weight_ref, 2 * size, size), ((1,), (1,))).astype(bf16)
+
+
+def feed(second_input, pieces, rows):
+    length, width = second_input.shape
+    size = pieces[0].shape[2] // 3
+    n = len(pieces)
+    return call_kernel(
+        lambda *refs: feed_kernel(n, *refs),
+        length,
+        [block_spec(block_of(length), width)] + any_specs(n),
+        [rows_out(length, size, f32)] * 2
+        + [rows_out(length, size, bf16), rows_out(length, width, bf16)],
+        [
+            pltpu.VMEM((pieces[0].shape[0], n, rows, 3 * size), bf16),
+            pltpu.SemaphoreType.DMA((n,)),
+        ],
+        (second_input, *pieces),
+        "feed",
+        6 * length * width * size,
+    )
+
+
+def feed_back_kernel(n, *refs):
+    gate_ref, upper_ref, grad_ref, unit_ref, inverse_ref, gain_ref, output_ref = refs[:7]
+    pieces = refs[7 : 7 + n]
+    grads_ref, back_ref, through_ref, sums_ref, weight_ref, sems = refs[7 + n :]
+    load_pieces(pieces, weight_ref, sems)
+    size = gate_ref.shape[1]
+    gate = gate_ref[...]
+    upper = upper_ref[...]
     hidden_grad = dot(grad_ref[...], weight_of(weight_ref, 2 * size, size), ((1,), (0,)))
     sigmoid = jax.nn.sigmoid(gate)
-    activated = gate * sigmoid
-    hidden = (activated * upper).astype(bf16)
-    hidden_ref[...] = hidden
     gate_grad = (hidden_grad * upper * sigmoid * (1.0 + gate * (1.0 - sigmoid))).astype(bf16)
     grads_ref[:, :size] = gate_grad
-    up_grad = (hidden_grad * activated).astype(bf16)
+    up_grad = (hidden_grad * (gate * sigmoid)).astype(bf16)
     grads_ref[:, size:] = up_grad
-    result_ref[...] = dot(hidden, weight_of(weight_ref, 2 * size, size), ((1,), (1,))).astype(bf16)
     second = dot(gate_grad, weight_of(weight_ref, 0, size), ((1,), (1,)))
     second += dot(up_grad, weight_of(weight_ref, size, size), ((1,), (1,)))
     unit = unit_ref[...].astype(f32)
@@ -659,20 +694,29 @@
         through_ref[i] = through[:, i * columns : (i + 1) * columns]
 
 
-def feed(second_input, down_grad, unit, inverse, gain, output_all, pieces, rows, n_seq):
-    length, width = second_input.shape
-    size = pieces[0].shape[2] // 3
+def feed_back(gate, upper, down_grad, unit, inverse, gain, output_all, pieces, rows, n_seq):
+    length, width = down_grad.shape
+    size = gate.shape[1]
     n = len(pieces)
     block = block_of(length)
+    half = block_spec(block, size)
     full = block_spec(block, width)
     return call_kernel(
-        lambda *refs: feed_kernel(n, *refs),
+        lambda *refs: feed_back_kernel(n, *refs),
         length,
-        [full, full, full, block_spec(block, 128), whole_spec(1, width), once_spec(width, width)]
+        [
+            half,
+            half,
+            full,
+            full,
+            block_spec(block, 128),
+            whole_spec(1, width),
+            once_spec(width, width),
+        ]
         + any_specs(n),
-        [rows_out(length, size, bf16), rows_out(length, 2 * size, bf16)]
-        + [rows_out(length, width, bf16)] * 2
-        + [
+        [
+            rows_out(length, 2 * size, bf16),
+            rows_out(length, width, bf16),
             (
                 jax.ShapeDtypeStruct((n_seq, length, width // n_seq), bf16),
                 pl.BlockSpec((n_seq, block, width // n_seq), lambda i: (0, i, 0)),
@@ -683,9 +727,9 @@
             pltpu.VMEM((pieces[0].shape[0], n, rows, 3 * size), bf16),
             pltpu.SemaphoreType.DMA((n,)),
         ],
-        (second_input, down_grad, unit, inverse, gain, output_all, *pieces),
-        "feed",
-        12 * length * width * size + 2 * length * width * width,
+        (gate, upper, down_grad, unit, inverse, gain, output_all, *pieces),
+        "feed_back",
+        6 * length * width * size + 2 * length * width * width,
     )
 
 
@@ -696,7 +740,7 @@
     load_pieces(pieces, weight_ref, sems)
     grad = grad_ref[...]
     first = dot(grad, weight_of(weight_ref, 0, grad.shape[1]), ((1,), (1,)))
-    unit, inverse = unit_of(center_ref[...].astype(f32))
+    unit, inverse = unit_of_centered(center_ref[...].astype(f32))
     add_sums(sums_ref, first * unit, first)
     add_sums(bias_ref, grad.astype(f32))
     both = back_ref[...].astype(f32) + norm_back(first, unit, inverse, gain_ref[...])
@@ -741,9 +785,10 @@
     for far in range(2):
         for near, ref in enumerate((keep_ref, send_ref)):
             batch_at = me ^ (2 * far + near)
-            ref[far, 0, :rows] = part_ref[batch_at]
-            if has_below:
-                ref[far, 0, rows:] = below_ref[0, batch_at]
+            for i in range(part_ref.shape[0]):
+                ref[far, i, :rows] = part_ref[i, batch_at]
+                if has_below:
+                    ref[far, i, rows:] = below_ref[i, batch_at]
 
 
 def weight_grad(left, right, n_seq, n_batch, rest=None, below=None):
@@ -760,7 +805,8 @@
             part = jnp.concatenate([part, below], axis=2)
         return part, None
     args = [left, right]
-    specs = [pl.BlockSpec((length, width // n_seq), lambda i: (0, i)), once_spec(length, c)]
+    many = GRAD_BLOCKS
+    specs = [pl.BlockSpec((length, many * width // n_seq), lambda i: (0, i)), once_spec(length, c)]
     high = rows
     if rest is not None:
         args.append(rest)
@@ -768,16 +814,16 @@
     if below is not None:
         high += below.shape[2]
         args.append(below)
-        specs.append(pl.BlockSpec((1,) + below.shape[1:], lambda i: (i, 0, 0, 0)))
+        specs.append(pl.BlockSpec((many,) + below.shape[1:], lambda i: (i, 0, 0, 0)))
     shape = jax.ShapeDtypeStruct((2, n_seq, high, c), bf16)
-    spec = pl.BlockSpec((2, 1, high, c), lambda i: (0, i, 0, 0))
+    spec = pl.BlockSpec((2, many, high, c), lambda i: (0, i, 0, 0))
     return pl.pallas_call(
         lambda *refs: grad_kernel(rows, rest is not None, below is not None, *refs),
-        grid=(n_seq,),
+        grid=(n_seq // many,),
         in_specs=specs,
         out_specs=[spec, spec],
         out_shape=[shape, shape],
-        scratch_shapes=[pltpu.VMEM((n_batch, rows, c), bf16)],
+        scratch_shapes=[pltpu.VMEM((many, n_batch, rows, c), bf16)],
         compiler_params=pltpu.CompilerParams(
             vmem_limit_bytes=VMEM_BYTES, dimension_semantics=("arbitrary",)
         ),
@@ -788,6 +834,41 @@
         ),
         name="weight_grad",
     )(*args)
+
+
+def unpack_kernel(blocks_ref, *refs):
+    parts, (out_ref, vectors_ref) = refs[:3], refs[3:]
+    rows = out_ref.shape[0]
+    width = out_ref.shape[1] // 3
+    columns = blocks_ref.shape[2] // 3
+    place = lax.axis_index("seq") // 2
+    total = jnp.zeros(vectors_ref.shape, f32)
+    for k in range(4):
+        far = place ^ k
+        for near in range(2):
+            at = far * 2 + near
+            block = (blocks_ref[at] if k == 0 else parts[k - 1][near]).astype(f32)
+            for i in range(3):
+                span = pl.ds(pl.multiple_of(i * width + at * columns, columns), columns)
+                out_ref[:, span] = block[:rows, i * columns : (i + 1) * columns]
+            total += block[rows : rows + 8]
+    vectors_ref[...] = total
+
+
+def unpack_joint(blocks, parts, rows):
+    n_seq, _, total = blocks.shape
+    return pl.pallas_call(
+        unpack_kernel,
+        out_shape=(
+            jax.ShapeDtypeStruct((rows, n_seq * total), f32),
+            jax.ShapeDtypeStruct((8, total), f32),
+        ),
+        compiler_params=pltpu.CompilerParams(vmem_limit_bytes=VMEM_BYTES),
+        cost_estimate=pl.CostEstimate(
+            flops=n_seq * rows * total, bytes_accessed=6 * n_seq * rows * total, transcendentals=0
+        ),
+        name="unpack_joint",
+    )(blocks, *parts)
 
 
 def grad_near(halves, n_batch):
@@ -844,6 +925,10 @@
         center_own = values - mean_of(values)
         ring = Gather(jnp.concatenate([center_own.astype(bf16), output_weight]), n_seq)
 
+        chosen = language[:, None] == jnp.arange(LANGS, dtype=jnp.int32)[None, :]
+        row_scale = jnp.sum(jnp.where(chosen, language_weight[None, :], 0.0), axis=1)
+        cotangent = output_grad[0] * row_scale[:, None]
+
         small = jnp.concatenate(
             [attention_gain, attention_shift, feedfwd_gain, feedfwd_shift, joint_bias]
         )
@@ -867,7 +952,8 @@
         blocks = exchange_end(flight, n_seq, 1)
         ring.step()
         flight = exchange_begin(blocks, n_seq, 2)
-        flight, ff_flight = ring.tie(flight, ff_flight)
+        flight, ff_flight, down_grad = ring.tie(flight, ff_flight, cotangent.astype(bf16))
+        down_grad = lax.all_gather(down_grad, "seq", axis=0, tiled=True)
         blocks = exchange_end(flight, n_seq, 2)
         ff_blocks = rest_of_exchange(exchange_end(ff_flight, n_seq, 4), n_seq)
         ring.step()
@@ -904,12 +990,6 @@
         bias_all = small_part(4 * piece, 3 * piece).reshape(3, n_seq, columns)
         bias = lax.dynamic_slice_in_dim(bias_all, seq_at, 1, 1).reshape(1, 3 * columns)
 
-        chosen = language[:, None] == jnp.arange(LANGS, dtype=jnp.int32)[None, :]
-        row_scale = jnp.sum(jnp.where(chosen, language_weight[None, :], 0.0), axis=1)
-        cotangent = output_grad[0] * row_scale[:, None]
-        down_grad = after(cotangent.astype(bf16), pieces[0])
-        down_grad = lax.all_gather(down_grad, "seq", axis=0, tiled=True)
-
         low, first_input, center = make_heads(
             center_pieces, gain_one, shift_one, bias, tables, pieces, rows, local
         )
@@ -938,8 +1018,10 @@
         )
         output_all = output_all.reshape(width, width)
 
-        hidden, middle_grads, result_part, back, through, second_sums = feed(
-            second_input,
+        gate, upper, hidden, result_part = feed(second_input, ff_pieces, rows)
+        middle_grads, back, through, second_sums = feed_back(
+            gate,
+            upper,
             down_grad,
             unit_two,
             inverse_two,
@@ -956,33 +1038,35 @@
 
         ring = Scatter(lambda at: lax.dynamic_index_in_dim(through, at, 0, False), n_seq)
         ring.step()
-        grad_down = grad_near(weight_grad(down_grad, hidden, n_seq, n_batch), n_batch)
+        grad_down = weight_grad(down_grad, hidden, n_seq, n_batch)
         (grad_down,) = ring.tie(grad_down)
         ring.step()
-        grad_down = grad_far_begin(grad_down, n_batch)
+        grad_down = grad_near(grad_down, n_batch)
         grad_both = weight_grad(second_input, middle_grads, n_seq, n_batch)
         grad_both, grad_down = ring.tie(grad_both, grad_down)
         ring.step()
         grad_both = grad_near(grad_both, n_batch)
-        grad_down = exchange_begin(grad_far_end(grad_down), n_seq, 4)
+        grad_down = grad_far_begin(grad_down, n_batch)
         grad_output = weight_grad(
             mixed_all, back, n_seq, n_batch, rest=cotangent.astype(bf16)
         )
-        grad_both, grad_output = ring.tie(grad_both, grad_output)
+        grad_both, grad_output, grad_down, result_sum = ring.tie(
+            grad_both, grad_output, grad_down, result_sum
+        )
         ring.step()
         grad_both = grad_far_begin(grad_both, n_batch)
         grad_output = grad_near(grad_output, n_batch)
+        grad_down = exchange_begin(grad_far_end(grad_down), n_seq, 4)
         heads_weight = lax.dynamic_slice_in_dim(output_all, seq_at * columns, columns, 0)
         from_cot = dot(down_grad, heads_weight, ((1,), (1,)))
-        from_cot, grad_output, grad_down = ring.tie(from_cot, grad_output, grad_down)
+        from_cot, grad_output = ring.tie(from_cot, grad_output)
         context_grad = (ring.total() + from_cot).astype(bf16)
-        grad_down = rest_of_exchange(exchange_end(grad_down, n_seq, 4), n_seq)
-        grad_down = exchange_begin(grad_down, n_seq, 1)
         joint_grad = attend_back(low, context_grad, context, lse, tables)
         joint_grad, grad_both, grad_down = tie(joint_grad, grad_both, grad_down)
         grad_output = grad_far_begin(grad_output, n_batch)
         grad_both = exchange_begin(grad_far_end(grad_both), n_seq, 4)
-        grad_down = exchange_begin(exchange_end(grad_down, n_seq, 1), n_seq, 2)
+        grad_down = rest_of_exchange(exchange_end(grad_down, n_seq, 4), n_seq)
+        grad_down = exchange_begin(grad_down, n_seq, 1)
         both, first_sums, bias_sums = first_back(joint_grad, center, gain_one, back, pieces, rows)
 
         ring = Scatter(lambda at: lax.dynamic_slice_in_dim(both, at * local, local, 0), n_seq)
@@ -995,26 +1079,31 @@
         vectors = jnp.concatenate(vectors, axis=3)
         vectors = jnp.pad(vectors, ((0, 0), (0, 0), (0, 15), (0, 3 * columns - 7 * piece)))
         grad_joint = weight_grad(first_input, joint_grad, n_seq, n_batch, below=vectors)
-        grad_joint, grad_both, grad_down = ring.tie(grad_joint, grad_both, grad_down)
+        grad_joint, grad_down, grad_both = ring.tie(grad_joint, grad_down, grad_both)
         ring.step()
         grad_joint = grad_near(grad_joint, n_batch)
         grad_both = rest_of_exchange(exchange_end(grad_both, n_seq, 4), n_seq)
         grad_both = exchange_begin(grad_both, n_seq, 1)
-        grad_down = exchange_end(grad_down, n_seq, 2)
+        grad_joint, grad_output = ring.tie(grad_joint, grad_output)
+        grad_output = lax.psum_scatter(
+            grad_far_end(grad_output), "seq", scatter_dimension=0, tiled=False
+        )
+        ring.step()
+        grad_joint = grad_far_begin(grad_joint, n_batch)
+        grad_down = exchange_begin(exchange_end(grad_down, n_seq, 1), n_seq, 2)
         projected_own = dot(own(mixed_all), output_all, ((1,), (0,)))
         result = values + projected_own + result_sum.astype(f32)
-        grad_joint, grad_output, result = ring.tie(grad_joint, grad_output, result)
-        grad_output = lax.psum_scatter(
-            grad_far_end(grad_output), "seq", scatter_dimension=0, tiled=False
-        )
-        ring.step()
-        grad_joint = grad_far_begin(grad_joint, n_batch)
-        grad_joint, grad_both = ring.tie(grad_joint, grad_both)
+        grad_joint, grad_both, grad_down, result = ring.tie(
+            grad_joint, grad_both, grad_down, result
+        )
+        grad_down = exchange_end(grad_down, n_seq, 2)
         ring.step()
         grad_joint = exchange_begin(grad_far_end(grad_joint), n_seq, 1)
         grad_both = exchange_begin(exchange_end(grad_both, n_seq, 1), n_seq, 2)
         (grad_joint,) = ring.tie(grad_joint)
-        grad_joint = exchange_far(exchange_end(grad_joint, n_seq, 1), n_seq)
+        grad_joint = exchange_end(grad_joint, n_seq, 1)
+        if n_seq == 8:
+            parts = exchange_parts(grad_joint)
         grad_both = exchange_end(grad_both, n_seq, 2)
         token_grad = cotangent + ring.total()
         grad_output = grad_output.astype(f32)
@@ -1026,10 +1115,16 @@
         grad_gate = unsplit(grad_both[:, :, :ff_local])
         grad_up = unsplit(grad_both[:, :, ff_local:])
         grad_down = unsplit(grad_down)
-        grad_joint = grad_joint.astype(f32)
-        vectors = jnp.sum(grad_joint[:, rows], axis=0)
-        grad_joint = grad_joint[:, :rows].reshape(n_seq, rows, 3, columns)
-        grad_joint = jnp.transpose(grad_joint, (1, 2, 0, 3)).reshape(rows, 3 * width)
+        if n_seq == 8:
+            done = tie(*parts, grad_gate, grad_up, grad_down, token_grad)
+            parts, (grad_gate, grad_up, grad_down, token_grad) = done[:3], done[3:]
+            grad_joint, vectors = unpack_joint(grad_joint, parts, rows)
+            vectors = vectors[0]
+        else:
+            grad_joint = exchange_far(grad_joint, n_seq).astype(f32)
+            vectors = jnp.sum(grad_joint[:, rows], axis=0)
+            grad_joint = grad_joint[:, :rows].reshape(n_seq, rows, 3, columns)
+            grad_joint = jnp.transpose(grad_joint, (1, 2, 0, 3)).reshape(rows, 3 * width)
         return (
             result[None],
             token_grad[None],

time: 751 us -> 692 us (0.921)
  waiting for transfers between devices: 334 us -> 276 us
    ppermute x28, waiting for transfers between devices: 177 us -> 143 us  [ring_step(): lax.ppermute(value, 'seq', [(RING[i], RING[(i + way) % 8]) for i in range...]
    ppermute x33, waiting for transfers between devices: 157 us -> 133 us  [swap(): return lax.ppermute(value, axis, [(i, i ^ bit) for i in range(number)])]
    pallas_call x4 -> x5, Pallas kernels: 91.8 us -> 99.8 us  [call_kernel(): pl.pallas_call(kernel, grid=(length // block,), in_specs=in_specs, out_sp...]
    unnamed x127 -> x119, local copies, waits for them, and re-layouts: 23.6 us -> 19.4 us
  transfers between devices with their start and end apart: 64 -> 64, of which waited for: 31 -> 31; matrix products, arithmetic and copies ran while one was open for 18% -> 19% of each run, Pallas kernels for 15% -> 24%
where the time goes in v3:
time: 692 us; the launch traced here: 685 us
  waiting for transfers between devices  276 us (40%)
  Pallas kernels  167 us (24%)
  starting transfers between devices  80.9 us (12%)
  local copies, waits for them, and re-layouts  74.3 us (11%)
  other arithmetic  59.6 us (9%)
  between operations  15.7 us (2%)
  matrix products  10.9 us (2%)
    ppermute x28, waiting for transfers between devices, ring_step(): lax.ppermute(value, 'seq', [(RING[i], RING[(i + way) % 8]) for i in range...  143 us
    ppermute x33, waiting for transfers between devices, swap(): return lax.ppermute(value, axis, [(i, i ^ bit) for i in range(number)])  133 us
    pallas_call x5, Pallas kernels, call_kernel(): pl.pallas_call(kernel, grid=(length // block,), in_specs=in_specs, out_sp...  99.8 us
    pallas_call x4, Pallas kernels, weight_grad(): pl.pallas_call(lambda *refs: grad_kernel(rows, rest is not None, below is...  43 us
    ppermute x33, starting transfers between devices, swap(): return lax.ppermute(value, axis, [(i, i ^ bit) for i in range(number)])  40.4 us
    ppermute x28, starting transfers between devices, ring_step(): lax.ppermute(value, 'seq', [(RING[i], RING[(i + way) % 8]) for i in range...  40.4 us
    unnamed x119, local copies, waits for them, and re-layouts  19.4 us
    dynamic_update_slice x13, local copies, waits for them, and re-layouts, exchange_end(): out = lax.dynamic_update_slice_in_dim(pairs, got, 1 - mine, 1)  14.7 us
  transfers between devices with their start and end apart: 64, of which 31 were waited for; matrix products, arithmetic and copies ran while one was open for 19% of the time, Pallas kernels for 24%

profile of v3, /device:TPU:8, one launch (start us, length us, event | category | flops | bytes accessed | tf_op | source)
XLA Modules:
  0.0 684.7 jit_solution(5214148881026808671)
XLA Ops:
  32.0 23.9 %collective-permute-done.refs_11_ = bf16[192,2048]{1,0:T(8,128)(2,1)} collective-permute-done((bf16[192,2048]{1,0:T(8,128)(2,1)}, bf16[192,2048]{1,0:T(8,128)(2,1)}, u32[]{:S(2)}, u32[]{:S(2)}) %collective-permute-start) | collective-permute-done | bytes 786464 | tf_op jit(solution)/shard_map/ppermute | solution.py:135
  63.2 17.5 %collective-permute-done.6 = bf16[1,1,4,64,2304]{4,3,2,1,0:T(8,128)(2,1)} collective-permute-done((bf16[1,1,4,64,2304]{4,3,2,1,0:T(8,128)(2,1)}, bf16[1,1,4,64,2304]{4,3,2,1,0:T(8,128)(2,1)}, u32[]{:S(2)}, u32[]{:S(2)}) %collective-permute-start.6) | collective-permute-done | bytes 1179680 | tf_op jit(solution)/shard_map/ppermute | solution.py:28
  80.7 13.1 %collective-permute-done.5 = bf16[2,1,2,80,768]{4,3,2,1,0:T(8,128)(2,1)} collective-permute-done((bf16[2,1,2,80,768]{4,3,2,1,0:T(8,128)(2,1)}, bf16[2,1,2,80,768]{4,3,2,1,0:T(8,128)(2,1)}, u32[]{:S(2)}, u32[]{:S(2)}) %collective-permute-start.5) | collective-permute-done | bytes 491552 | tf_op jit(solution)/shard_map/ppermute | solution.py:28
  109.6 32.1 %collective-permute-done.9 = bf16[1,1,4,80,768]{4,3,2,1,0:T(8,128)(2,1)} collective-permute-done((bf16[1,1,4,80,768]{4,3,2,1,0:T(8,128)(2,1)}, bf16[1,1,4,80,768]{4,3,2,1,0:T(8,128)(2,1)}, u32[]{:S(2)}, u32[]{:S(2)}) %collective-permute-start.9) | collective-permute-done | bytes 491552 | tf_op jit(solution)/shard_map/ppermute | solution.py:28
  150.2 24.7 %collective-permute-done.11.refs_17_ = bf16[192,2048]{1,0:T(8,128)(2,1)S(1)} collective-permute-done((bf16[192,2048]{1,0:T(8,128)(2,1)}, bf16[192,2048]{1,0:T(8,128)(2,1)S(1)}, u32[]{:S(2)}, u32[]{:S(2)}) %collective-permute-start.11) | collective-permute-done | bytes 786464 | tf_op jit(solution)/shard_map/ppermute | solution.py:135
  186.8 10.8 %make_heads.1 = (bf16[1024,768]{1,0:T(8,128)(2,1)}, bf16[1024,2048]{1,0:T(8,128)(2,1)}, bf16[1024,2048]{1,0:T(8,128)(2,1)}) custom-call(f32[1,2048]{1,0:T(1,128)} %reshape.317.refs_0_.refs_2_, f32[1,2048]{1,0:T(1,128)} %reshape.318.refs_1_, f32[1,768]{1,0:T(1,128)} %bitcast.197, f32[1024,128]{1,0:T(8,128)} %constant.288.clone.refs_3_.cos_ref, ...), custom_call_target="tpu_custom_call" | custom-call | flops 3221225472 | bytes 6442450 | tf_op jit(solution)/shard_map/make_heads/pallas_call | solution.py:470
  197.6 8.3 %attend.1 = (f32[1024,256]{1,0:T(8,128)}, bf16[1024,256]{1,0:T(8,128)(2,1)}, f32[1024,128]{1,0:T(8,128)}) custom-call(bf16[1024,768]{1,0:T(8,128)(2,1)} %get-tuple-element.161.low_ref), custom_call_target="tpu_custom_call" | custom-call | flops 2147483648 | bytes 12582912 | tf_op jit(solution)/shard_map/attend/pallas_call | solution.py:302
  205.9 36.4 %collective-permute-done.16 = bf16[2,1,2,64,2304]{4,3,2,1,0:T(8,128)(2,1)} collective-permute-done((bf16[2,1,2,64,2304]{4,3,2,1,0:T(8,128)(2,1)}, bf16[2,1,2,64,2304]{4,3,2,1,0:T(8,128)(2,1)}, u32[]{:S(2)}, u32[]{:S(2)}) %collective-permute-start.16) | collective-permute-done | bytes 1179680 | tf_op jit(solution)/shard_map/ppermute | solution.py:28
  249.8 11.4 %collective-permute-done.17.refs_9_ = bf16[1024,256]{1,0:T(8,128)(2,1)S(1)} collective-permute-done((bf16[1024,256]{1,0:T(8,128)(2,1)S(1)}, bf16[1024,256]{1,0:T(8,128)(2,1)S(1)}, u32[]{:S(2)}, u32[]{:S(2)}) %collective-permute-start.17) | collective-permute-done | bytes 524320 | tf_op jit(solution)/shard_map/ppermute | solution.py:135
  266.2 11.1 %collective-permute-done.19.refs_11_ = bf16[1024,256]{1,0:T(8,128)(2,1)S(1)} collective-permute-done((bf16[1024,256]{1,0:T(8,128)(2,1)S(1)}, bf16[1024,256]{1,0:T(8,128)(2,1)S(1)}, u32[]{:S(2)}, u32[]{:S(2)}) %collective-permute-start.19) | collective-permute-done | bytes 524320 | tf_op jit(solution)/shard_map/ppermute | solution.py:135
  280.6 9.7 %collective-permute-done.23.refs_12_ = bf16[1024,256]{1,0:T(8,128)(2,1)S(1)} collective-permute-done((bf16[1024,256]{1,0:T(8,128)(2,1)S(1)}, bf16[1024,256]{1,0:T(8,128)(2,1)S(1)}, u32[]{:S(2)}, u32[]{:S(2)}) %collective-permute-start.23) | collective-permute-done | bytes 524320 | tf_op jit(solution)/shard_map/ppermute | solution.py:135
  292.6 5.0 collective-permute-done.27.refs_3_.refs_9_
  304.6 20.1 %make_middle.1 = (bf16[1024,2048]{1,0:T(8,128)(2,1)}, bf16[1024,2048]{1,0:T(8,128)(2,1)}, f32[1024,128]{1,0:T(8,128)}, bf16[1024,2048]{1,0:T(8,128)(2,1)}, bf16[8,4,64,2048]{3,2,1,0:T(8,128)(2,1)}) custom-call(bf16[1024,2048]{1,0:T(8,128)(2,1)} %get-tuple-element.162.refs_0_.refs_1_, f32[1,2048]{1,0:T(1,128)} %reshape.320.refs_1_.refs_5_, ...), custom_call_target="tpu_custom_call" | custom-call | flops 8589934592 | bytes 17179868 | tf_op jit(solution)/shard_map/make_middle/pallas_call | solution.py:470
  324.7 16.7 %feed.1 = (f32[1024,768]{1,0:T(8,128)}, f32[1024,768]{1,0:T(8,128)}, bf16[1024,768]{1,0:T(8,128)(2,1)}, bf16[1024,2048]{1,0:T(8,128)(2,1)}) custom-call(bf16[1024,2048]{1,0:T(8,128)(2,1)} %get-tuple-element.178.refs_0_, bf16[8,64,2304]{2,1,0:T(8,128)(2,1)} %bitcast.159, bf16[8,64,2304]{2,1,0:T(8,128)(2,1)} %collective-permute-done.26.refs_2_.refs_8_, ...), custom_call_target="tpu_custom_call" | custom-call | flops 9663676416 | bytes 19327352 | tf_op jit(solution)/shard_map/feed/pallas_call | solution.py:470
  341.6 37.4 %feed_back.1 = (bf16[1024,1536]{1,0:T(8,128)(2,1)}, bf16[1024,2048]{1,0:T(8,128)(2,1)}, bf16[8,1024,256]{2,1,0:T(8,128)(2,1)}, f32[8,2048]{1,0:T(8,128)}) custom-call(f32[1024,768]{1,0:T(8,128)} %get-tuple-element.182.refs_0_, f32[1024,768]{1,0:T(8,128)} %get-tuple-element.183.refs_1_, bf16[1024,2048]{1,0:T(8,128)(2,1)} %all-gather.2.cloned.1.call-done.refs_2_.refs_0_, ...), custom_call_target="tpu_custom_call" | custom-call | flops 18253611008 | bytes 36507224 | tf_op jit(solution)/shard_map/feed_back/pallas_call | solution.py:470
  382.5 7.5 %weight_grad.4 = (bf16[2,8,64,768]{3,2,1,0:T(8,128)(2,1)}, bf16[2,8,64,768]{3,2,1,0:T(8,128)(2,1)}) custom-call(bf16[1024,2048]{1,0:T(8,128)(2,1)} %all-gather.2.cloned.1.call-done.refs_2_.refs_0_, bf16[1024,768]{1,0:T(8,128)(2,1)} %get-tuple-element.189.refs_1_), custom_call_target="tpu_custom_call" | custom-call | flops 3221225472 | bytes 12058624 | tf_op jit(solution)/shard_map/weight_grad/pallas_call | solution.py:820
  397.9 6.4 collective-permute-start.32
  404.4 11.1 %weight_grad.5 = (bf16[2,8,64,1536]{3,2,1,0:T(8,128)(2,1)}, bf16[2,8,64,1536]{3,2,1,0:T(8,128)(2,1)}) custom-call(bf16[1024,2048]{1,0:T(8,128)(2,1)} %get-tuple-element.178.refs_0_, bf16[1024,1536]{1,0:T(8,128)(2,1)} %get-tuple-element.194.refs_1_), custom_call_target="tpu_custom_call" | custom-call | flops 6442450944 | bytes 19922944 | tf_op jit(solution)/shard_map/weight_grad/pallas_call | solution.py:820
  429.9 16.2 %weight_grad.6 = (bf16[2,8,64,2048]{3,2,1,0:T(8,128)(2,1)}, bf16[2,8,64,2048]{3,2,1,0:T(8,128)(2,1)}) custom-call(bf16[1024,2048]{1,0:T(8,128)(2,1)} %get-tuple-element.203.refs_0_, bf16[1024,2048]{1,0:T(8,128)(2,1)} %get-tuple-element.204.refs_1_.refs_3_, bf16[128,2048]{1,0:T(8,128)(2,1)} %bitcast_convert_fusion.refs_2_), custom_call_target="tpu_custom_call" | custom-call | flops 8589934592 | bytes 25165824 | tf_op jit(solution)/shard_map/weight_grad/pallas_call | solution.py:820
  468.3 11.0 %collective-permute-done.38 = bf16[1024,256]{1,0:T(8,128)(2,1)} collective-permute-done((bf16[1024,256]{1,0:T(8,128)(2,1)}, bf16[1024,256]{1,0:T(8,128)(2,1)}, u32[]{:S(2)}, u32[]{:S(2)}) %collective-permute-start.38) | collective-permute-done | bytes 524320 | tf_op jit(solution)/shard_map/ppermute | solution.py:135
  490.9 13.5 %attend_back.1.refs_0_.refs_1_ = bf16[1024,768]{1,0:T(8,128)(2,1)} custom-call(bf16[1024,768]{1,0:T(8,128)(2,1)} %get-tuple-element.161.low_ref, bf16[1024,256]{1,0:T(8,128)(2,1)} %fusion.20.grad_ref, f32[1024,256]{1,0:T(8,128)} %get-tuple-element.217.context_ref, f32[1024,128]{1,0:T(8,128)} %get-tuple-element.218.lse_ref, ...), custom_call_target="tpu_custom_call" | custom-call | flops 5368709120 | bytes 12582912 | tf_op jit(solution)/shard_map/attend_back/pallas_call | solution.py:382
  507.2 14.8 %first_back.1 = (bf16[1024,2048]{1,0:T(8,128)(2,1)}, f32[8,2048]{1,0:T(8,128)}, f32[8,768]{1,0:T(8,128)}) custom-call(bf16[1024,768]{1,0:T(8,128)(2,1)} %attend_back.1.refs_0_.refs_1_, bf16[1024,2048]{1,0:T(8,128)(2,1)} %get-tuple-element.162.refs_0_.refs_1_, f32[1,2048]{1,0:T(1,128)} %reshape.317.refs_0_.refs_2_, ...), custom_call_target="tpu_custom_call" | custom-call | flops 3221225472 | bytes 6442450 | tf_op jit(solution)/shard_map/first_back/pallas_call | solution.py:470
  531.5 8.1 %weight_grad.7 = (bf16[2,8,80,768]{3,2,1,0:T(8,128)(2,1)}, bf16[2,8,80,768]{3,2,1,0:T(8,128)(2,1)}) custom-call(bf16[1024,2048]{1,0:T(8,128)(2,1)} %get-tuple-element.225.refs_0_, bf16[1024,768]{1,0:T(8,128)(2,1)} %attend_back.1.refs_0_.refs_1_, bf16[8,4,16,768]{3,2,1,0:T(8,128)(2,1)} %pad.22.refs_2_), custom_call_target="tpu_custom_call" | custom-call | flops 3221225472 | bytes 12058624 | tf_op jit(solution)/shard_map/weight_grad/pallas_call | solution.py:820
  539.6 9.2 %collective-permute-done.42 = bf16[128,2048]{1,0:T(8,128)(2,1)} collective-permute-done((bf16[128,2048]{1,0:T(8,128)(2,1)}, bf16[128,2048]{1,0:T(8,128)(2,1)}, u32[]{:S(2)}, u32[]{:S(2)}) %collective-permute-start.42) | collective-permute-done | bytes 524320 | tf_op jit(solution)/shard_map/ppermute | solution.py:135
  550.7 6.0 fusion.4
  565.8 7.3 %collective-permute-done.46 = bf16[128,2048]{1,0:T(8,128)(2,1)S(1)} collective-permute-done((bf16[128,2048]{1,0:T(8,128)(2,1)S(1)}, bf16[128,2048]{1,0:T(8,128)(2,1)S(1)}, u32[]{:S(2)}, u32[]{:S(2)}) %collective-permute-start.46) | collective-permute-done | bytes 524320 | tf_op jit(solution)/shard_map/ppermute | solution.py:135
  585.5 6.6 collective-permute-done.53
  593.7 6.3 collective-permute-done.52
  609.3 7.1 %collective-permute-start.60 = (bf16[2,1,2,64,1536]{4,3,2,1,0:T(8,128)(2,1)}, bf16[2,1,2,64,1536]{4,3,2,1,0:T(8,128)(2,1)}, u32[]{:S(2)}, u32[]{:S(2)}) collective-permute-start(bf16[2,1,2,64,1536]{4,3,2,1,0:T(8,128)(2,1)} %constant_dynamic-slice_fusion), channel_id=1, source_target_pairs={{0,8},{4,12},{8,0},{12,4},{16,24},{20,28},{24,16},{28,20},{1,9},{5... | collective-permute-start | bytes 2359304 | tf_op jit(solution)/shard_map/ppermute | solution.py:28
  622.5 6.3 collective-permute-done.55
  630.9 11.2 %collective-permute-start.57 = (bf16[1,2,80,768]{3,2,1,0:T(8,128)(2,1)}, bf16[1,2,80,768]{3,2,1,0:T(8,128)(2,1)}, u32[]{:S(2)}, u32[]{:S(2)}) collective-permute-start(bf16[1,2,80,768]{3,2,1,0:T(8,128)(2,1)} %get-tuple-element.302), channel_id=1, source_target_pairs={{0,8},{4,12},{8,0},{12,4},{16,24},{20,28},{24,16},{28,20},{1,9},{5... | collective-permute-start | bytes 737288 | tf_op jit(solution)/shard_map/ppermute | solution.py:28
  657.5 13.4 %collective-permute-done.59 = bf16[1,2,80,768]{3,2,1,0:T(8,128)(2,1)} collective-permute-done((bf16[1,2,80,768]{3,2,1,0:T(8,128)(2,1)}, bf16[1,2,80,768]{3,2,1,0:T(8,128)(2,1)}, u32[]{:S(2)}, u32[]{:S(2)}) %collective-permute-start.59) | collective-permute-done | bytes 245792 | tf_op jit(solution)/shard_map/ppermute | solution.py:28
  (351 shorter events, 228.3 us)
Async XLA Ops:
  7.2 334.4 %all-gather.2.cloned.1.call-start = ((), (), s32[]{:S(2)}) async-start(), calls=%async_computation.2 | async-start | bytes 4718592 | tf_op jit(solution)/shard_map/all_gather | solution.py:956
  11.0 45.0 %collective-permute-start = (bf16[192,2048]{1,0:T(8,128)(2,1)}, bf16[192,2048]{1,0:T(8,128)(2,1)}, u32[]{:S(2)}, u32[]{:S(2)}) collective-permute-start(bf16[192,2048]{1,0:T(8,128)(2,1)} %pad_maximum_fusion.1.refs_10_), channel_id=1, source_target_pairs={{0,4},{8,0},{16,8},{24,16},{28,24},{20,28},{12,20},{4,12},{1,5},{9... | collective-permute-start | bytes 2359304 | tf_op jit(solution)/shard_map/ppermute | solution.py:135
  11.0 45.0 %collective-permute-start.1 = (bf16[192,2048]{1,0:T(8,128)(2,1)}, bf16[192,2048]{1,0:T(8,128)(2,1)}, u32[]{:S(2)}, u32[]{:S(2)}) collective-permute-start(bf16[192,2048]{1,0:T(8,128)(2,1)} %pad_maximum_fusion.1.refs_10_), channel_id=1, source_target_pairs={{0,8},{8,16},{16,24},{24,28},{28,20},{20,12},{12,4},{4,0},{1,9},{9... | collective-permute-start | bytes 2359304 | tf_op jit(solution)/shard_map/ppermute | solution.py:135
  27.5 53.2 %collective-permute-start.6 = (bf16[1,1,4,64,2304]{4,3,2,1,0:T(8,128)(2,1)}, bf16[1,1,4,64,2304]{4,3,2,1,0:T(8,128)(2,1)}, u32[]{:S(2)}, u32[]{:S(2)}) collective-permute-start(bf16[1,1,4,64,2304]{4,3,2,1,0:T(8,128)(2,1)} %constant_dynamic-slice_fusion.13), channel_id=1, source_target_pairs={{0,16},{4,20},{8,24},{12,28},{16,0},{20,4},{24,8},{28,12},{1,17},{... | collective-permute-start | bytes 3538952 | tf_op jit(solution)/shard_map/ppermute | solution.py:28
  55.9 42.1 %collective-permute-start.3 = (bf16[192,2048]{1,0:T(8,128)(2,1)}, bf16[192,2048]{1,0:T(8,128)(2,1)}, u32[]{:S(2)}, u32[]{:S(2)}) collective-permute-start(bf16[192,2048]{1,0:T(8,128)(2,1)} %collective-permute-done.refs_11_), channel_id=1, source_target_pairs={{0,4},{8,0},{16,8},{24,16},{28,24},{20,28},{12,20},{4,12},{1,5},{9... | collective-permute-start | bytes 2359304 | tf_op jit(solution)/shard_map/ppermute | solution.py:135
  56.0 42.1 %collective-permute-start.4 = (bf16[192,2048]{1,0:T(8,128)(2,1)}, bf16[192,2048]{1,0:T(8,128)(2,1)}, u32[]{:S(2)}, u32[]{:S(2)}) collective-permute-start(bf16[192,2048]{1,0:T(8,128)(2,1)} %collective-permute-done.1.refs_12_), channel_id=1, source_target_pairs={{0,8},{8,16},{16,24},{24,28},{28,20},{20,12},{12,4},{4,0},{1,9},{9... | collective-permute-start | bytes 2359304 | tf_op jit(solution)/shard_map/ppermute | solution.py:135
  59.9 34.0 %collective-permute-start.5 = (bf16[2,1,2,80,768]{4,3,2,1,0:T(8,128)(2,1)}, bf16[2,1,2,80,768]{4,3,2,1,0:T(8,128)(2,1)}, u32[]{:S(2)}, u32[]{:S(2)}) collective-permute-start(bf16[2,1,2,80,768]{4,3,2,1,0:T(8,128)(2,1)} %constant_dynamic-slice_fusion.14), channel_id=1, source_target_pairs={{0,8},{4,12},{8,0},{12,4},{16,24},{20,28},{24,16},{28,20},{1,9},{5... | collective-permute-start | bytes 1474568 | tf_op jit(solution)/shard_map/ppermute | solution.py:28
  100.5 41.3 %collective-permute-start.10 = (bf16[4,1,1,64,2304]{4,3,1,0,2:T(8,128)(2,1)}, bf16[4,1,1,64,2304]{4,3,1,0,2:T(8,128)(2,1)}, u32[]{:S(2)}, u32[]{:S(2)}) collective-permute-start(bf16[4,1,1,64,2304]{4,3,1,0,2:T(8,128)(2,1)} %constant_dynamic-slice_fusion.11), channel_id=1, source_target_pairs={{0,4},{4,0},{8,12},{12,8},{16,20},{20,16},{24,28},{28,24},{1,5},{5... | collective-permute-start | bytes 3538952 | tf_op jit(solution)/shard_map/ppermute | solution.py:28
  103.3 38.5 %collective-permute-start.7 = (bf16[192,2048]{1,0:T(8,128)(2,1)}, bf16[192,2048]{1,0:T(8,128)(2,1)}, u32[]{:S(2)}, u32[]{:S(2)}) collective-permute-start(bf16[192,2048]{1,0:T(8,128)(2,1)} %collective-permute-done.3.refs_13_), channel_id=1, source_target_pairs={{0,4},{8,0},{16,8},{24,16},{28,24},{20,28},{12,20},{4,12},{1,5},{9... | collective-permute-start | bytes 2359304 | tf_op jit(solution)/shard_map/ppermute | solution.py:135
  103.3 38.5 %collective-permute-start.8 = (bf16[192,2048]{1,0:T(8,128)(2,1)}, bf16[192,2048]{1,0:T(8,128)(2,1)}, u32[]{:S(2)}, u32[]{:S(2)}) collective-permute-start(bf16[192,2048]{1,0:T(8,128)(2,1)} %collective-permute-done.4.refs_14_), channel_id=1, source_target_pairs={{0,8},{8,16},{16,24},{24,28},{28,20},{20,12},{12,4},{4,0},{1,9},{9... | collective-permute-start | bytes 2359304 | tf_op jit(solution)/shard_map/ppermute | solution.py:135
  107.2 34.5 %collective-permute-start.9 = (bf16[1,1,4,80,768]{4,3,2,1,0:T(8,128)(2,1)}, bf16[1,1,4,80,768]{4,3,2,1,0:T(8,128)(2,1)}, u32[]{:S(2)}, u32[]{:S(2)}) collective-permute-start(bf16[1,1,4,80,768]{4,3,2,1,0:T(8,128)(2,1)} %constant_dynamic-slice_fusion.12), channel_id=1, source_target_pairs={{0,16},{4,20},{8,24},{12,28},{16,0},{20,4},{24,8},{28,12},{1,17},{... | collective-permute-start | bytes 1474568 | tf_op jit(solution)/shard_map/ppermute | solution.py:28
  142.9 32.0 %collective-permute-start.13 = (bf16[8,80,768]{2,1,0:T(8,128)(2,1)S(1)}, bf16[8,80,768]{2,1,0:T(8,128)(2,1)}, u32[]{:S(2)}, u32[]{:S(2)}) collective-permute-start(bf16[8,80,768]{2,1,0:T(8,128)(2,1)S(1)} %bitcast.174), channel_id=1, source_target_pairs={{0,2},{1,3},{2,0},{3,1},{4,6},{5,7},{6,4},{7,5},{8,10},{9,11},{10,... | collective-permute-start | bytes 2949128 | tf_op jit(solution)/shard_map/ppermute | solution.py:28
  146.2 300.9 %reduce-scatter.3.cloned.1.call-start = ((), (), s32[]{:S(2)}) async-start(), calls=%async_computation.3 | async-start | bytes 4718592 | tf_op jit(solution)/shard_map/reduce_scatter | solution.py:1034
  146.2 28.6 %collective-permute-start.11 = (bf16[192,2048]{1,0:T(8,128)(2,1)}, bf16[192,2048]{1,0:T(8,128)(2,1)S(1)}, u32[]{:S(2)}, u32[]{:S(2)}) collective-permute-start(bf16[192,2048]{1,0:T(8,128)(2,1)} %collective-permute-done.8.refs_16_), channel_id=1, source_target_pairs={{0,8},{8,16},{16,24},{24,28},{28,20},{20,12},{12,4},{4,0},{1,9},{9... | collective-permute-start | bytes 2359304 | tf_op jit(solution)/shard_map/ppermute | solution.py:135
  150.2 28.9 %collective-permute-start.12 = (bf16[8,80,768]{2,1,0:T(8,128)(2,1)S(1)}, bf16[8,80,768]{2,1,0:T(8,128)(2,1)S(1)}, u32[]{:S(2)}, u32[]{:S(2)}) collective-permute-start(bf16[8,80,768]{2,1,0:T(8,128)(2,1)S(1)} %bitcast.175), channel_id=1, source_target_pairs={{0,1},{1,0},{2,3},{3,2},{4,5},{5,4},{6,7},{7,6},{8,9},{9,8},{10,11... | collective-permute-start | bytes 2949128 | tf_op jit(solution)/shard_map/ppermute | solution.py:28
  179.2 63.2 %collective-permute-start.15 = (bf16[512,2048]{1,0:T(8,128)(2,1)}, bf16[512,2048]{1,0:T(8,128)(2,1)}, u32[]{:S(2)}, u32[]{:S(2)}) collective-permute-start(bf16[512,2048]{1,0:T(8,128)(2,1)} %slice_dynamic-update-slice_fusion.refs_3_), channel_id=1, source_target_pairs={{0,2},{1,3},{2,0},{3,1},{4,6},{5,7},{6,4},{7,5},{8,10},{9,11},{10,... | collective-permute-start | bytes 6291464 | tf_op jit(solution)/shard_map/ppermute | solution.py:28
  182.3 60.0 %collective-permute-start.16 = (bf16[2,1,2,64,2304]{4,3,2,1,0:T(8,128)(2,1)}, bf16[2,1,2,64,2304]{4,3,2,1,0:T(8,128)(2,1)}, u32[]{:S(2)}, u32[]{:S(2)}) collective-permute-start(bf16[2,1,2,64,2304]{4,3,2,1,0:T(8,128)(2,1)} %constant_dynamic-slice_fusion.9), channel_id=1, source_target_pairs={{0,8},{4,12},{8,0},{12,4},{16,24},{20,28},{24,16},{28,20},{1,9},{5... | collective-permute-start | bytes 3538952 | tf_op jit(solution)/shard_map/ppermute | solution.py:28
  183.5 82.6 %collective-permute-start.21 = (bf16[512,2048]{1,0:T(8,128)(2,1)}, bf16[512,2048]{1,0:T(8,128)(2,1)}, u32[]{:S(2)}, u32[]{:S(2)}) collective-permute-start(bf16[512,2048]{1,0:T(8,128)(2,1)} %slice_dynamic-update-slice_fusion.refs_3_), channel_id=1, source_target_pairs={{0,1},{1,0},{2,3},{3,2},{4,5},{5,4},{6,7},{7,6},{8,9},{9,8},{10,11... | collective-permute-start | bytes 6291464 | tf_op jit(solution)/shard_map/ppermute | solution.py:28
  242.4 36.1 %collective-permute-start.22 = (bf16[512,2048]{1,0:T(8,128)(2,1)}, bf16[512,2048]{1,0:T(8,128)(2,1)S(1)}, u32[]{:S(2)}, u32[]{:S(2)}) collective-permute-start(bf16[512,2048]{1,0:T(8,128)(2,1)} %collective-permute-done.15.refs_5_), channel_id=1, source_target_pairs={{0,1},{1,0},{2,3},{3,2},{4,5},{5,4},{6,7},{7,6},{8,9},{9,8},{10,11... | collective-permute-start | bytes 6291464 | tf_op jit(solution)/shard_map/ppermute | solution.py:28
  243.8 53.8 %collective-permute-start.27 = (bf16[8,64,2304]{2,1,0:T(8,128)(2,1)S(1)}, bf16[8,64,2304]{2,1,0:T(8,128)(2,1)}, u32[]{:S(2)}, u32[]{:S(2)}) collective-permute-start(bf16[8,64,2304]{2,1,0:T(8,128)(2,1)S(1)} %bitcast.157), channel_id=1, source_target_pairs={{0,2},{1,3},{2,0},{3,1},{4,6},{5,7},{6,4},{7,5},{8,10},{9,11},{10,... | collective-permute-start | bytes 7077896 | tf_op jit(solution)/shard_map/ppermute | solution.py:28
  292.6 32.2 %collective-permute-start.26 = (bf16[8,64,2304]{2,1,0:T(8,128)(2,1)S(1)}, bf16[8,64,2304]{2,1,0:T(8,128)(2,1)}, u32[]{:S(2)}, u32[]{:S(2)}) collective-permute-start(bf16[8,64,2304]{2,1,0:T(8,128)(2,1)S(1)} %bitcast.158), channel_id=1, source_target_pairs={{0,1},{1,0},{2,3},{3,2},{4,5},{5,4},{6,7},{7,6},{8,9},{9,8},{10,11... | collective-permute-start | bytes 7077896 | tf_op jit(solution)/shard_map/ppermute | solution.py:28
  341.5 334.7 %reduce-scatter.5.cloned.1.call-start = ((), (), s32[]{:S(2)}) async-start(), calls=%async_computation.4 | async-start | bytes 2359296 | tf_op jit(solution)/shard_map/reduce_scatter | solution.py:1088
  395.1 26.4 %collective-permute-start.33 = (bf16[2,8,64,768]{3,2,1,0:T(8,128)(2,1)}, bf16[2,8,64,768]{3,2,1,0:T(8,128)(2,1)S(1)}, u32[]{:S(2)}, u32[]{:S(2)}) collective-permute-start(bf16[2,8,64,768]{3,2,1,0:T(8,128)(2,1)} %get-tuple-element.198), channel_id=1, source_target_pairs={{0,1},{1,0},{2,3},{3,2},{4,5},{5,4},{6,7},{7,6},{8,9},{9,8},{10,11... | collective-permute-start | bytes 4718600 | tf_op jit(solution)/shard_map/ppermute | solution.py:28
  447.1 32.3 %collective-permute-start.39 = (bf16[2,8,64,2048]{3,2,1,0:T(8,128)(2,1)}, bf16[2,8,64,2048]{3,2,1,0:T(8,128)(2,1)}, u32[]{:S(2)}, u32[]{:S(2)}) collective-permute-start(bf16[2,8,64,2048]{3,2,1,0:T(8,128)(2,1)} %get-tuple-element.213), channel_id=1, source_target_pairs={{0,1},{1,0},{2,3},{3,2},{4,5},{5,4},{6,7},{7,6},{8,9},{9,8},{10,11... | collective-permute-start | bytes 12582920 | tf_op jit(solution)/shard_map/ppermute | solution.py:28
  463.4 41.1 %collective-permute-start.40 = (bf16[8,64,1536]{2,1,0:T(8,128)(2,1)}, bf16[8,64,1536]{2,1,0:T(8,128)(2,1)}, u32[]{:S(2)}, u32[]{:S(2)}) collective-permute-start(bf16[8,64,1536]{2,1,0:T(8,128)(2,1)} %get-tuple-element.280), channel_id=1, source_target_pairs={{0,2},{1,3},{2,0},{3,1},{4,6},{5,7},{6,4},{7,5},{8,10},{9,11},{10,... | collective-permute-start | bytes 4718600 | tf_op jit(solution)/shard_map/ppermute | solution.py:28
  466.8 37.7 %collective-permute-start.41 = (bf16[1,1,4,64,768]{4,3,2,1,0:T(8,128)(2,1)S(1)}, bf16[1,1,4,64,768]{4,3,2,1,0:T(8,128)(2,1)S(1)}, u32[]{:S(2)}, u32[]{:S(2)}) collective-permute-start(bf16[1,1,4,64,768]{4,3,2,1,0:T(8,128)(2,1)S(1)} %constant_dynamic-slice_fusion.8), channel_id=1, source_target_pairs={{0,16},{4,20},{8,24},{12,28},{16,0},{20,4},{24,8},{28,12},{1,17},{... | collective-permute-start | bytes 1179656 | tf_op jit(solution)/shard_map/ppermute | solution.py:28
  486.6 86.5 %collective-permute-start.49 = (bf16[8,64,2048]{2,1,0:T(8,128)(2,1)}, bf16[8,64,2048]{2,1,0:T(8,128)(2,1)}, u32[]{:S(2)}, u32[]{:S(2)}) collective-permute-start(bf16[8,64,2048]{2,1,0:T(8,128)(2,1)} %get-tuple-element.278), channel_id=1, source_target_pairs={{0,2},{1,3},{2,0},{3,1},{4,6},{5,7},{6,4},{7,5},{8,10},{9,11},{10,... | collective-permute-start | bytes 6291464 | tf_op jit(solution)/shard_map/ppermute | solution.py:28
  507.2 43.5 %collective-permute-start.45 = (bf16[1,1,4,64,1536]{4,3,2,1,0:T(8,128)(2,1)}, bf16[1,1,4,64,1536]{4,3,2,1,0:T(8,128)(2,1)}, u32[]{:S(2)}, u32[]{:S(2)}) collective-permute-start(bf16[1,1,4,64,1536]{4,3,2,1,0:T(8,128)(2,1)} %constant_dynamic-slice_fusion.4), channel_id=1, source_target_pairs={{0,16},{4,20},{8,24},{12,28},{16,0},{20,4},{24,8},{28,12},{1,17},{... | collective-permute-start | bytes 2359304 | tf_op jit(solution)/shard_map/ppermute | solution.py:28
  524.4 24.4 %collective-permute-start.42 = (bf16[128,2048]{1,0:T(8,128)(2,1)}, bf16[128,2048]{1,0:T(8,128)(2,1)}, u32[]{:S(2)}, u32[]{:S(2)}) collective-permute-start(bf16[128,2048]{1,0:T(8,128)(2,1)} %get-tuple-element.291), channel_id=1, source_target_pairs={{0,8},{8,16},{16,24},{24,28},{28,20},{20,12},{12,4},{4,0},{1,9},{9... | collective-permute-start | bytes 1572872 | tf_op jit(solution)/shard_map/ppermute | solution.py:135
  609.3 37.6 %collective-permute-start.60 = (bf16[2,1,2,64,1536]{4,3,2,1,0:T(8,128)(2,1)}, bf16[2,1,2,64,1536]{4,3,2,1,0:T(8,128)(2,1)}, u32[]{:S(2)}, u32[]{:S(2)}) collective-permute-start(bf16[2,1,2,64,1536]{4,3,2,1,0:T(8,128)(2,1)} %constant_dynamic-slice_fusion), channel_id=1, source_target_pairs={{0,8},{4,12},{8,0},{12,4},{16,24},{20,28},{24,16},{28,20},{1,9},{5... | collective-permute-start | bytes 2359304 | tf_op jit(solution)/shard_map/ppermute | solution.py:28
  630.9 24.5 %collective-permute-start.57 = (bf16[1,2,80,768]{3,2,1,0:T(8,128)(2,1)}, bf16[1,2,80,768]{3,2,1,0:T(8,128)(2,1)}, u32[]{:S(2)}, u32[]{:S(2)}) collective-permute-start(bf16[1,2,80,768]{3,2,1,0:T(8,128)(2,1)} %get-tuple-element.302), channel_id=1, source_target_pairs={{0,8},{4,12},{8,0},{12,4},{16,24},{20,28},{24,16},{28,20},{1,9},{5... | collective-permute-start | bytes 737288 | tf_op jit(solution)/shard_map/ppermute | solution.py:28
  642.1 28.8 %collective-permute-start.59 = (bf16[1,2,80,768]{3,2,1,0:T(8,128)(2,1)}, bf16[1,2,80,768]{3,2,1,0:T(8,128)(2,1)}, u32[]{:S(2)}, u32[]{:S(2)}) collective-permute-start(bf16[1,2,80,768]{3,2,1,0:T(8,128)(2,1)} %get-tuple-element.300), channel_id=1, source_target_pairs={{0,24},{4,28},{8,16},{12,20},{16,8},{20,12},{24,0},{28,4},{1,25},{... | collective-permute-start | bytes 737288 | tf_op jit(solution)/shard_map/ppermute | solution.py:28
  (83 other events, 1112.5 us)
Sparse Core Ops, SparseCore 0:
  146.3 101.0 all-gather.1
  341.6 95.7 reduce-scatter.2
  585.6 83.8 reduce-scatter.4

commit v4 on v3

--- a/solution.py
+++ b/solution.py
@@ -882,16 +882,16 @@
     keep, got = halves
     if got is None:
         return scatter_far(keep, n_batch), None
-    keep, got = keep.astype(f32), got.astype(f32)
-    other = swap((keep[1] + got[1]).astype(bf16), "batch", n_batch, 2)
-    return (keep[0] + got[0]).astype(bf16), other
+    send = (keep[1].astype(f32) + got[1].astype(f32)).astype(bf16)
+    return (keep, got), swap(send, "batch", n_batch, 2)
 
 
 def grad_far_end(state):
-    keep, other = state
+    halves, other = state
     if other is None:
-        return keep
-    return (keep.astype(f32) + other.astype(f32)).astype(bf16)
+        return halves
+    keep, got = halves
+    return (keep[0].astype(f32) + got[0].astype(f32) + other.astype(f32)).astype(bf16)
 
 
 def make_body(n_seq, n_batch):
@@ -1079,15 +1079,17 @@
         vectors = jnp.concatenate(vectors, axis=3)
         vectors = jnp.pad(vectors, ((0, 0), (0, 0), (0, 15), (0, 3 * columns - 7 * piece)))
         grad_joint = weight_grad(first_input, joint_grad, n_seq, n_batch, below=vectors)
-        grad_joint, grad_down, grad_both = ring.tie(grad_joint, grad_down, grad_both)
+        grad_joint, grad_down, grad_both, grad_output = ring.tie(
+            grad_joint, grad_down, grad_both, grad_output
+        )
+        grad_output = lax.psum_scatter(
+            grad_far_end(grad_output), "seq", scatter_dimension=0, tiled=False
+        )
         ring.step()
         grad_joint = grad_near(grad_joint, n_batch)
         grad_both = rest_of_exchange(exchange_end(grad_both, n_seq, 4), n_seq)
         grad_both = exchange_begin(grad_both, n_seq, 1)
-        grad_joint, grad_output = ring.tie(grad_joint, grad_output)
-        grad_output = lax.psum_scatter(
-            grad_far_end(grad_output), "seq", scatter_dimension=0, tiled=False
-        )
+        (grad_joint,) = ring.tie(grad_joint)
         ring.step()
         grad_joint = grad_far_begin(grad_joint, n_batch)
         grad_down = exchange_begin(exchange_end(grad_down, n_seq, 1), n_seq, 2)

time: 692 us -> 688 us (level)
  other arithmetic: 59.6 us -> 52.1 us
  waiting for transfers between devices: 276 us -> 283 us
    ppermute x28, waiting for transfers between devices: 143 us -> 156 us  [ring_step(): lax.ppermute(value, 'seq', [(RING[i], RING[(i + way) % 8]) for i in range...]
    convert_element_type x16 -> x8, other arithmetic: 26.9 us -> 20.5 us  [the longest x4 10.4 us: grad_far_end(): (keep[0].astype(f32) + got[0].astype(f32) + other.astype(f32)).astype(bf16)]
  transfers between devices with their start and end apart: 64 -> 64, of which waited for: 31 -> 32; matrix products, arithmetic and copies ran while one was open for 19% -> 18% of each run, Pallas kernels for 24% -> 25%
where the time goes in v4:
time: 688 us; the launch traced here: 680 us
  waiting for transfers between devices  283 us (41%)
  Pallas kernels  167 us (24%)
  starting transfers between devices  77.6 us (11%)
  local copies, waits for them, and re-layouts  73.4 us (11%)
  other arithmetic  52.1 us (8%)
  between operations  16 us (2%)
  matrix products  10.9 us (2%)
    ppermute x28, waiting for transfers between devices, ring_step(): lax.ppermute(value, 'seq', [(RING[i], RING[(i + way) % 8]) for i in range...  156 us
    ppermute x33, waiting for transfers between devices, swap(): return lax.ppermute(value, axis, [(i, i ^ bit) for i in range(number)])  127 us
    pallas_call x5, Pallas kernels, call_kernel(): pl.pallas_call(kernel, grid=(length // block,), in_specs=in_specs, out_sp...  99.5 us
    pallas_call x4, Pallas kernels, weight_grad(): pl.pallas_call(lambda *refs: grad_kernel(rows, rest is not None, below is...  43.1 us
    ppermute x28, starting transfers between devices, ring_step(): lax.ppermute(value, 'seq', [(RING[i], RING[(i + way) % 8]) for i in range...  40.7 us
    ppermute x33, starting transfers between devices, swap(): return lax.ppermute(value, axis, [(i, i ^ bit) for i in range(number)])  36.9 us
    unnamed x119, local copies, waits for them, and re-layouts  18.5 us
    dynamic_update_slice x13, local copies, waits for them, and re-layouts, exchange_end(): out = lax.dynamic_update_slice_in_dim(pairs, got, 1 - mine, 1)  14.7 us
  transfers between devices with their start and end apart: 64, of which 32 were waited for; matrix products, arithmetic and copies ran while one was open for 18% of the time, Pallas kernels for 25%

profile of v4, /device:TPU:8, one launch (start us, length us, event | category | flops | bytes accessed | tf_op | source)
XLA Modules:
  0.0 680.2 jit_solution(12004497108204081217)
XLA Ops:
  32.0 23.9 %collective-permute-done.refs_11_ = bf16[192,2048]{1,0:T(8,128)(2,1)} collective-permute-done((bf16[192,2048]{1,0:T(8,128)(2,1)}, bf16[192,2048]{1,0:T(8,128)(2,1)}, u32[]{:S(2)}, u32[]{:S(2)}) %collective-permute-start) | collective-permute-done | bytes 786464 | tf_op jit(solution)/shard_map/ppermute | solution.py:135
  63.2 17.5 %collective-permute-done.6 = bf16[1,1,4,64,2304]{4,3,2,1,0:T(8,128)(2,1)} collective-permute-done((bf16[1,1,4,64,2304]{4,3,2,1,0:T(8,128)(2,1)}, bf16[1,1,4,64,2304]{4,3,2,1,0:T(8,128)(2,1)}, u32[]{:S(2)}, u32[]{:S(2)}) %collective-permute-start.6) | collective-permute-done | bytes 1179680 | tf_op jit(solution)/shard_map/ppermute | solution.py:28
  80.7 13.1 %collective-permute-done.5 = bf16[2,1,2,80,768]{4,3,2,1,0:T(8,128)(2,1)} collective-permute-done((bf16[2,1,2,80,768]{4,3,2,1,0:T(8,128)(2,1)}, bf16[2,1,2,80,768]{4,3,2,1,0:T(8,128)(2,1)}, u32[]{:S(2)}, u32[]{:S(2)}) %collective-permute-start.5) | collective-permute-done | bytes 491552 | tf_op jit(solution)/shard_map/ppermute | solution.py:28
  109.7 32.1 %collective-permute-done.9 = bf16[1,1,4,80,768]{4,3,2,1,0:T(8,128)(2,1)} collective-permute-done((bf16[1,1,4,80,768]{4,3,2,1,0:T(8,128)(2,1)}, bf16[1,1,4,80,768]{4,3,2,1,0:T(8,128)(2,1)}, u32[]{:S(2)}, u32[]{:S(2)}) %collective-permute-start.9) | collective-permute-done | bytes 491552 | tf_op jit(solution)/shard_map/ppermute | solution.py:28
  150.1 24.6 %collective-permute-done.11.refs_17_ = bf16[192,2048]{1,0:T(8,128)(2,1)S(1)} collective-permute-done((bf16[192,2048]{1,0:T(8,128)(2,1)}, bf16[192,2048]{1,0:T(8,128)(2,1)S(1)}, u32[]{:S(2)}, u32[]{:S(2)}) %collective-permute-start.11) | collective-permute-done | bytes 786464 | tf_op jit(solution)/shard_map/ppermute | solution.py:135
  186.6 10.8 %make_heads.1 = (bf16[1024,768]{1,0:T(8,128)(2,1)}, bf16[1024,2048]{1,0:T(8,128)(2,1)}, bf16[1024,2048]{1,0:T(8,128)(2,1)}) custom-call(f32[1,2048]{1,0:T(1,128)} %reshape.329.refs_0_.refs_2_, f32[1,2048]{1,0:T(1,128)} %reshape.330.refs_1_, f32[1,768]{1,0:T(1,128)} %bitcast.205, f32[1024,128]{1,0:T(8,128)} %constant.288.clone.refs_3_.cos_ref, ...), custom_call_target="tpu_custom_call" | custom-call | flops 3221225472 | bytes 6442450 | tf_op jit(solution)/shard_map/make_heads/pallas_call | solution.py:470
  197.4 8.4 %attend.1 = (f32[1024,256]{1,0:T(8,128)}, bf16[1024,256]{1,0:T(8,128)(2,1)}, f32[1024,128]{1,0:T(8,128)}) custom-call(bf16[1024,768]{1,0:T(8,128)(2,1)} %get-tuple-element.165.low_ref), custom_call_target="tpu_custom_call" | custom-call | flops 2147483648 | bytes 12582912 | tf_op jit(solution)/shard_map/attend/pallas_call | solution.py:302
  205.7 36.4 %collective-permute-done.16 = bf16[2,1,2,64,2304]{4,3,2,1,0:T(8,128)(2,1)} collective-permute-done((bf16[2,1,2,64,2304]{4,3,2,1,0:T(8,128)(2,1)}, bf16[2,1,2,64,2304]{4,3,2,1,0:T(8,128)(2,1)}, u32[]{:S(2)}, u32[]{:S(2)}) %collective-permute-start.16) | collective-permute-done | bytes 1179680 | tf_op jit(solution)/shard_map/ppermute | solution.py:28
  244.7 4.9 collective-permute-start.17
  249.7 11.4 %collective-permute-done.17.refs_9_ = bf16[1024,256]{1,0:T(8,128)(2,1)S(1)} collective-permute-done((bf16[1024,256]{1,0:T(8,128)(2,1)S(1)}, bf16[1024,256]{1,0:T(8,128)(2,1)S(1)}, u32[]{:S(2)}, u32[]{:S(2)}) %collective-permute-start.17) | collective-permute-done | bytes 524320 | tf_op jit(solution)/shard_map/ppermute | solution.py:135
  266.1 11.1 %collective-permute-done.19.refs_11_ = bf16[1024,256]{1,0:T(8,128)(2,1)S(1)} collective-permute-done((bf16[1024,256]{1,0:T(8,128)(2,1)S(1)}, bf16[1024,256]{1,0:T(8,128)(2,1)S(1)}, u32[]{:S(2)}, u32[]{:S(2)}) %collective-permute-start.19) | collective-permute-done | bytes 524320 | tf_op jit(solution)/shard_map/ppermute | solution.py:135
  280.5 9.7 %collective-permute-done.23.refs_12_ = bf16[1024,256]{1,0:T(8,128)(2,1)S(1)} collective-permute-done((bf16[1024,256]{1,0:T(8,128)(2,1)S(1)}, bf16[1024,256]{1,0:T(8,128)(2,1)S(1)}, u32[]{:S(2)}, u32[]{:S(2)}) %collective-permute-start.23) | collective-permute-done | bytes 524320 | tf_op jit(solution)/shard_map/ppermute | solution.py:135
  304.2 20.1 %make_middle.1 = (bf16[1024,2048]{1,0:T(8,128)(2,1)}, bf16[1024,2048]{1,0:T(8,128)(2,1)}, f32[1024,128]{1,0:T(8,128)}, bf16[1024,2048]{1,0:T(8,128)(2,1)}, bf16[8,4,64,2048]{3,2,1,0:T(8,128)(2,1)}) custom-call(bf16[1024,2048]{1,0:T(8,128)(2,1)} %get-tuple-element.166.refs_0_.refs_1_, f32[1,2048]{1,0:T(1,128)} %reshape.332.refs_1_.refs_5_, ...), custom_call_target="tpu_custom_call" | custom-call | flops 8589934592 | bytes 17179868 | tf_op jit(solution)/shard_map/make_middle/pallas_call | solution.py:470
  324.4 16.7 %feed.1 = (f32[1024,768]{1,0:T(8,128)}, f32[1024,768]{1,0:T(8,128)}, bf16[1024,768]{1,0:T(8,128)(2,1)}, bf16[1024,2048]{1,0:T(8,128)(2,1)}) custom-call(bf16[1024,2048]{1,0:T(8,128)(2,1)} %get-tuple-element.182.refs_0_, bf16[8,64,2304]{2,1,0:T(8,128)(2,1)} %bitcast.167, bf16[8,64,2304]{2,1,0:T(8,128)(2,1)} %collective-permute-done.26.refs_2_.refs_8_, ...), custom_call_target="tpu_custom_call" | custom-call | flops 9663676416 | bytes 19327352 | tf_op jit(solution)/shard_map/feed/pallas_call | solution.py:470
  341.2 37.3 %feed_back.1 = (bf16[1024,1536]{1,0:T(8,128)(2,1)}, bf16[1024,2048]{1,0:T(8,128)(2,1)}, bf16[8,1024,256]{2,1,0:T(8,128)(2,1)}, f32[8,2048]{1,0:T(8,128)}) custom-call(f32[1024,768]{1,0:T(8,128)} %get-tuple-element.186.refs_0_, f32[1024,768]{1,0:T(8,128)} %get-tuple-element.187.refs_1_, bf16[1024,2048]{1,0:T(8,128)(2,1)} %all-gather.2.cloned.1.call-done.refs_2_.refs_0_, ...), custom_call_target="tpu_custom_call" | custom-call | flops 18253611008 | bytes 36507224 | tf_op jit(solution)/shard_map/feed_back/pallas_call | solution.py:470
  382.3 7.5 %weight_grad.4 = (bf16[2,8,64,768]{3,2,1,0:T(8,128)(2,1)}, bf16[2,8,64,768]{3,2,1,0:T(8,128)(2,1)}) custom-call(bf16[1024,2048]{1,0:T(8,128)(2,1)} %all-gather.2.cloned.1.call-done.refs_2_.refs_0_, bf16[1024,768]{1,0:T(8,128)(2,1)} %get-tuple-element.193.refs_1_), custom_call_target="tpu_custom_call" | custom-call | flops 3221225472 | bytes 12058624 | tf_op jit(solution)/shard_map/weight_grad/pallas_call | solution.py:820
  397.6 6.7 collective-permute-start.32
  404.3 11.1 %weight_grad.5 = (bf16[2,8,64,1536]{3,2,1,0:T(8,128)(2,1)}, bf16[2,8,64,1536]{3,2,1,0:T(8,128)(2,1)}) custom-call(bf16[1024,2048]{1,0:T(8,128)(2,1)} %get-tuple-element.182.refs_0_, bf16[1024,1536]{1,0:T(8,128)(2,1)} %get-tuple-element.198.refs_1_), custom_call_target="tpu_custom_call" | custom-call | flops 6442450944 | bytes 19922944 | tf_op jit(solution)/shard_map/weight_grad/pallas_call | solution.py:820
  427.8 16.3 %weight_grad.6 = (bf16[2,8,64,2048]{3,2,1,0:T(8,128)(2,1)}, bf16[2,8,64,2048]{3,2,1,0:T(8,128)(2,1)}) custom-call(bf16[1024,2048]{1,0:T(8,128)(2,1)} %get-tuple-element.207.refs_0_, bf16[1024,2048]{1,0:T(8,128)(2,1)} %get-tuple-element.208.refs_1_.refs_3_, bf16[128,2048]{1,0:T(8,128)(2,1)} %bitcast_convert_fusion.refs_2_), custom_call_target="tpu_custom_call" | custom-call | flops 8589934592 | bytes 25165824 | tf_op jit(solution)/shard_map/weight_grad/pallas_call | solution.py:820
  464.0 13.7 %collective-permute-done.38 = bf16[1024,256]{1,0:T(8,128)(2,1)S(1)} collective-permute-done((bf16[1024,256]{1,0:T(8,128)(2,1)S(1)}, bf16[1024,256]{1,0:T(8,128)(2,1)S(1)}, u32[]{:S(2)}, u32[]{:S(2)}) %collective-permute-start.38) | collective-permute-done | bytes 524320 | tf_op jit(solution)/shard_map/ppermute | solution.py:135
  484.3 13.6 %attend_back.1.refs_0_.refs_1_ = bf16[1024,768]{1,0:T(8,128)(2,1)} custom-call(bf16[1024,768]{1,0:T(8,128)(2,1)} %get-tuple-element.165.low_ref, bf16[1024,256]{1,0:T(8,128)(2,1)} %fusion.14.grad_ref, f32[1024,256]{1,0:T(8,128)} %get-tuple-element.221.context_ref, f32[1024,128]{1,0:T(8,128)} %get-tuple-element.222.lse_ref, ...), custom_call_target="tpu_custom_call" | custom-call | flops 5368709120 | bytes 12582912 | tf_op jit(solution)/shard_map/attend_back/pallas_call | solution.py:382
  500.9 14.6 %first_back.1 = (bf16[1024,2048]{1,0:T(8,128)(2,1)}, f32[8,2048]{1,0:T(8,128)}, f32[8,768]{1,0:T(8,128)}) custom-call(bf16[1024,768]{1,0:T(8,128)(2,1)} %attend_back.1.refs_0_.refs_1_, bf16[1024,2048]{1,0:T(8,128)(2,1)} %get-tuple-element.166.refs_0_.refs_1_, f32[1,2048]{1,0:T(1,128)} %reshape.329.refs_0_.refs_2_, ...), custom_call_target="tpu_custom_call" | custom-call | flops 3221225472 | bytes 6442450 | tf_op jit(solution)/shard_map/first_back/pallas_call | solution.py:470
  525.0 8.2 %weight_grad.7 = (bf16[2,8,80,768]{3,2,1,0:T(8,128)(2,1)}, bf16[2,8,80,768]{3,2,1,0:T(8,128)(2,1)}) custom-call(bf16[1024,2048]{1,0:T(8,128)(2,1)} %get-tuple-element.230.refs_0_, bf16[1024,768]{1,0:T(8,128)(2,1)} %attend_back.1.refs_0_.refs_1_, bf16[8,4,16,768]{3,2,1,0:T(8,128)(2,1)} %pad.22.refs_2_), custom_call_target="tpu_custom_call" | custom-call | flops 3221225472 | bytes 12058624 | tf_op jit(solution)/shard_map/weight_grad/pallas_call | solution.py:820
  533.1 11.4 %collective-permute-done.42 = bf16[128,2048]{1,0:T(8,128)(2,1)} collective-permute-done((bf16[128,2048]{1,0:T(8,128)(2,1)}, bf16[128,2048]{1,0:T(8,128)(2,1)}, u32[]{:S(2)}, u32[]{:S(2)}) %collective-permute-start.42) | collective-permute-done | bytes 524320 | tf_op jit(solution)/shard_map/ppermute | solution.py:135
  545.9 6.0 fusion.2
  561.5 6.8 collective-permute-done.47
  580.3 8.0 %collective-permute-done.50 = bf16[128,2048]{1,0:T(8,128)(2,1)} collective-permute-done((bf16[128,2048]{1,0:T(8,128)(2,1)}, bf16[128,2048]{1,0:T(8,128)(2,1)}, u32[]{:S(2)}, u32[]{:S(2)}) %collective-permute-start.50) | collective-permute-done | bytes 524320 | tf_op jit(solution)/shard_map/ppermute | solution.py:135
  588.3 5.4 collective-permute-done.52
  602.5 7.4 %collective-permute-start.60 = (bf16[2,1,2,64,1536]{4,3,2,1,0:T(8,128)(2,1)}, bf16[2,1,2,64,1536]{4,3,2,1,0:T(8,128)(2,1)}, u32[]{:S(2)}, u32[]{:S(2)}) collective-permute-start(bf16[2,1,2,64,1536]{4,3,2,1,0:T(8,128)(2,1)} %constant_dynamic-slice_fusion), channel_id=1, source_target_pairs={{0,8},{4,12},{8,0},{12,4},{16,24},{20,28},{24,16},{28,20},{1,9},{5... | collective-permute-start | bytes 2359304 | tf_op jit(solution)/shard_map/ppermute | solution.py:28
  616.0 7.0 %collective-permute-done.55 = bf16[128,2048]{1,0:T(8,128)(2,1)} collective-permute-done((bf16[128,2048]{1,0:T(8,128)(2,1)}, bf16[128,2048]{1,0:T(8,128)(2,1)}, u32[]{:S(2)}, u32[]{:S(2)}) %collective-permute-start.55) | collective-permute-done | bytes 524320 | tf_op jit(solution)/shard_map/ppermute | solution.py:135
  625.1 10.5 %collective-permute-start.57 = (bf16[1,2,80,768]{3,2,1,0:T(8,128)(2,1)}, bf16[1,2,80,768]{3,2,1,0:T(8,128)(2,1)}, u32[]{:S(2)}, u32[]{:S(2)}) collective-permute-start(bf16[1,2,80,768]{3,2,1,0:T(8,128)(2,1)} %get-tuple-element.302), channel_id=1, source_target_pairs={{0,8},{4,12},{8,0},{12,4},{16,24},{20,28},{24,16},{28,20},{1,9},{5... | collective-permute-start | bytes 737288 | tf_op jit(solution)/shard_map/ppermute | solution.py:28
  651.4 14.7 %collective-permute-done.59 = bf16[1,2,80,768]{3,2,1,0:T(8,128)(2,1)} collective-permute-done((bf16[1,2,80,768]{3,2,1,0:T(8,128)(2,1)}, bf16[1,2,80,768]{3,2,1,0:T(8,128)(2,1)}, u32[]{:S(2)}, u32[]{:S(2)}) %collective-permute-start.59) | collective-permute-done | bytes 245792 | tf_op jit(solution)/shard_map/ppermute | solution.py:28
  (343 shorter events, 217.2 us)
Async XLA Ops:
  7.2 334.0 %all-gather.2.cloned.1.call-start = ((), (), s32[]{:S(2)}) async-start(), calls=%async_computation.2 | async-start | bytes 4718592 | tf_op jit(solution)/shard_map/all_gather | solution.py:956
  11.0 45.0 %collective-permute-start = (bf16[192,2048]{1,0:T(8,128)(2,1)}, bf16[192,2048]{1,0:T(8,128)(2,1)}, u32[]{:S(2)}, u32[]{:S(2)}) collective-permute-start(bf16[192,2048]{1,0:T(8,128)(2,1)} %pad_maximum_fusion.1.refs_10_), channel_id=1, source_target_pairs={{0,4},{8,0},{16,8},{24,16},{28,24},{20,28},{12,20},{4,12},{1,5},{9... | collective-permute-start | bytes 2359304 | tf_op jit(solution)/shard_map/ppermute | solution.py:135
  11.0 45.0 %collective-permute-start.1 = (bf16[192,2048]{1,0:T(8,128)(2,1)}, bf16[192,2048]{1,0:T(8,128)(2,1)}, u32[]{:S(2)}, u32[]{:S(2)}) collective-permute-start(bf16[192,2048]{1,0:T(8,128)(2,1)} %pad_maximum_fusion.1.refs_10_), channel_id=1, source_target_pairs={{0,8},{8,16},{16,24},{24,28},{28,20},{20,12},{12,4},{4,0},{1,9},{9... | collective-permute-start | bytes 2359304 | tf_op jit(solution)/shard_map/ppermute | solution.py:135
  27.5 53.2 %collective-permute-start.6 = (bf16[1,1,4,64,2304]{4,3,2,1,0:T(8,128)(2,1)}, bf16[1,1,4,64,2304]{4,3,2,1,0:T(8,128)(2,1)}, u32[]{:S(2)}, u32[]{:S(2)}) collective-permute-start(bf16[1,1,4,64,2304]{4,3,2,1,0:T(8,128)(2,1)} %constant_dynamic-slice_fusion.13), channel_id=1, source_target_pairs={{0,16},{4,20},{8,24},{12,28},{16,0},{20,4},{24,8},{28,12},{1,17},{... | collective-permute-start | bytes 3538952 | tf_op jit(solution)/shard_map/ppermute | solution.py:28
  55.9 42.1 %collective-permute-start.3 = (bf16[192,2048]{1,0:T(8,128)(2,1)}, bf16[192,2048]{1,0:T(8,128)(2,1)}, u32[]{:S(2)}, u32[]{:S(2)}) collective-permute-start(bf16[192,2048]{1,0:T(8,128)(2,1)} %collective-permute-done.refs_11_), channel_id=1, source_target_pairs={{0,4},{8,0},{16,8},{24,16},{28,24},{20,28},{12,20},{4,12},{1,5},{9... | collective-permute-start | bytes 2359304 | tf_op jit(solution)/shard_map/ppermute | solution.py:135
  56.0 42.1 %collective-permute-start.4 = (bf16[192,2048]{1,0:T(8,128)(2,1)}, bf16[192,2048]{1,0:T(8,128)(2,1)}, u32[]{:S(2)}, u32[]{:S(2)}) collective-permute-start(bf16[192,2048]{1,0:T(8,128)(2,1)} %collective-permute-done.1.refs_12_), channel_id=1, source_target_pairs={{0,8},{8,16},{16,24},{24,28},{28,20},{20,12},{12,4},{4,0},{1,9},{9... | collective-permute-start | bytes 2359304 | tf_op jit(solution)/shard_map/ppermute | solution.py:135
  59.9 34.0 %collective-permute-start.5 = (bf16[2,1,2,80,768]{4,3,2,1,0:T(8,128)(2,1)}, bf16[2,1,2,80,768]{4,3,2,1,0:T(8,128)(2,1)}, u32[]{:S(2)}, u32[]{:S(2)}) collective-permute-start(bf16[2,1,2,80,768]{4,3,2,1,0:T(8,128)(2,1)} %constant_dynamic-slice_fusion.14), channel_id=1, source_target_pairs={{0,8},{4,12},{8,0},{12,4},{16,24},{20,28},{24,16},{28,20},{1,9},{5... | collective-permute-start | bytes 1474568 | tf_op jit(solution)/shard_map/ppermute | solution.py:28
  100.5 41.3 %collective-permute-start.10 = (bf16[4,1,1,64,2304]{4,3,1,0,2:T(8,128)(2,1)}, bf16[4,1,1,64,2304]{4,3,1,0,2:T(8,128)(2,1)}, u32[]{:S(2)}, u32[]{:S(2)}) collective-permute-start(bf16[4,1,1,64,2304]{4,3,1,0,2:T(8,128)(2,1)} %constant_dynamic-slice_fusion.11), channel_id=1, source_target_pairs={{0,4},{4,0},{8,12},{12,8},{16,20},{20,16},{24,28},{28,24},{1,5},{5... | collective-permute-start | bytes 3538952 | tf_op jit(solution)/shard_map/ppermute | solution.py:28
  103.3 38.5 %collective-permute-start.7 = (bf16[192,2048]{1,0:T(8,128)(2,1)}, bf16[192,2048]{1,0:T(8,128)(2,1)}, u32[]{:S(2)}, u32[]{:S(2)}) collective-permute-start(bf16[192,2048]{1,0:T(8,128)(2,1)} %collective-permute-done.3.refs_13_), channel_id=1, source_target_pairs={{0,4},{8,0},{16,8},{24,16},{28,24},{20,28},{12,20},{4,12},{1,5},{9... | collective-permute-start | bytes 2359304 | tf_op jit(solution)/shard_map/ppermute | solution.py:135
  103.3 38.5 %collective-permute-start.8 = (bf16[192,2048]{1,0:T(8,128)(2,1)}, bf16[192,2048]{1,0:T(8,128)(2,1)}, u32[]{:S(2)}, u32[]{:S(2)}) collective-permute-start(bf16[192,2048]{1,0:T(8,128)(2,1)} %collective-permute-done.4.refs_14_), channel_id=1, source_target_pairs={{0,8},{8,16},{16,24},{24,28},{28,20},{20,12},{12,4},{4,0},{1,9},{9... | collective-permute-start | bytes 2359304 | tf_op jit(solution)/shard_map/ppermute | solution.py:135
  107.2 34.5 %collective-permute-start.9 = (bf16[1,1,4,80,768]{4,3,2,1,0:T(8,128)(2,1)}, bf16[1,1,4,80,768]{4,3,2,1,0:T(8,128)(2,1)}, u32[]{:S(2)}, u32[]{:S(2)}) collective-permute-start(bf16[1,1,4,80,768]{4,3,2,1,0:T(8,128)(2,1)} %constant_dynamic-slice_fusion.12), channel_id=1, source_target_pairs={{0,16},{4,20},{8,24},{12,28},{16,0},{20,4},{24,8},{28,12},{1,17},{... | collective-permute-start | bytes 1474568 | tf_op jit(solution)/shard_map/ppermute | solution.py:28
  142.9 31.8 %collective-permute-start.13 = (bf16[8,80,768]{2,1,0:T(8,128)(2,1)S(1)}, bf16[8,80,768]{2,1,0:T(8,128)(2,1)}, u32[]{:S(2)}, u32[]{:S(2)}) collective-permute-start(bf16[8,80,768]{2,1,0:T(8,128)(2,1)S(1)} %bitcast.182), channel_id=1, source_target_pairs={{0,2},{1,3},{2,0},{3,1},{4,6},{5,7},{6,4},{7,5},{8,10},{9,11},{10,... | collective-permute-start | bytes 2949128 | tf_op jit(solution)/shard_map/ppermute | solution.py:28
  146.1 300.7 %reduce-scatter.3.cloned.1.call-start = ((), (), s32[]{:S(2)}) async-start(), calls=%async_computation.3 | async-start | bytes 4718592 | tf_op jit(solution)/shard_map/reduce_scatter | solution.py:1034
  146.2 28.5 %collective-permute-start.11 = (bf16[192,2048]{1,0:T(8,128)(2,1)}, bf16[192,2048]{1,0:T(8,128)(2,1)S(1)}, u32[]{:S(2)}, u32[]{:S(2)}) collective-permute-start(bf16[192,2048]{1,0:T(8,128)(2,1)} %collective-permute-done.8.refs_16_), channel_id=1, source_target_pairs={{0,8},{8,16},{16,24},{24,28},{28,20},{20,12},{12,4},{4,0},{1,9},{9... | collective-permute-start | bytes 2359304 | tf_op jit(solution)/shard_map/ppermute | solution.py:135
  150.1 28.9 %collective-permute-start.12 = (bf16[8,80,768]{2,1,0:T(8,128)(2,1)S(1)}, bf16[8,80,768]{2,1,0:T(8,128)(2,1)S(1)}, u32[]{:S(2)}, u32[]{:S(2)}) collective-permute-start(bf16[8,80,768]{2,1,0:T(8,128)(2,1)S(1)} %bitcast.183), channel_id=1, source_target_pairs={{0,1},{1,0},{2,3},{3,2},{4,5},{5,4},{6,7},{7,6},{8,9},{9,8},{10,11... | collective-permute-start | bytes 2949128 | tf_op jit(solution)/shard_map/ppermute | solution.py:28
  179.0 63.2 %collective-permute-start.15 = (bf16[512,2048]{1,0:T(8,128)(2,1)}, bf16[512,2048]{1,0:T(8,128)(2,1)}, u32[]{:S(2)}, u32[]{:S(2)}) collective-permute-start(bf16[512,2048]{1,0:T(8,128)(2,1)} %slice_dynamic-update-slice_fusion.refs_3_), channel_id=1, source_target_pairs={{0,2},{1,3},{2,0},{3,1},{4,6},{5,7},{6,4},{7,5},{8,10},{9,11},{10,... | collective-permute-start | bytes 6291464 | tf_op jit(solution)/shard_map/ppermute | solution.py:28
  182.1 60.0 %collective-permute-start.16 = (bf16[2,1,2,64,2304]{4,3,2,1,0:T(8,128)(2,1)}, bf16[2,1,2,64,2304]{4,3,2,1,0:T(8,128)(2,1)}, u32[]{:S(2)}, u32[]{:S(2)}) collective-permute-start(bf16[2,1,2,64,2304]{4,3,2,1,0:T(8,128)(2,1)} %constant_dynamic-slice_fusion.9), channel_id=1, source_target_pairs={{0,8},{4,12},{8,0},{12,4},{16,24},{20,28},{24,16},{28,20},{1,9},{5... | collective-permute-start | bytes 3538952 | tf_op jit(solution)/shard_map/ppermute | solution.py:28
  183.3 82.7 %collective-permute-start.21 = (bf16[512,2048]{1,0:T(8,128)(2,1)}, bf16[512,2048]{1,0:T(8,128)(2,1)}, u32[]{:S(2)}, u32[]{:S(2)}) collective-permute-start(bf16[512,2048]{1,0:T(8,128)(2,1)} %slice_dynamic-update-slice_fusion.refs_3_), channel_id=1, source_target_pairs={{0,1},{1,0},{2,3},{3,2},{4,5},{5,4},{6,7},{7,6},{8,9},{9,8},{10,11... | collective-permute-start | bytes 6291464 | tf_op jit(solution)/shard_map/ppermute | solution.py:28
  242.2 36.2 %collective-permute-start.22 = (bf16[512,2048]{1,0:T(8,128)(2,1)}, bf16[512,2048]{1,0:T(8,128)(2,1)S(1)}, u32[]{:S(2)}, u32[]{:S(2)}) collective-permute-start(bf16[512,2048]{1,0:T(8,128)(2,1)} %collective-permute-done.15.refs_5_), channel_id=1, source_target_pairs={{0,1},{1,0},{2,3},{3,2},{4,5},{5,4},{6,7},{7,6},{8,9},{9,8},{10,11... | collective-permute-start | bytes 6291464 | tf_op jit(solution)/shard_map/ppermute | solution.py:28
  243.6 53.8 %collective-permute-start.27 = (bf16[8,64,2304]{2,1,0:T(8,128)(2,1)S(1)}, bf16[8,64,2304]{2,1,0:T(8,128)(2,1)}, u32[]{:S(2)}, u32[]{:S(2)}) collective-permute-start(bf16[8,64,2304]{2,1,0:T(8,128)(2,1)S(1)} %bitcast.165), channel_id=1, source_target_pairs={{0,2},{1,3},{2,0},{3,1},{4,6},{5,7},{6,4},{7,5},{8,10},{9,11},{10,... | collective-permute-start | bytes 7077896 | tf_op jit(solution)/shard_map/ppermute | solution.py:28
  292.4 31.9 %collective-permute-start.26 = (bf16[8,64,2304]{2,1,0:T(8,128)(2,1)S(1)}, bf16[8,64,2304]{2,1,0:T(8,128)(2,1)}, u32[]{:S(2)}, u32[]{:S(2)}) collective-permute-start(bf16[8,64,2304]{2,1,0:T(8,128)(2,1)S(1)} %bitcast.166), channel_id=1, source_target_pairs={{0,1},{1,0},{2,3},{3,2},{4,5},{5,4},{6,7},{7,6},{8,9},{9,8},{10,11... | collective-permute-start | bytes 7077896 | tf_op jit(solution)/shard_map/ppermute | solution.py:28
  341.1 330.4 %reduce-scatter.5.cloned.1.call-start = ((), (), s32[]{:S(2)}) async-start(), calls=%async_computation.4 | async-start | bytes 2359296 | tf_op jit(solution)/shard_map/reduce_scatter | solution.py:1085
  394.9 26.3 %collective-permute-start.33 = (bf16[2,8,64,768]{3,2,1,0:T(8,128)(2,1)}, bf16[2,8,64,768]{3,2,1,0:T(8,128)(2,1)S(1)}, u32[]{:S(2)}, u32[]{:S(2)}) collective-permute-start(bf16[2,8,64,768]{3,2,1,0:T(8,128)(2,1)} %get-tuple-element.202), channel_id=1, source_target_pairs={{0,1},{1,0},{2,3},{3,2},{4,5},{5,4},{6,7},{7,6},{8,9},{9,8},{10,11... | collective-permute-start | bytes 4718600 | tf_op jit(solution)/shard_map/ppermute | solution.py:28
  446.8 30.9 %collective-permute-start.39 = (bf16[2,8,64,2048]{3,2,1,0:T(8,128)(2,1)}, bf16[2,8,64,2048]{3,2,1,0:T(8,128)(2,1)}, u32[]{:S(2)}, u32[]{:S(2)}) collective-permute-start(bf16[2,8,64,2048]{3,2,1,0:T(8,128)(2,1)} %get-tuple-element.217), channel_id=1, source_target_pairs={{0,1},{1,0},{2,3},{3,2},{4,5},{5,4},{6,7},{7,6},{8,9},{9,8},{10,11... | collective-permute-start | bytes 12582920 | tf_op jit(solution)/shard_map/ppermute | solution.py:28
  460.1 37.8 %collective-permute-start.40 = (bf16[8,64,1536]{2,1,0:T(8,128)(2,1)}, bf16[8,64,1536]{2,1,0:T(8,128)(2,1)S(1)}, u32[]{:S(2)}, u32[]{:S(2)}) collective-permute-start(bf16[8,64,1536]{2,1,0:T(8,128)(2,1)} %fusion.5), channel_id=1, source_target_pairs={{0,2},{1,3},{2,0},{3,1},{4,6},{5,7},{6,4},{7,5},{8,10},{9,11},{10,... | collective-permute-start | bytes 4718600 | tf_op jit(solution)/shard_map/ppermute | solution.py:28
  462.4 35.5 %collective-permute-start.41 = (bf16[1,1,4,64,768]{4,3,2,1,0:T(8,128)(2,1)S(1)}, bf16[1,1,4,64,768]{4,3,2,1,0:T(8,128)(2,1)S(1)}, u32[]{:S(2)}, u32[]{:S(2)}) collective-permute-start(bf16[1,1,4,64,768]{4,3,2,1,0:T(8,128)(2,1)S(1)} %constant_dynamic-slice_fusion.8), channel_id=1, source_target_pairs={{0,16},{4,20},{8,24},{12,28},{16,0},{20,4},{24,8},{28,12},{1,17},{... | collective-permute-start | bytes 1179656 | tf_op jit(solution)/shard_map/ppermute | solution.py:28
  481.4 64.4 %collective-permute-start.46 = (bf16[8,64,2048]{2,1,0:T(8,128)(2,1)}, bf16[8,64,2048]{2,1,0:T(8,128)(2,1)}, u32[]{:S(2)}, u32[]{:S(2)}) collective-permute-start(bf16[8,64,2048]{2,1,0:T(8,128)(2,1)} %fusion.3), channel_id=1, source_target_pairs={{0,2},{1,3},{2,0},{3,1},{4,6},{5,7},{6,4},{7,5},{8,10},{9,11},{10,... | collective-permute-start | bytes 6291464 | tf_op jit(solution)/shard_map/ppermute | solution.py:28
  500.9 44.9 %collective-permute-start.45 = (bf16[1,1,4,64,1536]{4,3,2,1,0:T(8,128)(2,1)}, bf16[1,1,4,64,1536]{4,3,2,1,0:T(8,128)(2,1)}, u32[]{:S(2)}, u32[]{:S(2)}) collective-permute-start(bf16[1,1,4,64,1536]{4,3,2,1,0:T(8,128)(2,1)} %constant_dynamic-slice_fusion.4), channel_id=1, source_target_pairs={{0,16},{4,20},{8,24},{12,28},{16,0},{20,4},{24,8},{28,12},{1,17},{... | collective-permute-start | bytes 2359304 | tf_op jit(solution)/shard_map/ppermute | solution.py:28
  517.9 26.7 %collective-permute-start.42 = (bf16[128,2048]{1,0:T(8,128)(2,1)}, bf16[128,2048]{1,0:T(8,128)(2,1)}, u32[]{:S(2)}, u32[]{:S(2)}) collective-permute-start(bf16[128,2048]{1,0:T(8,128)(2,1)} %get-tuple-element.291), channel_id=1, source_target_pairs={{0,8},{8,16},{16,24},{24,28},{28,20},{20,12},{12,4},{4,0},{1,9},{9... | collective-permute-start | bytes 1572872 | tf_op jit(solution)/shard_map/ppermute | solution.py:135
  520.4 25.5 %collective-permute-start.43 = (bf16[128,2048]{1,0:T(8,128)(2,1)}, bf16[128,2048]{1,0:T(8,128)(2,1)}, u32[]{:S(2)}, u32[]{:S(2)}) collective-permute-start(bf16[128,2048]{1,0:T(8,128)(2,1)} %get-tuple-element.290), channel_id=1, source_target_pairs={{0,4},{8,0},{16,8},{24,16},{28,24},{20,28},{12,20},{4,12},{1,5},{9... | collective-permute-start | bytes 1572872 | tf_op jit(solution)/shard_map/ppermute | solution.py:135
  602.5 37.8 %collective-permute-start.60 = (bf16[2,1,2,64,1536]{4,3,2,1,0:T(8,128)(2,1)}, bf16[2,1,2,64,1536]{4,3,2,1,0:T(8,128)(2,1)}, u32[]{:S(2)}, u32[]{:S(2)}) collective-permute-start(bf16[2,1,2,64,1536]{4,3,2,1,0:T(8,128)(2,1)} %constant_dynamic-slice_fusion), channel_id=1, source_target_pairs={{0,8},{4,12},{8,0},{12,4},{16,24},{20,28},{24,16},{28,20},{1,9},{5... | collective-permute-start | bytes 2359304 | tf_op jit(solution)/shard_map/ppermute | solution.py:28
  635.6 30.6 %collective-permute-start.59 = (bf16[1,2,80,768]{3,2,1,0:T(8,128)(2,1)}, bf16[1,2,80,768]{3,2,1,0:T(8,128)(2,1)}, u32[]{:S(2)}, u32[]{:S(2)}) collective-permute-start(bf16[1,2,80,768]{3,2,1,0:T(8,128)(2,1)} %get-tuple-element.300), channel_id=1, source_target_pairs={{0,24},{4,28},{8,16},{12,20},{16,8},{20,12},{24,0},{28,4},{1,25},{... | collective-permute-start | bytes 737288 | tf_op jit(solution)/shard_map/ppermute | solution.py:28
  (83 other events, 1169.6 us)
Sparse Core Ops, SparseCore 0:
  146.3 100.9 all-gather.1
  341.2 98.0 reduce-scatter.2
  580.2 84.0 reduce-scatter.4

commit v5 on v4

--- a/solution.py
+++ b/solution.py
@@ -1093,10 +1093,8 @@
         ring.step()
         grad_joint = grad_far_begin(grad_joint, n_batch)
         grad_down = exchange_begin(exchange_end(grad_down, n_seq, 1), n_seq, 2)
-        projected_own = dot(own(mixed_all), output_all, ((1,), (0,)))
-        result = values + projected_own + result_sum.astype(f32)
-        grad_joint, grad_both, grad_down, result = ring.tie(
-            grad_joint, grad_both, grad_down, result
+        grad_joint, grad_both, grad_down, result_sum = ring.tie(
+            grad_joint, grad_both, grad_down, result_sum
         )
         grad_down = exchange_end(grad_down, n_seq, 2)
         ring.step()
@@ -1108,6 +1106,8 @@
             parts = exchange_parts(grad_joint)
         grad_both = exchange_end(grad_both, n_seq, 2)
         token_grad = cotangent + ring.total()
+        mixed_own = after(own(mixed_all), grad_joint)
+        result = values + dot(mixed_own, output_all, ((1,), (0,))) + result_sum.astype(f32)
         grad_output = grad_output.astype(f32)
 
         def unsplit(grad):
@@ -1118,8 +1118,8 @@
         grad_up = unsplit(grad_both[:, :, ff_local:])
         grad_down = unsplit(grad_down)
         if n_seq == 8:
-            done = tie(*parts, grad_gate, grad_up, grad_down, token_grad)
-            parts, (grad_gate, grad_up, grad_down, token_grad) = done[:3], done[3:]
+            done = tie(*parts, grad_gate, grad_up, grad_down, token_grad, result)
+            parts, (grad_gate, grad_up, grad_down, token_grad, result) = done[:3], done[3:]
             grad_joint, vectors = unpack_joint(grad_joint, parts, rows)
             vectors = vectors[0]
         else:

time: 688 us -> 685 us (level)
  waiting for transfers between devices: 283 us -> 272 us
  local copies, waits for them, and re-layouts: 73.4 us -> 80.9 us
  transfers between devices with their start and end apart: 64 -> 64, of which waited for: 32 -> 31; matrix products, arithmetic and copies ran while one was open for 18% -> 19% of each run, Pallas kernels for 25% -> 25%
where the time goes in v5:
time: 685 us; the launch traced here: 677 us
  waiting for transfers between devices  272 us (40%)
  Pallas kernels  167 us (24%)
  local copies, waits for them, and re-layouts  80.9 us (12%)
  starting transfers between devices  76.4 us (11%)
  other arithmetic  54.4 us (8%)
  between operations  16 us (2%)
  matrix products  10.8 us (2%)
    ppermute x28, waiting for transfers between devices, ring_step(): lax.ppermute(value, 'seq', [(RING[i], RING[(i + way) % 8]) for i in range...  149 us
    ppermute x33, waiting for transfers between devices, swap(): return lax.ppermute(value, axis, [(i, i ^ bit) for i in range(number)])  122 us
    pallas_call x5, Pallas kernels, call_kernel(): pl.pallas_call(kernel, grid=(length // block,), in_specs=in_specs, out_sp...  99.5 us
    pallas_call x4, Pallas kernels, weight_grad(): pl.pallas_call(lambda *refs: grad_kernel(rows, rest is not None, below is...  43 us
    ppermute x28, starting transfers between devices, ring_step(): lax.ppermute(value, 'seq', [(RING[i], RING[(i + way) % 8]) for i in range...  40.6 us
    ppermute x33, starting transfers between devices, swap(): return lax.ppermute(value, axis, [(i, i ^ bit) for i in range(number)])  35.6 us
    unnamed x119, local copies, waits for them, and re-layouts  18.5 us
  transfers between devices with their start and end apart: 64, of which 31 were waited for; matrix products, arithmetic and copies ran while one was open for 19% of the time, Pallas kernels for 25%

profile of v5, /device:TPU:8, one launch (start us, length us, event | category | flops | bytes accessed | tf_op | source)
XLA Modules:
  0.0 677.5 jit_solution(16776928518598575637)
XLA Ops:
  32.0 23.9 %collective-permute-done.refs_11_ = bf16[192,2048]{1,0:T(8,128)(2,1)} collective-permute-done((bf16[192,2048]{1,0:T(8,128)(2,1)}, bf16[192,2048]{1,0:T(8,128)(2,1)}, u32[]{:S(2)}, u32[]{:S(2)}) %collective-permute-start) | collective-permute-done | bytes 786464 | tf_op jit(solution)/shard_map/ppermute | solution.py:135
  63.2 17.5 %collective-permute-done.6 = bf16[1,1,4,64,2304]{4,3,2,1,0:T(8,128)(2,1)} collective-permute-done((bf16[1,1,4,64,2304]{4,3,2,1,0:T(8,128)(2,1)}, bf16[1,1,4,64,2304]{4,3,2,1,0:T(8,128)(2,1)}, u32[]{:S(2)}, u32[]{:S(2)}) %collective-permute-start.6) | collective-permute-done | bytes 1179680 | tf_op jit(solution)/shard_map/ppermute | solution.py:28
  80.7 13.1 %collective-permute-done.5 = bf16[2,1,2,80,768]{4,3,2,1,0:T(8,128)(2,1)} collective-permute-done((bf16[2,1,2,80,768]{4,3,2,1,0:T(8,128)(2,1)}, bf16[2,1,2,80,768]{4,3,2,1,0:T(8,128)(2,1)}, u32[]{:S(2)}, u32[]{:S(2)}) %collective-permute-start.5) | collective-permute-done | bytes 491552 | tf_op jit(solution)/shard_map/ppermute | solution.py:28
  109.7 32.1 %collective-permute-done.9 = bf16[1,1,4,80,768]{4,3,2,1,0:T(8,128)(2,1)} collective-permute-done((bf16[1,1,4,80,768]{4,3,2,1,0:T(8,128)(2,1)}, bf16[1,1,4,80,768]{4,3,2,1,0:T(8,128)(2,1)}, u32[]{:S(2)}, u32[]{:S(2)}) %collective-permute-start.9) | collective-permute-done | bytes 491552 | tf_op jit(solution)/shard_map/ppermute | solution.py:28
  150.1 24.6 %collective-permute-done.11.refs_17_ = bf16[192,2048]{1,0:T(8,128)(2,1)S(1)} collective-permute-done((bf16[192,2048]{1,0:T(8,128)(2,1)}, bf16[192,2048]{1,0:T(8,128)(2,1)S(1)}, u32[]{:S(2)}, u32[]{:S(2)}) %collective-permute-start.11) | collective-permute-done | bytes 786464 | tf_op jit(solution)/shard_map/ppermute | solution.py:135
  186.6 10.8 %make_heads.1 = (bf16[1024,768]{1,0:T(8,128)(2,1)}, bf16[1024,2048]{1,0:T(8,128)(2,1)}, bf16[1024,2048]{1,0:T(8,128)(2,1)}) custom-call(f32[1,2048]{1,0:T(1,128)} %reshape.329.refs_0_.refs_2_, f32[1,2048]{1,0:T(1,128)} %reshape.330.refs_1_, f32[1,768]{1,0:T(1,128)} %bitcast.206, f32[1024,128]{1,0:T(8,128)} %constant.288.clone.refs_3_.cos_ref, ...), custom_call_target="tpu_custom_call" | custom-call | flops 3221225472 | bytes 6442450 | tf_op jit(solution)/shard_map/make_heads/pallas_call | solution.py:470
  197.4 8.3 %attend.1 = (f32[1024,256]{1,0:T(8,128)}, bf16[1024,256]{1,0:T(8,128)(2,1)}, f32[1024,128]{1,0:T(8,128)}) custom-call(bf16[1024,768]{1,0:T(8,128)(2,1)} %get-tuple-element.167.low_ref), custom_call_target="tpu_custom_call" | custom-call | flops 2147483648 | bytes 12582912 | tf_op jit(solution)/shard_map/attend/pallas_call | solution.py:302
  205.7 36.4 %collective-permute-done.16 = bf16[2,1,2,64,2304]{4,3,2,1,0:T(8,128)(2,1)} collective-permute-done((bf16[2,1,2,64,2304]{4,3,2,1,0:T(8,128)(2,1)}, bf16[2,1,2,64,2304]{4,3,2,1,0:T(8,128)(2,1)}, u32[]{:S(2)}, u32[]{:S(2)}) %collective-permute-start.16) | collective-permute-done | bytes 1179680 | tf_op jit(solution)/shard_map/ppermute | solution.py:28
  244.7 4.9 collective-permute-start.17
  249.7 11.4 %collective-permute-done.17.refs_9_ = bf16[1024,256]{1,0:T(8,128)(2,1)S(1)} collective-permute-done((bf16[1024,256]{1,0:T(8,128)(2,1)S(1)}, bf16[1024,256]{1,0:T(8,128)(2,1)S(1)}, u32[]{:S(2)}, u32[]{:S(2)}) %collective-permute-start.17) | collective-permute-done | bytes 524320 | tf_op jit(solution)/shard_map/ppermute | solution.py:135
  266.1 11.1 %collective-permute-done.19.refs_11_ = bf16[1024,256]{1,0:T(8,128)(2,1)S(1)} collective-permute-done((bf16[1024,256]{1,0:T(8,128)(2,1)S(1)}, bf16[1024,256]{1,0:T(8,128)(2,1)S(1)}, u32[]{:S(2)}, u32[]{:S(2)}) %collective-permute-start.19) | collective-permute-done | bytes 524320 | tf_op jit(solution)/shard_map/ppermute | solution.py:135
  280.5 9.7 %collective-permute-done.23.refs_12_ = bf16[1024,256]{1,0:T(8,128)(2,1)S(1)} collective-permute-done((bf16[1024,256]{1,0:T(8,128)(2,1)S(1)}, bf16[1024,256]{1,0:T(8,128)(2,1)S(1)}, u32[]{:S(2)}, u32[]{:S(2)}) %collective-permute-start.23) | collective-permute-done | bytes 524320 | tf_op jit(solution)/shard_map/ppermute | solution.py:135
  292.4 4.9 collective-permute-done.27.refs_3_.refs_9_
  304.2 20.1 %make_middle.1 = (bf16[1024,2048]{1,0:T(8,128)(2,1)}, bf16[1024,2048]{1,0:T(8,128)(2,1)}, f32[1024,128]{1,0:T(8,128)}, bf16[1024,2048]{1,0:T(8,128)(2,1)}, bf16[8,4,64,2048]{3,2,1,0:T(8,128)(2,1)}) custom-call(bf16[1024,2048]{1,0:T(8,128)(2,1)} %get-tuple-element.168.refs_0_.refs_1_, f32[1,2048]{1,0:T(1,128)} %reshape.332.refs_1_.refs_5_, ...), custom_call_target="tpu_custom_call" | custom-call | flops 8589934592 | bytes 17179868 | tf_op jit(solution)/shard_map/make_middle/pallas_call | solution.py:470
  324.4 16.7 %feed.1 = (f32[1024,768]{1,0:T(8,128)}, f32[1024,768]{1,0:T(8,128)}, bf16[1024,768]{1,0:T(8,128)(2,1)}, bf16[1024,2048]{1,0:T(8,128)(2,1)}) custom-call(bf16[1024,2048]{1,0:T(8,128)(2,1)} %get-tuple-element.184.refs_0_, bf16[8,64,2304]{2,1,0:T(8,128)(2,1)} %bitcast.168, bf16[8,64,2304]{2,1,0:T(8,128)(2,1)} %collective-permute-done.26.refs_2_.refs_8_, ...), custom_call_target="tpu_custom_call" | custom-call | flops 9663676416 | bytes 19327352 | tf_op jit(solution)/shard_map/feed/pallas_call | solution.py:470
  341.2 37.3 %feed_back.1 = (bf16[1024,1536]{1,0:T(8,128)(2,1)}, bf16[1024,2048]{1,0:T(8,128)(2,1)}, bf16[8,1024,256]{2,1,0:T(8,128)(2,1)}, f32[8,2048]{1,0:T(8,128)}) custom-call(f32[1024,768]{1,0:T(8,128)} %get-tuple-element.188.refs_0_, f32[1024,768]{1,0:T(8,128)} %get-tuple-element.189.refs_1_, bf16[1024,2048]{1,0:T(8,128)(2,1)} %all-gather.2.cloned.1.call-done.refs_2_.refs_0_, ...), custom_call_target="tpu_custom_call" | custom-call | flops 18253611008 | bytes 36507224 | tf_op jit(solution)/shard_map/feed_back/pallas_call | solution.py:470
  382.4 7.5 %weight_grad.4 = (bf16[2,8,64,768]{3,2,1,0:T(8,128)(2,1)}, bf16[2,8,64,768]{3,2,1,0:T(8,128)(2,1)}) custom-call(bf16[1024,2048]{1,0:T(8,128)(2,1)} %all-gather.2.cloned.1.call-done.refs_2_.refs_0_, bf16[1024,768]{1,0:T(8,128)(2,1)} %get-tuple-element.195.refs_1_), custom_call_target="tpu_custom_call" | custom-call | flops 3221225472 | bytes 12058624 | tf_op jit(solution)/shard_map/weight_grad/pallas_call | solution.py:820
  397.7 6.7 collective-permute-start.32
  404.3 11.1 %weight_grad.5 = (bf16[2,8,64,1536]{3,2,1,0:T(8,128)(2,1)}, bf16[2,8,64,1536]{3,2,1,0:T(8,128)(2,1)}) custom-call(bf16[1024,2048]{1,0:T(8,128)(2,1)} %get-tuple-element.184.refs_0_, bf16[1024,1536]{1,0:T(8,128)(2,1)} %get-tuple-element.200.refs_1_), custom_call_target="tpu_custom_call" | custom-call | flops 6442450944 | bytes 19922944 | tf_op jit(solution)/shard_map/weight_grad/pallas_call | solution.py:820
  427.8 16.3 %weight_grad.6 = (bf16[2,8,64,2048]{3,2,1,0:T(8,128)(2,1)}, bf16[2,8,64,2048]{3,2,1,0:T(8,128)(2,1)}) custom-call(bf16[1024,2048]{1,0:T(8,128)(2,1)} %get-tuple-element.209.refs_0_, bf16[1024,2048]{1,0:T(8,128)(2,1)} %get-tuple-element.210.refs_1_.refs_3_, bf16[128,2048]{1,0:T(8,128)(2,1)} %bitcast_convert_fusion.refs_2_), custom_call_target="tpu_custom_call" | custom-call | flops 8589934592 | bytes 25165824 | tf_op jit(solution)/shard_map/weight_grad/pallas_call | solution.py:820
  464.6 13.8 %collective-permute-done.38 = bf16[1024,256]{1,0:T(8,128)(2,1)S(1)} collective-permute-done((bf16[1024,256]{1,0:T(8,128)(2,1)S(1)}, bf16[1024,256]{1,0:T(8,128)(2,1)S(1)}, u32[]{:S(2)}, u32[]{:S(2)}) %collective-permute-start.38) | collective-permute-done | bytes 524320 | tf_op jit(solution)/shard_map/ppermute | solution.py:135
  484.8 13.6 %attend_back.1.refs_0_.refs_1_ = bf16[1024,768]{1,0:T(8,128)(2,1)} custom-call(bf16[1024,768]{1,0:T(8,128)(2,1)} %get-tuple-element.167.low_ref, bf16[1024,256]{1,0:T(8,128)(2,1)} %fusion.14.grad_ref, f32[1024,256]{1,0:T(8,128)} %get-tuple-element.223.context_ref, f32[1024,128]{1,0:T(8,128)} %get-tuple-element.224.lse_ref, ...), custom_call_target="tpu_custom_call" | custom-call | flops 5368709120 | bytes 12582912 | tf_op jit(solution)/shard_map/attend_back/pallas_call | solution.py:382
  501.5 14.6 %first_back.1 = (bf16[1024,2048]{1,0:T(8,128)(2,1)}, f32[8,2048]{1,0:T(8,128)}, f32[8,768]{1,0:T(8,128)}) custom-call(bf16[1024,768]{1,0:T(8,128)(2,1)} %attend_back.1.refs_0_.refs_1_, bf16[1024,2048]{1,0:T(8,128)(2,1)} %get-tuple-element.168.refs_0_.refs_1_, f32[1,2048]{1,0:T(1,128)} %reshape.329.refs_0_.refs_2_, ...), custom_call_target="tpu_custom_call" | custom-call | flops 3221225472 | bytes 6442450 | tf_op jit(solution)/shard_map/first_back/pallas_call | solution.py:470
  535.5 8.1 %weight_grad.7 = (bf16[2,8,80,768]{3,2,1,0:T(8,128)(2,1)}, bf16[2,8,80,768]{3,2,1,0:T(8,128)(2,1)}) custom-call(bf16[1024,2048]{1,0:T(8,128)(2,1)} %get-tuple-element.232.refs_0_, bf16[1024,768]{1,0:T(8,128)(2,1)} %attend_back.1.refs_0_.refs_1_, bf16[8,4,16,768]{3,2,1,0:T(8,128)(2,1)} %pad.22.refs_2_), custom_call_target="tpu_custom_call" | custom-call | flops 3221225472 | bytes 12058624 | tf_op jit(solution)/shard_map/weight_grad/pallas_call | solution.py:820
  556.2 8.9 %collective-permute-done.47 = bf16[128,2048]{1,0:T(8,128)(2,1)S(1)} collective-permute-done((bf16[128,2048]{1,0:T(8,128)(2,1)S(1)}, bf16[128,2048]{1,0:T(8,128)(2,1)S(1)}, u32[]{:S(2)}, u32[]{:S(2)}) %collective-permute-start.47) | collective-permute-done | bytes 524320 | tf_op jit(solution)/shard_map/ppermute | solution.py:135
  578.1 6.5 collective-permute-done.50
  585.1 5.4 collective-permute-done.52
  604.6 7.1 %collective-permute-start.60 = (bf16[2,1,2,64,1536]{4,3,2,1,0:T(8,128)(2,1)S(1)}, bf16[2,1,2,64,1536]{4,3,2,1,0:T(8,128)(2,1)S(1)}, u32[]{:S(2)}, u32[]{:S(2)}) collective-permute-start(bf16[2,1,2,64,1536]{4,3,2,1,0:T(8,128)(2,1)S(1)} %constant_dynamic-slice_fusion.1), channel_id=1, source_target_pairs={{0,8},{4,12},{8,0},{12,4},{16,24},{20,28},{24,16},{28,20},{1,9},{5... | collective-permute-start | bytes 2359304 | tf_op jit(solution)/shard_map/ppermute | solution.py:28
  611.7 9.2 %collective-permute-done.55 = bf16[128,2048]{1,0:T(8,128)(2,1)} collective-permute-done((bf16[128,2048]{1,0:T(8,128)(2,1)}, bf16[128,2048]{1,0:T(8,128)(2,1)}, u32[]{:S(2)}, u32[]{:S(2)}) %collective-permute-start.55) | collective-permute-done | bytes 524320 | tf_op jit(solution)/shard_map/ppermute | solution.py:135
  623.0 9.6 %collective-permute-start.57 = (bf16[1,2,80,768]{3,2,1,0:T(8,128)(2,1)}, bf16[1,2,80,768]{3,2,1,0:T(8,128)(2,1)}, u32[]{:S(2)}, u32[]{:S(2)}) collective-permute-start(bf16[1,2,80,768]{3,2,1,0:T(8,128)(2,1)} %get-tuple-element.306), channel_id=1, source_target_pairs={{0,8},{4,12},{8,0},{12,4},{16,24},{20,28},{24,16},{28,20},{1,9},{5... | collective-permute-start | bytes 737288 | tf_op jit(solution)/shard_map/ppermute | solution.py:28
  634.1 5.9 fusion.2
  650.6 12.8 %collective-permute-done.59 = bf16[1,2,80,768]{3,2,1,0:T(8,128)(2,1)} collective-permute-done((bf16[1,2,80,768]{3,2,1,0:T(8,128)(2,1)}, bf16[1,2,80,768]{3,2,1,0:T(8,128)(2,1)}, u32[]{:S(2)}, u32[]{:S(2)}) %collective-permute-start.59) | collective-permute-done | bytes 245792 | tf_op jit(solution)/shard_map/ppermute | solution.py:28
  (344 shorter events, 221.4 us)
Async XLA Ops:
  7.2 334.0 %all-gather.2.cloned.1.call-start = ((), (), s32[]{:S(2)}) async-start(), calls=%async_computation.2 | async-start | bytes 4718592 | tf_op jit(solution)/shard_map/all_gather | solution.py:956
  11.0 45.0 %collective-permute-start = (bf16[192,2048]{1,0:T(8,128)(2,1)}, bf16[192,2048]{1,0:T(8,128)(2,1)}, u32[]{:S(2)}, u32[]{:S(2)}) collective-permute-start(bf16[192,2048]{1,0:T(8,128)(2,1)} %pad_maximum_fusion.1.refs_10_), channel_id=1, source_target_pairs={{0,4},{8,0},{16,8},{24,16},{28,24},{20,28},{12,20},{4,12},{1,5},{9... | collective-permute-start | bytes 2359304 | tf_op jit(solution)/shard_map/ppermute | solution.py:135
  11.0 45.0 %collective-permute-start.1 = (bf16[192,2048]{1,0:T(8,128)(2,1)}, bf16[192,2048]{1,0:T(8,128)(2,1)}, u32[]{:S(2)}, u32[]{:S(2)}) collective-permute-start(bf16[192,2048]{1,0:T(8,128)(2,1)} %pad_maximum_fusion.1.refs_10_), channel_id=1, source_target_pairs={{0,8},{8,16},{16,24},{24,28},{28,20},{20,12},{12,4},{4,0},{1,9},{9... | collective-permute-start | bytes 2359304 | tf_op jit(solution)/shard_map/ppermute | solution.py:135
  27.5 53.2 %collective-permute-start.6 = (bf16[1,1,4,64,2304]{4,3,2,1,0:T(8,128)(2,1)}, bf16[1,1,4,64,2304]{4,3,2,1,0:T(8,128)(2,1)}, u32[]{:S(2)}, u32[]{:S(2)}) collective-permute-start(bf16[1,1,4,64,2304]{4,3,2,1,0:T(8,128)(2,1)} %constant_dynamic-slice_fusion.14), channel_id=1, source_target_pairs={{0,16},{4,20},{8,24},{12,28},{16,0},{20,4},{24,8},{28,12},{1,17},{... | collective-permute-start | bytes 3538952 | tf_op jit(solution)/shard_map/ppermute | solution.py:28
  55.9 42.1 %collective-permute-start.3 = (bf16[192,2048]{1,0:T(8,128)(2,1)}, bf16[192,2048]{1,0:T(8,128)(2,1)}, u32[]{:S(2)}, u32[]{:S(2)}) collective-permute-start(bf16[192,2048]{1,0:T(8,128)(2,1)} %collective-permute-done.refs_11_), channel_id=1, source_target_pairs={{0,4},{8,0},{16,8},{24,16},{28,24},{20,28},{12,20},{4,12},{1,5},{9... | collective-permute-start | bytes 2359304 | tf_op jit(solution)/shard_map/ppermute | solution.py:135
  56.0 42.1 %collective-permute-start.4 = (bf16[192,2048]{1,0:T(8,128)(2,1)}, bf16[192,2048]{1,0:T(8,128)(2,1)}, u32[]{:S(2)}, u32[]{:S(2)}) collective-permute-start(bf16[192,2048]{1,0:T(8,128)(2,1)} %collective-permute-done.1.refs_12_), channel_id=1, source_target_pairs={{0,8},{8,16},{16,24},{24,28},{28,20},{20,12},{12,4},{4,0},{1,9},{9... | collective-permute-start | bytes 2359304 | tf_op jit(solution)/shard_map/ppermute | solution.py:135
  59.9 34.0 %collective-permute-start.5 = (bf16[2,1,2,80,768]{4,3,2,1,0:T(8,128)(2,1)}, bf16[2,1,2,80,768]{4,3,2,1,0:T(8,128)(2,1)}, u32[]{:S(2)}, u32[]{:S(2)}) collective-permute-start(bf16[2,1,2,80,768]{4,3,2,1,0:T(8,128)(2,1)} %constant_dynamic-slice_fusion.15), channel_id=1, source_target_pairs={{0,8},{4,12},{8,0},{12,4},{16,24},{20,28},{24,16},{28,20},{1,9},{5... | collective-permute-start | bytes 1474568 | tf_op jit(solution)/shard_map/ppermute | solution.py:28
  100.5 41.3 %collective-permute-start.10 = (bf16[4,1,1,64,2304]{4,3,1,0,2:T(8,128)(2,1)}, bf16[4,1,1,64,2304]{4,3,1,0,2:T(8,128)(2,1)}, u32[]{:S(2)}, u32[]{:S(2)}) collective-permute-start(bf16[4,1,1,64,2304]{4,3,1,0,2:T(8,128)(2,1)} %constant_dynamic-slice_fusion.12), channel_id=1, source_target_pairs={{0,4},{4,0},{8,12},{12,8},{16,20},{20,16},{24,28},{28,24},{1,5},{5... | collective-permute-start | bytes 3538952 | tf_op jit(solution)/shard_map/ppermute | solution.py:28
  103.3 38.5 %collective-permute-start.7 = (bf16[192,2048]{1,0:T(8,128)(2,1)}, bf16[192,2048]{1,0:T(8,128)(2,1)}, u32[]{:S(2)}, u32[]{:S(2)}) collective-permute-start(bf16[192,2048]{1,0:T(8,128)(2,1)} %collective-permute-done.3.refs_13_), channel_id=1, source_target_pairs={{0,4},{8,0},{16,8},{24,16},{28,24},{20,28},{12,20},{4,12},{1,5},{9... | collective-permute-start | bytes 2359304 | tf_op jit(solution)/shard_map/ppermute | solution.py:135
  103.3 38.5 %collective-permute-start.8 = (bf16[192,2048]{1,0:T(8,128)(2,1)}, bf16[192,2048]{1,0:T(8,128)(2,1)}, u32[]{:S(2)}, u32[]{:S(2)}) collective-permute-start(bf16[192,2048]{1,0:T(8,128)(2,1)} %collective-permute-done.4.refs_14_), channel_id=1, source_target_pairs={{0,8},{8,16},{16,24},{24,28},{28,20},{20,12},{12,4},{4,0},{1,9},{9... | collective-permute-start | bytes 2359304 | tf_op jit(solution)/shard_map/ppermute | solution.py:135
  107.2 34.5 %collective-permute-start.9 = (bf16[1,1,4,80,768]{4,3,2,1,0:T(8,128)(2,1)}, bf16[1,1,4,80,768]{4,3,2,1,0:T(8,128)(2,1)}, u32[]{:S(2)}, u32[]{:S(2)}) collective-permute-start(bf16[1,1,4,80,768]{4,3,2,1,0:T(8,128)(2,1)} %constant_dynamic-slice_fusion.13), channel_id=1, source_target_pairs={{0,16},{4,20},{8,24},{12,28},{16,0},{20,4},{24,8},{28,12},{1,17},{... | collective-permute-start | bytes 1474568 | tf_op jit(solution)/shard_map/ppermute | solution.py:28
  142.9 31.8 %collective-permute-start.13 = (bf16[8,80,768]{2,1,0:T(8,128)(2,1)S(1)}, bf16[8,80,768]{2,1,0:T(8,128)(2,1)}, u32[]{:S(2)}, u32[]{:S(2)}) collective-permute-start(bf16[8,80,768]{2,1,0:T(8,128)(2,1)S(1)} %bitcast.183), channel_id=1, source_target_pairs={{0,2},{1,3},{2,0},{3,1},{4,6},{5,7},{6,4},{7,5},{8,10},{9,11},{10,... | collective-permute-start | bytes 2949128 | tf_op jit(solution)/shard_map/ppermute | solution.py:28
  146.1 300.7 %reduce-scatter.3.cloned.1.call-start = ((), (), s32[]{:S(2)}) async-start(), calls=%async_computation.3 | async-start | bytes 4718592 | tf_op jit(solution)/shard_map/reduce_scatter | solution.py:1034
  146.2 28.5 %collective-permute-start.11 = (bf16[192,2048]{1,0:T(8,128)(2,1)}, bf16[192,2048]{1,0:T(8,128)(2,1)S(1)}, u32[]{:S(2)}, u32[]{:S(2)}) collective-permute-start(bf16[192,2048]{1,0:T(8,128)(2,1)} %collective-permute-done.8.refs_16_), channel_id=1, source_target_pairs={{0,8},{8,16},{16,24},{24,28},{28,20},{20,12},{12,4},{4,0},{1,9},{9... | collective-permute-start | bytes 2359304 | tf_op jit(solution)/shard_map/ppermute | solution.py:135
  150.1 28.9 %collective-permute-start.12 = (bf16[8,80,768]{2,1,0:T(8,128)(2,1)S(1)}, bf16[8,80,768]{2,1,0:T(8,128)(2,1)S(1)}, u32[]{:S(2)}, u32[]{:S(2)}) collective-permute-start(bf16[8,80,768]{2,1,0:T(8,128)(2,1)S(1)} %bitcast.184), channel_id=1, source_target_pairs={{0,1},{1,0},{2,3},{3,2},{4,5},{5,4},{6,7},{7,6},{8,9},{9,8},{10,11... | collective-permute-start | bytes 2949128 | tf_op jit(solution)/shard_map/ppermute | solution.py:28
  179.0 63.2 %collective-permute-start.15 = (bf16[512,2048]{1,0:T(8,128)(2,1)}, bf16[512,2048]{1,0:T(8,128)(2,1)}, u32[]{:S(2)}, u32[]{:S(2)}) collective-permute-start(bf16[512,2048]{1,0:T(8,128)(2,1)} %slice_dynamic-update-slice_fusion.refs_3_), channel_id=1, source_target_pairs={{0,2},{1,3},{2,0},{3,1},{4,6},{5,7},{6,4},{7,5},{8,10},{9,11},{10,... | collective-permute-start | bytes 6291464 | tf_op jit(solution)/shard_map/ppermute | solution.py:28
  182.1 60.0 %collective-permute-start.16 = (bf16[2,1,2,64,2304]{4,3,2,1,0:T(8,128)(2,1)}, bf16[2,1,2,64,2304]{4,3,2,1,0:T(8,128)(2,1)}, u32[]{:S(2)}, u32[]{:S(2)}) collective-permute-start(bf16[2,1,2,64,2304]{4,3,2,1,0:T(8,128)(2,1)} %constant_dynamic-slice_fusion.10), channel_id=1, source_target_pairs={{0,8},{4,12},{8,0},{12,4},{16,24},{20,28},{24,16},{28,20},{1,9},{5... | collective-permute-start | bytes 3538952 | tf_op jit(solution)/shard_map/ppermute | solution.py:28
  183.3 82.7 %collective-permute-start.21 = (bf16[512,2048]{1,0:T(8,128)(2,1)}, bf16[512,2048]{1,0:T(8,128)(2,1)}, u32[]{:S(2)}, u32[]{:S(2)}) collective-permute-start(bf16[512,2048]{1,0:T(8,128)(2,1)} %slice_dynamic-update-slice_fusion.refs_3_), channel_id=1, source_target_pairs={{0,1},{1,0},{2,3},{3,2},{4,5},{5,4},{6,7},{7,6},{8,9},{9,8},{10,11... | collective-permute-start | bytes 6291464 | tf_op jit(solution)/shard_map/ppermute | solution.py:28
  242.2 36.2 %collective-permute-start.22 = (bf16[512,2048]{1,0:T(8,128)(2,1)}, bf16[512,2048]{1,0:T(8,128)(2,1)S(1)}, u32[]{:S(2)}, u32[]{:S(2)}) collective-permute-start(bf16[512,2048]{1,0:T(8,128)(2,1)} %collective-permute-done.15.refs_5_), channel_id=1, source_target_pairs={{0,1},{1,0},{2,3},{3,2},{4,5},{5,4},{6,7},{7,6},{8,9},{9,8},{10,11... | collective-permute-start | bytes 6291464 | tf_op jit(solution)/shard_map/ppermute | solution.py:28
  243.6 53.8 %collective-permute-start.27 = (bf16[8,64,2304]{2,1,0:T(8,128)(2,1)S(1)}, bf16[8,64,2304]{2,1,0:T(8,128)(2,1)}, u32[]{:S(2)}, u32[]{:S(2)}) collective-permute-start(bf16[8,64,2304]{2,1,0:T(8,128)(2,1)S(1)} %bitcast.166), channel_id=1, source_target_pairs={{0,2},{1,3},{2,0},{3,1},{4,6},{5,7},{6,4},{7,5},{8,10},{9,11},{10,... | collective-permute-start | bytes 7077896 | tf_op jit(solution)/shard_map/ppermute | solution.py:28
  292.4 31.9 %collective-permute-start.26 = (bf16[8,64,2304]{2,1,0:T(8,128)(2,1)S(1)}, bf16[8,64,2304]{2,1,0:T(8,128)(2,1)}, u32[]{:S(2)}, u32[]{:S(2)}) collective-permute-start(bf16[8,64,2304]{2,1,0:T(8,128)(2,1)S(1)} %bitcast.167), channel_id=1, source_target_pairs={{0,1},{1,0},{2,3},{3,2},{4,5},{5,4},{6,7},{7,6},{8,9},{9,8},{10,11... | collective-permute-start | bytes 7077896 | tf_op jit(solution)/shard_map/ppermute | solution.py:28
  341.1 327.7 %reduce-scatter.5.cloned.1.call-start = ((), (), s32[]{:S(2)}) async-start(), calls=%async_computation.4 | async-start | bytes 2359296 | tf_op jit(solution)/shard_map/reduce_scatter | solution.py:1085
  394.9 26.3 %collective-permute-start.33 = (bf16[2,8,64,768]{3,2,1,0:T(8,128)(2,1)}, bf16[2,8,64,768]{3,2,1,0:T(8,128)(2,1)S(1)}, u32[]{:S(2)}, u32[]{:S(2)}) collective-permute-start(bf16[2,8,64,768]{3,2,1,0:T(8,128)(2,1)} %get-tuple-element.204), channel_id=1, source_target_pairs={{0,1},{1,0},{2,3},{3,2},{4,5},{5,4},{6,7},{7,6},{8,9},{9,8},{10,11... | collective-permute-start | bytes 4718600 | tf_op jit(solution)/shard_map/ppermute | solution.py:28
  446.8 31.5 %collective-permute-start.39 = (bf16[2,8,64,2048]{3,2,1,0:T(8,128)(2,1)}, bf16[2,8,64,2048]{3,2,1,0:T(8,128)(2,1)}, u32[]{:S(2)}, u32[]{:S(2)}) collective-permute-start(bf16[2,8,64,2048]{3,2,1,0:T(8,128)(2,1)} %get-tuple-element.219), channel_id=1, source_target_pairs={{0,1},{1,0},{2,3},{3,2},{4,5},{5,4},{6,7},{7,6},{8,9},{9,8},{10,11... | collective-permute-start | bytes 12582920 | tf_op jit(solution)/shard_map/ppermute | solution.py:28
  460.7 37.8 %collective-permute-start.40 = (bf16[8,64,1536]{2,1,0:T(8,128)(2,1)}, bf16[8,64,1536]{2,1,0:T(8,128)(2,1)S(1)}, u32[]{:S(2)}, u32[]{:S(2)}) collective-permute-start(bf16[8,64,1536]{2,1,0:T(8,128)(2,1)} %fusion.5), channel_id=1, source_target_pairs={{0,2},{1,3},{2,0},{3,1},{4,6},{5,7},{6,4},{7,5},{8,10},{9,11},{10,... | collective-permute-start | bytes 4718600 | tf_op jit(solution)/shard_map/ppermute | solution.py:28
  463.0 35.5 %collective-permute-start.41 = (bf16[1,1,4,64,768]{4,3,2,1,0:T(8,128)(2,1)S(1)}, bf16[1,1,4,64,768]{4,3,2,1,0:T(8,128)(2,1)S(1)}, u32[]{:S(2)}, u32[]{:S(2)}) collective-permute-start(bf16[1,1,4,64,768]{4,3,2,1,0:T(8,128)(2,1)S(1)} %constant_dynamic-slice_fusion.9), channel_id=1, source_target_pairs={{0,16},{4,20},{8,24},{12,28},{16,0},{20,4},{24,8},{28,12},{1,17},{... | collective-permute-start | bytes 1179656 | tf_op jit(solution)/shard_map/ppermute | solution.py:28
  482.0 64.4 %collective-permute-start.46 = (bf16[8,64,2048]{2,1,0:T(8,128)(2,1)}, bf16[8,64,2048]{2,1,0:T(8,128)(2,1)}, u32[]{:S(2)}, u32[]{:S(2)}) collective-permute-start(bf16[8,64,2048]{2,1,0:T(8,128)(2,1)} %fusion.3), channel_id=1, source_target_pairs={{0,2},{1,3},{2,0},{3,1},{4,6},{5,7},{6,4},{7,5},{8,10},{9,11},{10,... | collective-permute-start | bytes 6291464 | tf_op jit(solution)/shard_map/ppermute | solution.py:28
  501.5 44.9 %collective-permute-start.45 = (bf16[1,1,4,64,1536]{4,3,2,1,0:T(8,128)(2,1)}, bf16[1,1,4,64,1536]{4,3,2,1,0:T(8,128)(2,1)S(1)}, u32[]{:S(2)}, u32[]{:S(2)}) collective-permute-start(bf16[1,1,4,64,1536]{4,3,2,1,0:T(8,128)(2,1)} %constant_dynamic-slice_fusion.5), channel_id=1, source_target_pairs={{0,16},{4,20},{8,24},{12,28},{16,0},{20,4},{24,8},{28,12},{1,17},{... | collective-permute-start | bytes 2359304 | tf_op jit(solution)/shard_map/ppermute | solution.py:28
  518.4 26.7 %collective-permute-start.42 = (bf16[128,2048]{1,0:T(8,128)(2,1)}, bf16[128,2048]{1,0:T(8,128)(2,1)}, u32[]{:S(2)}, u32[]{:S(2)}) collective-permute-start(bf16[128,2048]{1,0:T(8,128)(2,1)} %get-tuple-element.295), channel_id=1, source_target_pairs={{0,8},{8,16},{16,24},{24,28},{28,20},{20,12},{12,4},{4,0},{1,9},{9... | collective-permute-start | bytes 1572872 | tf_op jit(solution)/shard_map/ppermute | solution.py:135
  604.6 38.6 %collective-permute-start.60 = (bf16[2,1,2,64,1536]{4,3,2,1,0:T(8,128)(2,1)S(1)}, bf16[2,1,2,64,1536]{4,3,2,1,0:T(8,128)(2,1)S(1)}, u32[]{:S(2)}, u32[]{:S(2)}) collective-permute-start(bf16[2,1,2,64,1536]{4,3,2,1,0:T(8,128)(2,1)S(1)} %constant_dynamic-slice_fusion.1), channel_id=1, source_target_pairs={{0,8},{4,12},{8,0},{12,4},{16,24},{20,28},{24,16},{28,20},{1,9},{5... | collective-permute-start | bytes 2359304 | tf_op jit(solution)/shard_map/ppermute | solution.py:28
  623.0 27.6 %collective-permute-start.57 = (bf16[1,2,80,768]{3,2,1,0:T(8,128)(2,1)}, bf16[1,2,80,768]{3,2,1,0:T(8,128)(2,1)}, u32[]{:S(2)}, u32[]{:S(2)}) collective-permute-start(bf16[1,2,80,768]{3,2,1,0:T(8,128)(2,1)} %get-tuple-element.306), channel_id=1, source_target_pairs={{0,8},{4,12},{8,0},{12,4},{16,24},{20,28},{24,16},{28,20},{1,9},{5... | collective-permute-start | bytes 737288 | tf_op jit(solution)/shard_map/ppermute | solution.py:28
  632.6 30.8 %collective-permute-start.59 = (bf16[1,2,80,768]{3,2,1,0:T(8,128)(2,1)}, bf16[1,2,80,768]{3,2,1,0:T(8,128)(2,1)}, u32[]{:S(2)}, u32[]{:S(2)}) collective-permute-start(bf16[1,2,80,768]{3,2,1,0:T(8,128)(2,1)} %get-tuple-element.304), channel_id=1, source_target_pairs={{0,24},{4,28},{8,16},{12,20},{16,8},{20,12},{24,0},{28,4},{1,25},{... | collective-permute-start | bytes 737288 | tf_op jit(solution)/shard_map/ppermute | solution.py:28
  (83 other events, 1225.5 us)
Sparse Core Ops, SparseCore 0:
  146.3 100.9 all-gather.1
  341.2 98.1 reduce-scatter.2
  578.2 84.3 reduce-scatter.4
